TPU v7x, 512 devices: a whole 4x8x8 slice. The times are simulated.
512 devices in a mesh: dp: 32 (over y, x_hi, core), tensor: 16 (over z, x_lo).
Axes of the slice: x: 4 (x_hi: 2, x_lo: 2; x = x_hi * 2 + x_lo), y: 8, z: 8, core: 2. Of those that a mesh axis runs over, the one named last changes fastest.
Arguments:
- ranks: int32 [28672], P('tensor'), may hold values from 0 to 28671, as said below
- down_weight: bfloat16 [28672, 8192], P('tensor', 'dp'), may hold values from -0.03125 to 0.03125
- inputs: bfloat16 [3, 256, 8192], P(None, 'tensor', 'dp'), may hold values from -6 to 6
- grad_out: bfloat16 [3, 256, 8192], P(None, 'tensor', 'dp'), may hold values from -0.29882812 to 0.29882812
- gate_small: bfloat16 [256, 7168], P('dp', 'tensor'), may hold values from -6 to 6
- up_small: bfloat16 [256, 7168], P('dp', 'tensor'), may hold values from -6 to 6
- gate_mid: bfloat16 [256, 14336], P('dp', 'tensor'), may hold values from -6 to 6
- up_mid: bfloat16 [256, 14336], P('dp', 'tensor'), may hold values from -6 to 6
- gate_full: bfloat16 [256, 28672], P('dp', 'tensor'), may hold values from -6 to 6
- up_full: bfloat16 [256, 28672], P('dp', 'tensor'), may hold values from -6 to 6
Outputs:
- down_grad: bfloat16 [28672, 8192], P('tensor', 'dp')
- gate_grad: bfloat16 [8192, 28672], P('dp', 'tensor')
- up_grad: bfloat16 [8192, 28672], P('dp', 'tensor')
Inputs may be any that keep to these rules, and one draw needn't show every extreme that they name: ranks is a permutation of the neurons; the 28672 // 16 consecutive neurons of block j have exactly the ranks that leave remainder j when divided by 16.
All inputs are finite; a program needn't handle non-finite values.
Results may differ from a plain program's by a relative error of at most 0.0049.
Values may be sent and summed in bfloat16 or wider, within the bound.
No kernel may reach another device: no remote copies, remote signals or barrier semaphores. Data moves between devices by JAX's collectives and lax.ppermute only.
A program may use at most 64 MiB of HBM per device.

v0:
```python
import jax
import jax.numpy as jnp
from jax import lax
from jax.sharding import PartitionSpec as P


def for_sending(x):
    return jax.tree.map(lambda a: a.astype(jnp.bfloat16) if a.dtype == jnp.float32 else a, x)


def hidden_of(gate_value, up_value):
    gate_float = gate_value.astype(jnp.float32)
    up_float = up_value.astype(jnp.float32)
    return (gate_float * jax.nn.sigmoid(gate_float) * up_float).astype(jnp.bfloat16)


def slopes_of(gate_value, up_value, upstream):
    gate_float = gate_value.astype(jnp.float32)
    up_float = up_value.astype(jnp.float32)
    sigmoid_gate = jax.nn.sigmoid(gate_float)
    active = gate_float * sigmoid_gate
    gate_slope = (
        upstream * up_float * (sigmoid_gate * (1.0 + gate_float * (1.0 - sigmoid_gate)))
    ).astype(jnp.bfloat16)
    up_slope = (upstream * active).astype(jnp.bfloat16)
    return (gate_slope, up_slope)


def rows_product(left, right):
    return lax.dot_general(
        left, right, (((0,), (0,)), ((), ())), preferred_element_type=jnp.float32
    )


def per_device(
    ranks, down_weight, inputs, grad_out, gate_small, up_small, gate_mid, up_mid, gate_full, up_full
):
    position = ranks // lax.axis_size("tensor")
    sorted_down = jnp.take(down_weight, jnp.argsort(position), axis=0)
    gates = (gate_small, gate_mid, gate_full)
    ups = (up_small, up_mid, up_full)
    widths = tuple((item.shape[1] for item in gates))
    every_grad = lax.all_gather(grad_out, "tensor", axis=1, tiled=True)
    partials = tuple(
        (
            lax.dot_general(
                every_grad[index],
                sorted_down[: widths[index]],
                (((1,), (1,)), ((), ())),
                preferred_element_type=jnp.float32,
            )
            for index in range(3)
        )
    )
    local_hidden = tuple((hidden_of(gates[index], ups[index]) for index in range(3)))
    hidden_all = jax.tree.map(
        lambda part, own: part.astype(own.dtype),
        lax.all_gather(for_sending(local_hidden), "dp", axis=0, tiled=True),
        local_hidden,
    )
    upstream = lax.psum_scatter(partials, "dp", scatter_dimension=0, tiled=True)
    local_slopes = []
    for index in range(3):
        local_slopes.extend(slopes_of(gates[index], ups[index], upstream[index]))
    slope_all = lax.all_gather(for_sending(tuple(local_slopes)), "dp", axis=0, tiled=True)
    gate_slopes = slope_all[0::2]
    up_slopes = slope_all[1::2]
    bounds = (0,) + widths
    blocks = []
    for index in range(3):
        start_col = bounds[index]
        stop_col = bounds[index + 1]
        total = rows_product(hidden_all[index][:, start_col:stop_col], every_grad[index])
        for source in range(index + 1, 3):
            total = total + rows_product(
                hidden_all[source][:, start_col:stop_col], every_grad[source]
            )
        blocks.append(total)
    down_sorted = jnp.concatenate(blocks, 0)
    down_grad = jnp.take(down_sorted, position, axis=0).astype(jnp.bfloat16)
    empty = jnp.zeros((inputs.shape[2], widths[2]), jnp.float32)
    portion = lax.all_gather(inputs, "tensor", axis=1, tiled=True)
    gate_total = empty
    up_total = empty
    for index in range(3):
        gate_rows = gate_slopes[index]
        up_rows = up_slopes[index]
        gate_total = gate_total.at[:, : widths[index]].add(rows_product(portion[index], gate_rows))
        up_total = up_total.at[:, : widths[index]].add(rows_product(portion[index], up_rows))
    gate_grad = jnp.take(gate_total, position, axis=1).astype(jnp.bfloat16)
    up_grad = jnp.take(up_total, position, axis=1).astype(jnp.bfloat16)
    return (down_grad, gate_grad, up_grad)


def solution(mesh):
    return jax.shard_map(
        per_device,
        mesh=mesh,
        in_specs=(
            P("tensor"),
            P("tensor", "dp"),
            P(None, "tensor", "dp"),
            P(None, "tensor", "dp"),
            P("dp", "tensor"),
            P("dp", "tensor"),
            P("dp", "tensor"),
            P("dp", "tensor"),
            P("dp", "tensor"),
            P("dp", "tensor"),
        ),
        out_specs=(P("tensor", "dp"), P("dp", "tensor"), P("dp", "tensor")),
        check_vma=False,
    )
```

profile of v0, /device:TPU:1, one launch (start us, length us, event | category | flops | bytes accessed | tf_op | source)
XLA Modules:
  0.0 748.7 jit_solution(11502392150959802158)
XLA Ops:
  7.2 0.8 compare_and_fusion.1
  8.0 5.0 sort.17
  13.1 35.9 %all_gather.34 = bf16[3,256,256]{2,1,0:T(8,128)(2,1)S(1)} all-gather(bf16[3,16,256]{2,1,0:T(8,128)(2,1)} %param.31), channel_id=1, replica_groups=mesh['dp'=32,'tensor'=16] {'tensor'}, dimensions={1}, use_global_device_ids=true | all-gather | bytes 417792 | tf_op jit(solution)/shard_map/all_gather | solution.py:43
  49.0 5.5 gather_fusion.1
  54.5 0.3 broadcast_select_fusion
  55.1 1.0 copy.32
  56.1 1.2 convolution_bitcast_fusion.5
  57.4 1.6 convolution_bitcast_fusion.2
  59.1 1.7 copy.36
  60.8 0.6 compare_reduce_fusion.1
  61.5 0.7 compare_reduce_fusion
  62.2 24.6 %all_gather.38 = bf16[3,256,256]{2,1,0:T(8,128)(2,1)S(1)} all-gather(bf16[3,16,256]{2,1,0:T(8,128)(2,1)S(1)} %copy-done.7), channel_id=1, replica_groups=mesh['dp'=32,'tensor'=16] {'tensor'}, dimensions={1}, use_global_device_ids=true | all-gather | bytes 417792 | tf_op jit(solution)/shard_map/all_gather | solution.py:82
  86.8 1.3 dynamic-slice.44
  88.7 86.7 %reduce-scatter.8.cloned.1.call-done = f32[8,448]{1,0:T(8,128)} async-done(((f32[256,448]{1,0:T(8,128)}), f32[8,448]{1,0:T(8,128)}) %reduce-scatter.8.cloned.1.call-update) | async-done | bytes 14352 | tf_op jit(solution)/shard_map/reduce_scatter | solution.py:61
  175.4 0.7 multiply_convert_fusion.2
  176.1 45.6 %all_gather.41 = bf16[256,448]{1,0:T(8,128)(2,1)S(1)} all-gather(bf16[8,448]{1,0:T(8,128)(2,1)S(1)} %get-tuple-element.108), channel_id=1, replica_groups=mesh['dp'=32,'tensor'=16] {'dp'}, dimensions={0}, use_global_device_ids=true | all-gather | bytes 236544 | tf_op jit(solution)/shard_map/all_gather | solution.py:65
  221.7 0.9 fusion.4
  222.8 37.9 %all_gather.37 = bf16[256,448]{1,0:T(8,128)(2,1)S(1)} all-gather(bf16[8,448]{1,0:T(8,128)(2,1)S(1)} %get-tuple-element.109), channel_id=1, replica_groups=mesh['dp'=32,'tensor'=16] {'dp'}, dimensions={0}, use_global_device_ids=true | all-gather | bytes 236544 | tf_op jit(solution)/shard_map/all_gather | solution.py:65
  260.7 0.9 fusion.5
  261.6 1.4 scatter-add.14
  263.0 39.8 %all_gather.33 = bf16[256,448]{1,0:T(8,128)(2,1)S(1)} all-gather(bf16[8,448]{1,0:T(8,128)(2,1)S(1)} %get-tuple-element.110), channel_id=1, replica_groups=mesh['dp'=32,'tensor'=16] {'dp'}, dimensions={0}, use_global_device_ids=true | all-gather | bytes 236544 | tf_op jit(solution)/shard_map/all_gather | solution.py:58
  302.7 1.0 fusion.15
  303.8 148.6 %all-reduce.5.cloned.1.call-done = f32[256,896]{0,1:T(8,128)} async-done(((f32[256,896]{0,1:T(8,128)}), f32[256,896]{0,1:T(8,128)}) %all-reduce.5.cloned.1.call-update) | async-done | bytes 917520
  452.4 2.0 constant_dynamic-slice_fusion
  454.3 1.8 copy.25
  456.1 0.8 multiply_convert_fusion.1
  457.0 41.6 %all_gather.42 = bf16[256,896]{1,0:T(8,128)(2,1)S(1)} all-gather(bf16[8,896]{1,0:T(8,128)(2,1)S(1)} %get-tuple-element.105), channel_id=1, replica_groups=mesh['dp'=32,'tensor'=16] {'dp'}, dimensions={0}, use_global_device_ids=true | all-gather | bytes 473088 | tf_op jit(solution)/shard_map/all_gather | solution.py:65
  498.6 39.9 %all_gather.39 = bf16[256,896]{1,0:T(8,128)(2,1)S(1)} all-gather(bf16[8,896]{1,0:T(8,128)(2,1)S(1)} %get-tuple-element.106), channel_id=1, replica_groups=mesh['dp'=32,'tensor'=16] {'dp'}, dimensions={0}, use_global_device_ids=true | all-gather | bytes 473088 | tf_op jit(solution)/shard_map/all_gather | solution.py:65
  538.6 39.0 %all_gather.35 = bf16[256,896]{1,0:T(8,128)(2,1)S(1)} all-gather(bf16[8,896]{1,0:T(8,128)(2,1)S(1)} %get-tuple-element.107), channel_id=1, replica_groups=mesh['dp'=32,'tensor'=16] {'dp'}, dimensions={0}, use_global_device_ids=true | all-gather | bytes 473088 | tf_op jit(solution)/shard_map/all_gather | solution.py:58
  577.5 1.2 fusion.10
  578.7 1.0 convolution_add_fusion.2
  579.8 1.1 fusion.3
  580.8 3.1 fusion.2
  583.9 1.5 multiply_convert_fusion
  585.4 43.0 %all_gather.43 = bf16[256,1792]{1,0:T(8,128)(2,1)S(1)} all-gather(bf16[8,1792]{1,0:T(8,128)(2,1)S(1)} %get-tuple-element.102), channel_id=1, replica_groups=mesh['dp'=32,'tensor'=16] {'dp'}, dimensions={0}, use_global_device_ids=true | all-gather | bytes 946176 | tf_op jit(solution)/shard_map/all_gather | solution.py:65
  628.4 42.5 %all_gather.40 = bf16[256,1792]{1,0:T(8,128)(2,1)} all-gather(bf16[8,1792]{1,0:T(8,128)(2,1)S(1)} %get-tuple-element.103), channel_id=1, replica_groups=mesh['dp'=32,'tensor'=16] {'dp'}, dimensions={0}, use_global_device_ids=true | all-gather | bytes 946176 | tf_op jit(solution)/shard_map/all_gather | solution.py:65
  670.9 2.0 fusion
  672.9 5.5 gather_fusion.3
  678.4 2.2 fusion.1
  680.6 6.1 gather_fusion.2
  686.7 41.7 %all_gather.36 = bf16[256,1792]{1,0:T(8,128)(2,1)S(1)} all-gather(bf16[8,1792]{1,0:T(8,128)(2,1)S(1)} %copy-done.6), channel_id=1, replica_groups=mesh['dp'=32,'tensor'=16] {'dp'}, dimensions={0}, use_global_device_ids=true | all-gather | bytes 946176 | tf_op jit(solution)/shard_map/all_gather | solution.py:58
  728.4 0.3 fusion.7
  728.7 0.4 convolution_add_fusion
  729.1 0.3 convolution_add_fusion.1
  729.5 6.1 gather_fusion
  735.5 3.1 bitcast_convert_fusion
  738.6 2.2 copy.30
  740.8 1.4 copy.31
  (36 shorter events, 0.7 us)
Async XLA Ops:
  7.2 41.8 %copy-start = (bf16[1792,256]{1,0:T(8,128)(2,1)S(1)}, bf16[1792,256]{1,0:T(8,128)(2,1)}, u32[]{:S(2)}) copy-start(bf16[1792,256]{1,0:T(8,128)(2,1)} %param.29) | copy-start | bytes 2752516
  7.2 168.2 %reduce-scatter.8.cloned.1.call-start = ((), (), s32[]{:S(2)}) async-start(), calls=%async_computation.2 | async-start | bytes 540672 | tf_op jit(solution)/shard_map/reduce_scatter | solution.py:61
  54.8 2.6 copy-start.2
  56.1 396.3 %all-reduce.5.cloned.1.call-start = ((), (), s32[]{:S(2)}) async-start(), calls=%async_computation.4 | async-start | bytes 1835008
  57.4 526.5 %reduce-scatter.10.cloned.1.call-start = ((), (), s32[]{:S(2)}) async-start(), calls=%async_computation.3 | async-start | bytes 1892352 | tf_op jit(solution)/shard_map/reduce_scatter | solution.py:61
  60.8 1.4 copy-start.7
  60.8 114.6 %copy-start.8 = (bf16[8,448]{1,0:T(8,128)(2,1)S(1)}, bf16[8,448]{1,0:T(8,128)(2,1)}, u32[]{:S(2)}) copy-start(bf16[8,448]{1,0:T(8,128)(2,1)} %param.32) | copy-start | bytes 21508
  60.8 114.6 %copy-start.9 = (bf16[8,448]{1,0:T(8,128)(2,1)S(1)}, bf16[8,448]{1,0:T(8,128)(2,1)}, u32[]{:S(2)}) copy-start(bf16[8,448]{1,0:T(8,128)(2,1)} %param.33) | copy-start | bytes 21508
  456.1 122.6 %copy-start.4 = (f32[448,256]{1,0:T(8,128)S(1)}, f32[448,256]{1,0:T(8,128)}, u32[]{:S(2)}) copy-start(f32[448,256]{1,0:T(8,128)} %fusion.15) | copy-start | bytes 1376260
  580.8 47.6 %copy-start.1 = (f32[256,1792]{0,1:T(8,128)}, f32[256,1792]{0,1:T(8,128)S(1)}, u32[]{:S(2)}) copy-start(f32[256,1792]{0,1:T(8,128)S(1)} %fusion.3) | copy-start | bytes 5505028
  680.6 6.1 copy-start.6
  686.7 42.0 %copy-start.5 = (f32[448,256]{1,0:T(8,128)S(1)}, f32[448,256]{1,0:T(8,128)}, u32[]{:S(2)}) copy-start(f32[448,256]{1,0:T(8,128)} %fusion.10) | copy-start | bytes 1376260
  686.7 42.5 %copy-start.3 = (f32[448,256]{1,0:T(8,128)S(1)}, f32[448,256]{1,0:T(8,128)}, u32[]{:S(2)}) copy-start(f32[448,256]{1,0:T(8,128)} %convolution_add_fusion.2) | copy-start | bytes 1376260
Sparse Core Ops, SparseCore 0:
  56.2 119.1 reduce-scatter.7
  179.1 273.2 all-reduce.4
  457.1 123.0 reduce-scatter.9
where the time goes:
time: 749 us
  blocking collectives  432 us (58%)
  waiting for transfers between devices  235 us (31%)
  local copies, waits for them, and re-layouts  35.9 us (5%)
  matrix products  17.5 us (2%)
  between operations  14.5 us (2%)
  other arithmetic  13.7 us (2%)
    all_gather x6, blocking collectives, per_device(): lax.all_gather(for_sending(tuple(local_slopes)), 'dp', axis=0, tiled=True)  251 us
    unnamed x4, waiting for transfers between devices  149 us
    all_gather x3, blocking collectives, per_device(): lax.all_gather(for_sending(local_hidden), 'dp', axis=0, tiled=True)  120 us
    reduce_scatter x2, waiting for transfers between devices, per_device(): upstream = lax.psum_scatter(partials, 'dp', scatter_dimension=0, tiled=True)  86.7 us
    all_gather x1, blocking collectives, per_device(): every_grad = lax.all_gather(grad_out, 'tensor', axis=1, tiled=True)  35.9 us
    all_gather x1, blocking collectives, per_device(): portion = lax.all_gather(inputs, 'tensor', axis=1, tiled=True)  24.6 us
  transfers between devices with their start and end apart: 3, of which 2 were waited for; matrix products, arithmetic and copies ran while one was open for 3% of the time, Pallas kernels for 0%

commit v1 on v0

v1 whole, which is shorter than its diff:
```python
import functools

import jax
import jax.numpy as jnp
from jax import lax
from jax.experimental import pallas as pl
from jax.experimental.pallas import tpu as pltpu
from jax.sharding import PartitionSpec as P

VMEM = pl.BlockSpec(memory_space=pltpu.VMEM)
SMEM = pl.BlockSpec(memory_space=pltpu.SMEM)
LIMIT = pltpu.CompilerParams(vmem_limit_bytes=48 * 1024 * 1024)
TILE = 256


def padded(width):
    return -(-width // 128) * 128


def sort_kernel(position, down, ranked):
    count = down.shape[0]

    @pl.loop(0, count // TILE)
    def _(block):
        start = pl.multiple_of(block * TILE, TILE)
        rows = lax.broadcasted_iota(jnp.int32, (TILE, count), 0) + start
        chosen = (rows == position[...]).astype(jnp.float32).astype(jnp.bfloat16)
        ranked[pl.ds(start, TILE), :] = jnp.dot(
            chosen, down[...], preferred_element_type=jnp.float32
        ).astype(jnp.bfloat16)


def partial_kernel(widths, half, tokens, ranked, out):
    blocks = tokens.shape[0] // 2
    rows = blocks * tokens.shape[2]
    first = half[0] * blocks
    offset = 0
    for index, width in enumerate(widths):
        left = tokens[pl.ds(first, blocks), index].reshape(rows, tokens.shape[3])
        out[:, offset : offset + width] = lax.dot_general(
            left, ranked[:width], (((1,), (1,)), ((), ())), preferred_element_type=jnp.float32
        ).astype(out.dtype)
        offset += width


def final_kernel(
    widths, position, gate_up, upstream, tokens, down_grad, gate_grad, up_grad, hidden, gates, ups, totals
):
    count = position.shape[1]
    rows = gate_up.shape[0]
    features = tokens.shape[3]
    offset = 0
    for width in widths:
        step = 128

        @pl.loop(0, width // step)
        def _(block, offset=offset, width=width):
            start = pl.multiple_of(block * step, step)
            gate = gate_up[:, pl.ds(2 * offset + start, step)].astype(jnp.float32)
            up = gate_up[:, pl.ds(2 * offset + width + start, step)].astype(jnp.float32)
            place = pl.ds(offset + start, step)
            above = upstream[:, place].astype(jnp.float32)
            sigmoid = jax.nn.sigmoid(gate)
            active = gate * sigmoid
            hidden[:, place] = (active * up).astype(jnp.bfloat16)
            gates[:, place] = (above * up * (sigmoid * (1.0 + gate * (1.0 - sigmoid)))).astype(
                jnp.bfloat16
            )
            ups[:, place] = (above * active).astype(jnp.bfloat16)

        offset += width

    starts = (0, widths[0], widths[0] + widths[1])
    bounds = (0,) + widths
    sources = ((hidden, 3), (gates, 0), (ups, 0))
    for which, (array, base) in enumerate(sources):
        for band in range(3):
            low, high = bounds[band], bounds[band + 1]
            total = None
            for index in range(band, 3):
                left = tokens[:, base + index].reshape(rows, features)
                term = lax.dot_general(
                    left,
                    array[:, starts[index] + low : starts[index] + high],
                    (((0,), (0,)), ((), ())),
                    preferred_element_type=jnp.float32,
                )
                total = term if total is None else total + term
            totals[which * features : (which + 1) * features, low:high] = total.astype(jnp.bfloat16)

    @pl.loop(0, count // TILE)
    def _(block):
        start = pl.multiple_of(block * TILE, TILE)
        ranks_here = lax.broadcasted_iota(jnp.int32, (count, TILE), 0)
        chosen = (ranks_here == position[:, pl.ds(start, TILE)]).astype(jnp.float32).astype(jnp.bfloat16)
        moved = jnp.dot(totals[...], chosen, preferred_element_type=jnp.float32)
        down_grad[pl.ds(start, TILE), :] = moved[:features].T.astype(jnp.bfloat16)
        gate_grad[:, pl.ds(start, TILE)] = moved[features : 2 * features].astype(jnp.bfloat16)
        up_grad[:, pl.ds(start, TILE)] = moved[2 * features :].astype(jnp.bfloat16)


def sort_rows(position, down):
    return pl.pallas_call(
        sort_kernel,
        out_shape=jax.ShapeDtypeStruct(down.shape, jnp.bfloat16),
        in_specs=[VMEM, VMEM],
        out_specs=VMEM,
        compiler_params=LIMIT,
    )(position, down)


def partial_of(widths, half, tokens, ranked, dtype):
    rows = tokens.shape[0] // 2 * tokens.shape[2]
    return pl.pallas_call(
        functools.partial(partial_kernel, widths),
        out_shape=jax.ShapeDtypeStruct((rows, sum(widths)), dtype),
        in_specs=[SMEM, VMEM, VMEM],
        out_specs=VMEM,
        compiler_params=LIMIT,
    )(half, tokens, ranked)


def finish(widths, position, gate_up, upstream, tokens):
    count = position.shape[1]
    rows = gate_up.shape[0]
    features = tokens.shape[3]
    return pl.pallas_call(
        functools.partial(final_kernel, widths),
        out_shape=(
            jax.ShapeDtypeStruct((count, features), jnp.bfloat16),
            jax.ShapeDtypeStruct((features, count), jnp.bfloat16),
            jax.ShapeDtypeStruct((features, count), jnp.bfloat16),
        ),
        in_specs=[VMEM] * 4,
        out_specs=(VMEM,) * 3,
        scratch_shapes=[pltpu.VMEM((rows, sum(widths)), jnp.bfloat16)] * 3
        + [pltpu.VMEM((3 * features, count), jnp.bfloat16)],
        compiler_params=LIMIT,
    )(position, gate_up, upstream, tokens)


def per_device(
    ranks, down_weight, inputs, grad_out, gate_small, up_small, gate_mid, up_mid, gate_full, up_full
):
    n_dp = lax.axis_size("dp")
    n_tensor = lax.axis_size("tensor")
    chips = n_dp // 2
    widths = tuple(padded(item.shape[1]) for item in (gate_small, gate_mid, gate_full))
    total = sum(widths)

    pairs = ((gate_small, up_small), (gate_mid, up_mid), (gate_full, up_full))
    local = jnp.concatenate(
        [
            jnp.pad(item, ((0, 0), (0, width - item.shape[1])))
            for pair, width in zip(pairs, widths)
            for item in pair
        ],
        axis=1,
    )
    gate_up = lax.all_gather(local, "dp", axis=0, tiled=True)

    position = (ranks // n_tensor)[None, :]
    ranked = sort_rows(position, down_weight)

    own = jnp.concatenate([inputs, grad_out], axis=0)
    tokens = lax.all_to_all(
        jnp.broadcast_to(own[None], (n_tensor,) + own.shape), "tensor", 0, 0, tiled=True
    )

    core = lax.axis_index("dp") % 2
    grads = tokens[:, 3:]
    sent = partial_of(widths, (1 - core)[None], grads, ranked, jnp.bfloat16)
    other = lax.ppermute(sent, "dp", [(item, item ^ 1) for item in range(n_dp)])
    kept = partial_of(widths, core[None], grads, ranked, jnp.float32)
    summed = (kept + other.astype(jnp.float32)).astype(jnp.bfloat16)

    by_core = [[2 * chip + side for chip in range(chips)] for side in range(2)]
    block = summed.shape[0] // chips
    pieces = lax.all_to_all(
        summed.reshape(chips, block, total), "dp", 0, 0, axis_index_groups=by_core, tiled=True
    )
    reduced = jnp.sum(pieces.astype(jnp.float32), axis=0).astype(jnp.bfloat16)
    spread = lax.all_to_all(
        jnp.broadcast_to(reduced[None], (chips, block, total)),
        "dp",
        0,
        0,
        axis_index_groups=by_core,
        tiled=True,
    ).reshape(chips * block, total)
    by_chip = [[2 * chip, 2 * chip + 1] for chip in range(chips)]
    upstream = lax.all_gather(spread, "dp", axis=0, axis_index_groups=by_chip, tiled=True)
    return finish(widths, position, gate_up, upstream, tokens)


def solution(mesh):
    return jax.shard_map(
        per_device,
        mesh=mesh,
        in_specs=(
            P("tensor"),
            P("tensor", "dp"),
            P(None, "tensor", "dp"),
            P(None, "tensor", "dp"),
            P("dp", "tensor"),
            P("dp", "tensor"),
            P("dp", "tensor"),
            P("dp", "tensor"),
            P("dp", "tensor"),
            P("dp", "tensor"),
        ),
        out_specs=(P("tensor", "dp"), P("dp", "tensor"), P("dp", "tensor")),
        check_vma=False,
    )
```

time: 749 us -> 167 us (0.22)
  blocking collectives: 432 us -> 64.1 us
  waiting for transfers between devices: 235 us -> 49.3 us
  local copies, waits for them, and re-layouts: 35.9 us -> 5.12 us
  matrix products: 17.5 us -> 0 us
  starting transfers between devices: 0.12 us -> 17 us
  Pallas kernels: 0 us -> 15.8 us
  other arithmetic: 13.7 us -> 1.1 us
    all_gather x11 -> x0, blocking collectives: 432 us -> none  [the longest x6 251 us: per_device(): lax.all_gather(for_sending(tuple(local_slopes)), 'dp', axis=0, tiled=True)]
    unnamed x4 -> x2, waiting for transfers between devices: 149 us -> 0.03 us
    reduce_scatter x2 -> x0, waiting for transfers between devices: 86.7 us -> none  [per_device(): upstream = lax.psum_scatter(partials, 'dp', scatter_dimension=0, tiled=True)]
    all_to_all x0 -> x2, blocking collectives: none -> 64.1 us  [the longest x1 34.2 us: per_device(): lax.all_to_all(summed.reshape(chips, block, total), 'dp', 0, 0, axis_inde...]
    all_gather x0 -> x2, waiting for transfers between devices: none -> 31 us  [the longest x1 19 us: per_device(): lax.all_gather(spread, 'dp', axis=0, axis_index_groups=by_chip, tiled=True)]
    gather x4 -> x0, local copies, waits for them, and re-layouts: 23 us -> none  [the longest x1 6.06 us: per_device(): gate_grad = jnp.take(gate_total, position, axis=1).astype(jnp.bfloat16)]
    dot_general x15 -> x0, matrix products: 17.5 us -> none  [the longest x12 14.4 us: rows_product(): lax.dot_general(left, right, (((0,), (0,)), ((), ())), preferred_element_...]
    all_to_all x0 -> x1, waiting for transfers between devices: none -> 16.9 us  [per_device(): lax.all_to_all(jnp.broadcast_to(own[None], (n_tensor,) + own.shape), 'ten...]
  transfers between devices with their start and end apart: 3 -> 4, of which waited for: 2 -> 4; matrix products, arithmetic and copies ran while one was open for 3% -> 0% of each run, Pallas kernels for 0% -> 2%
where the time goes in v1:
time: 167 us
  blocking collectives  64.1 us (38%)
  waiting for transfers between devices  49.3 us (30%)
  starting transfers between devices  17 us (10%)
  Pallas kernels  15.8 us (9%)
  between operations  14.3 us (9%)
  local copies, waits for them, and re-layouts  5.12 us (3%)
    all_to_all x1, blocking collectives, per_device(): lax.all_to_all(summed.reshape(chips, block, total), 'dp', 0, 0, axis_inde...  34.2 us
    all_to_all x1, blocking collectives, per_device(): lax.all_to_all(jnp.broadcast_to(reduced[None], (chips, block, total)), 'd...  29.9 us
    all_gather x1, waiting for transfers between devices, per_device(): lax.all_gather(spread, 'dp', axis=0, axis_index_groups=by_chip, tiled=True)  19 us
    all_to_all x1, waiting for transfers between devices, per_device(): lax.all_to_all(jnp.broadcast_to(own[None], (n_tensor,) + own.shape), 'ten...  16.9 us
    all_gather x1, waiting for transfers between devices, per_device(): gate_up = lax.all_gather(local, 'dp', axis=0, tiled=True)  12 us
    all_to_all x1, starting transfers between devices, per_device(): lax.all_to_all(jnp.broadcast_to(own[None], (n_tensor,) + own.shape), 'ten...  11.9 us
    pallas_call x1, Pallas kernels, finish(): pl.pallas_call(functools.partial(final_kernel, widths), out_shape=(jax.Sh...  11.7 us
    ppermute x1, starting transfers between devices, per_device(): other = lax.ppermute(sent, 'dp', [(item, item ^ 1) for item in range(n_dp)])  5 us
  transfers between devices with their start and end apart: 4, of which 4 were waited for; matrix products, arithmetic and copies ran while one was open for 0% of the time, Pallas kernels for 2%

profile of v1, /device:TPU:1, one launch (start us, length us, event | category | flops | bytes accessed | tf_op | source)
XLA Modules:
  0.0 166.7 jit_solution(15785301080366972643)
XLA Ops:
  7.2 0.0 copy-start.8
  7.2 0.0 copy-start.9
  7.2 0.0 copy-start.6
  7.2 0.0 copy-start.7
  7.2 0.0 copy-start.4
  7.2 0.0 copy-start.5
  7.2 0.0 copy-start.10
  7.2 0.0 copy-start.2
  7.2 0.8 pad_maximum_fusion
  8.1 1.0 broadcast_in_dim.23
  9.0 11.9 %all-to-all-start = ((bf16[16,6,16,256]{3,2,1,0:T(8,128)(2,1)}), bf16[16,6,16,256]{3,2,1,0:T(8,128)(2,1)S(1)}, u32[]{:S(2)}, u32[]{:S(2)}) async-start(bf16[16,6,16,256]{3,2,1,0:T(8,128)(2,1)} %broadcast_in_dim.23), calls=%async_computation | async-start | bytes 1572864 | tf_op jit(solution)/shard_map/all_to_all | solution.py:166
  21.0 0.0 all-gather.3.cloned.1.call-start
  21.0 0.0 copy-done.8
  21.0 0.0 copy-done.9
  21.0 0.0 copy-done.6
  21.1 0.0 copy-done.7
  21.1 0.0 copy-done.4
  21.1 0.0 copy-done.5
  21.1 0.0 copy-start.3
  21.2 0.6 copy-done.3
  21.8 0.0 all-gather.3.cloned.1.call-update
  21.8 0.0 all-gather.5.cloned.1.call-start
  21.9 0.0 copy-done.10
  21.9 0.0 copy-done.2
  21.9 2.9 %shard_map.121.ranked = bf16[1792,256]{1,0:T(8,128)(2,1)S(1)} custom-call(s32[1,1792]{1,0:T(1,128)S(1)} %broadcast_in_dim.10.position, bf16[1792,256]{1,0:T(8,128)(2,1)S(1)} %copy-done.2), custom_call_target="tpu_custom_call" | custom-call | tf_op jit(solution)/shard_map/pallas_call | solution.py:103
  24.8 16.9 %all-to-all-done.tokens = bf16[16,6,16,256]{3,2,1,0:T(8,128)(2,1)S(1)} async-done(((bf16[16,6,16,256]{3,2,1,0:T(8,128)(2,1)}), bf16[16,6,16,256]{3,2,1,0:T(8,128)(2,1)S(1)}, u32[]{:S(2)}, u32[]{:S(2)}) %all-to-all-start) | async-done | bytes 786464 | tf_op jit(solution)/shard_map/all_to_all | solution.py:166
  41.8 0.6 shard_map.123
  42.4 5.0 %collective-permute-start = (bf16[128,3200]{1,0:T(8,128)(2,1)S(1)}, bf16[128,3200]{1,0:T(8,128)(2,1)S(1)}, u32[]{:S(2)}, u32[]{:S(2)}) collective-permute-start(bf16[128,3200]{1,0:T(8,128)(2,1)S(1)} %shard_map.123), channel_id=1, source_target_pairs={{0,16},{16,0},{32,48},{48,32},{64,80},{80,64},{96,112},{112,96},{1... | collective-permute-start | bytes 2457608 | tf_op jit(solution)/shard_map/ppermute | solution.py:173
  47.4 0.6 shard_map.122
  48.0 1.3 collective-permute-done
  49.3 0.1 fusion
  49.5 34.2 %all_to_all.15 = bf16[16,8,3200]{2,1,0:T(8,128)(2,1)S(1)} all-to-all(bf16[16,8,3200]{2,1,0:T(8,128)(2,1)S(1)} %fusion), channel_id=1, replica_groups={{0,32,64,96,128,160,192,224,256,288,320,352,384,416,448,480},{16,48,80,..., dimensions={0} | all-to-all | bytes 1638400 | tf_op jit(solution)/shard_map/all_to_all | solution.py:179
  83.7 0.1 reduce_sum.12
  83.8 0.1 broadcast_in_dim.25
  83.9 29.9 %all_to_all.16 = bf16[16,8,3200]{2,1,0:T(8,128)(2,1)} all-to-all(bf16[16,8,3200]{2,1,0:T(8,128)(2,1)S(1)} %broadcast_in_dim.25), channel_id=1, replica_groups={{0,32,64,96,128,160,192,224,256,288,320,352,384,416,448,480},{16,48,80,..., dimensions={0} | all-to-all | bytes 1638400 | tf_op jit(solution)/shard_map/all_to_all | solution.py:183
  113.8 0.0 all-gather.5.cloned.1.call-update
  113.8 12.0 %all-gather.3.cloned.1.call-done.gate_up = bf16[256,6400]{1,0:T(8,128)(2,1)} async-done(((bf16[8,6400]{1,0:T(8,128)(2,1)}), bf16[256,6400]{1,0:T(8,128)(2,1)}) %all-gather.3.cloned.1.call-update) | async-done | bytes 3276816 | tf_op jit(solution)/shard_map/all_gather | solution.py:160
  125.8 19.0 %all-gather.5.cloned.1.call-done.upstream = bf16[256,3200]{1,0:T(8,128)(2,1)} async-done(((bf16[128,3200]{1,0:T(8,128)(2,1)}), bf16[256,3200]{1,0:T(8,128)(2,1)}) %all-gather.5.cloned.1.call-update) | async-done | bytes 1638416 | tf_op jit(solution)/shard_map/all_gather | solution.py:192
  144.8 0.0 copy-start
  144.8 1.9 %copy-done = bf16[256,6400]{1,0:T(8,128)(2,1)S(1)} copy-done((bf16[256,6400]{1,0:T(8,128)(2,1)S(1)}, bf16[256,6400]{1,0:T(8,128)(2,1)}, u32[]{:S(2)}) %copy-start) | copy-done | bytes 3276824
  146.7 0.0 copy-start.1
  146.7 1.4 copy-done.1
  148.1 11.7 %shard_map.124 = (bf16[1792,256]{1,0:T(8,128)(2,1)}, bf16[256,1792]{1,0:T(8,128)(2,1)}, bf16[256,1792]{1,0:T(8,128)(2,1)}) custom-call(s32[1,1792]{1,0:T(1,128)S(1)} %broadcast_in_dim.10.position, bf16[256,6400]{1,0:T(8,128)(2,1)S(1)} %copy-done, bf16[256,3200]{1,0:T(8,128)(2,1)S(1)} %copy-done.1, bf16[16,6,16,256]{3,2,1,0:T(8,128)(2,1)S(1)} %all-to-all-done.tokens), custom_call_target="tpu_custom_call" | custom-call | tf_op jit(solution)/shard_map/pallas_call | solution.py:127
  (9 shorter events, 0.1 us)
Async XLA Ops:
  7.2 13.8 %copy-start.8 = (bf16[8,448]{1,0:T(8,128)(2,1)S(1)}, bf16[8,448]{1,0:T(8,128)(2,1)}, u32[]{:S(2)}) copy-start(bf16[8,448]{1,0:T(8,128)(2,1)} %param.14) | copy-start | bytes 21508
  7.2 13.8 %copy-start.9 = (bf16[8,448]{1,0:T(8,128)(2,1)S(1)}, bf16[8,448]{1,0:T(8,128)(2,1)}, u32[]{:S(2)}) copy-start(bf16[8,448]{1,0:T(8,128)(2,1)} %param.15) | copy-start | bytes 21508
  7.2 13.9 %copy-start.6 = (bf16[8,896]{1,0:T(8,128)(2,1)S(1)}, bf16[8,896]{1,0:T(8,128)(2,1)}, u32[]{:S(2)}) copy-start(bf16[8,896]{1,0:T(8,128)(2,1)} %param.16) | copy-start | bytes 43012
  7.2 13.9 %copy-start.7 = (bf16[8,896]{1,0:T(8,128)(2,1)S(1)}, bf16[8,896]{1,0:T(8,128)(2,1)}, u32[]{:S(2)}) copy-start(bf16[8,896]{1,0:T(8,128)(2,1)} %param.17) | copy-start | bytes 43012
  7.2 13.9 %copy-start.4 = (bf16[8,1792]{1,0:T(8,128)(2,1)S(1)}, bf16[8,1792]{1,0:T(8,128)(2,1)}, u32[]{:S(2)}) copy-start(bf16[8,1792]{1,0:T(8,128)(2,1)} %param.18) | copy-start | bytes 86020
  7.2 13.9 %copy-start.5 = (bf16[8,1792]{1,0:T(8,128)(2,1)S(1)}, bf16[8,1792]{1,0:T(8,128)(2,1)}, u32[]{:S(2)}) copy-start(bf16[8,1792]{1,0:T(8,128)(2,1)} %param.19) | copy-start | bytes 86020
  7.2 14.6 %copy-start.10 = (s32[1792]{0:T(1024)S(1)}, s32[1792]{0:T(1024)}, u32[]{:S(2)}) copy-start(s32[1792]{0:T(1024)} %param.10) | copy-start | bytes 21508
  7.2 14.7 %copy-start.2 = (bf16[1792,256]{1,0:T(8,128)(2,1)S(1)}, bf16[1792,256]{1,0:T(8,128)(2,1)}, u32[]{:S(2)}) copy-start(bf16[1792,256]{1,0:T(8,128)(2,1)} %down.1) | copy-start | bytes 2752516
  9.0 32.7 %all-to-all-start = ((bf16[16,6,16,256]{3,2,1,0:T(8,128)(2,1)}), bf16[16,6,16,256]{3,2,1,0:T(8,128)(2,1)S(1)}, u32[]{:S(2)}, u32[]{:S(2)}) async-start(bf16[16,6,16,256]{3,2,1,0:T(8,128)(2,1)} %broadcast_in_dim.23), calls=%async_computation | async-start | bytes 1572864 | tf_op jit(solution)/shard_map/all_to_all | solution.py:166
  21.0 104.9 %all-gather.3.cloned.1.call-start = ((), (), s32[]{:S(2)}) async-start(), calls=%async_computation.3 | async-start | bytes 3379200 | tf_op jit(solution)/shard_map/all_gather | solution.py:160
  21.1 0.6 copy-start.3
  21.8 123.0 %all-gather.5.cloned.1.call-start = ((), (), s32[]{:S(2)}) async-start(), calls=%async_computation.4 | async-start | bytes 2457600 | tf_op jit(solution)/shard_map/all_gather | solution.py:192
  42.4 6.9 %collective-permute-start = (bf16[128,3200]{1,0:T(8,128)(2,1)S(1)}, bf16[128,3200]{1,0:T(8,128)(2,1)S(1)}, u32[]{:S(2)}, u32[]{:S(2)}) collective-permute-start(bf16[128,3200]{1,0:T(8,128)(2,1)S(1)} %shard_map.123), channel_id=1, source_target_pairs={{0,16},{16,0},{32,48},{48,32},{64,80},{80,64},{96,112},{112,96},{1... | collective-permute-start | bytes 2457608 | tf_op jit(solution)/shard_map/ppermute | solution.py:173
  144.8 1.9 %copy-start = (bf16[256,6400]{1,0:T(8,128)(2,1)S(1)}, bf16[256,6400]{1,0:T(8,128)(2,1)}, u32[]{:S(2)}) copy-start(bf16[256,6400]{1,0:T(8,128)(2,1)} %all-gather.3.cloned.1.call-done.gate_up) | copy-start | bytes 9830404
  146.7 1.4 copy-start.1
Sparse Core Ops, SparseCore 0:
  25.7 100.1 all-gather.2
  127.9 16.8 all-gather.4

commit v2 on v1

v2 whole, which is shorter than its diff:
```python
import functools

import jax
import jax.numpy as jnp
from jax import lax
from jax.experimental import pallas as pl
from jax.experimental.pallas import tpu as pltpu
from jax.sharding import PartitionSpec as P

VMEM = pl.BlockSpec(memory_space=pltpu.VMEM)
SMEM = pl.BlockSpec(memory_space=pltpu.SMEM)
LIMIT = pltpu.CompilerParams(vmem_limit_bytes=48 * 1024 * 1024)
TILE = 256


def padded(width):
    return -(-width // 128) * 128


def sort_kernel(position, down, ranked):
    count = down.shape[0]

    @pl.loop(0, count // TILE)
    def _(block):
        start = pl.multiple_of(block * TILE, TILE)
        rows = lax.broadcasted_iota(jnp.int32, (TILE, count), 0) + start
        chosen = (rows == position[...]).astype(jnp.float32).astype(jnp.bfloat16)
        ranked[pl.ds(start, TILE), :] = jnp.dot(
            chosen, down[...], preferred_element_type=jnp.float32
        ).astype(jnp.bfloat16)


def split_sides(block, side):
    rows = block.shape[1] // 2
    pair = block.astype(jnp.float32).reshape(block.shape[0], 2, rows, block.shape[2])
    own = jnp.where(side == 0, pair[:, 0], pair[:, 1])
    other = jnp.where(side == 0, pair[:, 1], pair[:, 0])
    flat = (block.shape[0] * rows, block.shape[2])
    return own.reshape(flat).astype(jnp.bfloat16), other.reshape(flat).astype(jnp.bfloat16)


def partial_kernel(widths, side, tokens, ranked, out):
    offset = 0
    for index, width in enumerate(widths):
        left, _ = split_sides(tokens[:, 3 + index], side[0])
        out[:, offset : offset + width] = lax.dot_general(
            left, ranked[:width], (((1,), (1,)), ((), ())), preferred_element_type=jnp.float32
        ).astype(out.dtype)
        offset += width


def banded(widths, sides, array, stored, low_row):
    bounds = (0,) + widths
    starts = (0, widths[0], widths[0] + widths[1])
    features = sides[0].shape[1]
    for band in range(3):
        low, high = bounds[band], bounds[band + 1]
        total = None
        for index in range(band, 3):
            term = lax.dot_general(
                sides[index],
                array[:, starts[index] + low : starts[index] + high],
                (((0,), (0,)), ((), ())),
                preferred_element_type=jnp.float32,
            )
            total = term if total is None else total + term
        stored[low_row : low_row + features, low:high] = total.astype(jnp.bfloat16)


def chosen_ranks(position, start):
    count = position.shape[1]
    ranks_here = lax.broadcasted_iota(jnp.int32, (count, TILE), 0)
    return (ranks_here == position[:, pl.ds(start, TILE)]).astype(jnp.float32).astype(jnp.bfloat16)


def hidden_kernel(
    widths, side, position, pairs, tokens, down_grad, gate_rate, up_rate, hidden, totals
):
    count = position.shape[1]
    features = tokens.shape[3]
    rows = pairs.shape[0] * pairs.shape[2]
    offset = 0
    for width in widths:
        step = 128

        @pl.loop(0, width // step)
        def _(block, offset=offset, width=width):
            start = pl.multiple_of(block * step, step)
            place = pl.ds(offset + start, step)
            for row, which in ((0, side[0]), (rows, 1 - side[0])):
                gate = pairs[:, which, :, pl.ds(2 * offset + start, step)].astype(jnp.float32)
                up = pairs[:, which, :, pl.ds(2 * offset + width + start, step)].astype(jnp.float32)
                gate = gate.reshape(rows, step)
                up = up.reshape(rows, step)
                sigmoid = jax.nn.sigmoid(gate)
                active = gate * sigmoid
                hidden[row : row + rows, place] = (active * up).astype(jnp.bfloat16)
                gate_rate[row : row + rows, place] = up * (sigmoid * (1.0 + gate * (1.0 - sigmoid)))
                up_rate[row : row + rows, place] = active

        offset += width

    sides = [
        jnp.concatenate(split_sides(tokens[:, 3 + index], side[0]), axis=0) for index in range(3)
    ]
    banded(widths, sides, hidden, totals, 0)

    @pl.loop(0, count // TILE)
    def _(block):
        start = pl.multiple_of(block * TILE, TILE)
        moved = jnp.dot(
            totals[...], chosen_ranks(position, start), preferred_element_type=jnp.float32
        )
        down_grad[pl.ds(start, TILE), :] = moved.T.astype(jnp.bfloat16)


def slopes_kernel(
    widths, side, position, own_up, other_up, gate_rate, up_rate, tokens, gate_grad, up_grad, gates, ups, totals
):
    count = position.shape[1]
    features = tokens.shape[3]
    rows = own_up.shape[0]
    step = 128

    @pl.loop(0, sum(widths) // step)
    def _(block):
        place = pl.ds(pl.multiple_of(block * step, step), step)
        for row, above in ((0, own_up), (rows, other_up)):
            upstream = above[:, place].astype(jnp.float32)
            gates[row : row + rows, place] = (
                upstream * gate_rate[row : row + rows, place]
            ).astype(jnp.bfloat16)
            ups[row : row + rows, place] = (
                upstream * up_rate[row : row + rows, place]
            ).astype(jnp.bfloat16)

    sides = [jnp.concatenate(split_sides(tokens[:, index], side[0]), axis=0) for index in range(3)]
    banded(widths, sides, gates, totals, 0)
    banded(widths, sides, ups, totals, features)

    @pl.loop(0, count // TILE)
    def _(block):
        start = pl.multiple_of(block * TILE, TILE)
        moved = jnp.dot(
            totals[...], chosen_ranks(position, start), preferred_element_type=jnp.float32
        )
        gate_grad[:, pl.ds(start, TILE)] = moved[:features].astype(jnp.bfloat16)
        up_grad[:, pl.ds(start, TILE)] = moved[features:].astype(jnp.bfloat16)


def sort_rows(position, down):
    return pl.pallas_call(
        sort_kernel,
        out_shape=jax.ShapeDtypeStruct(down.shape, jnp.bfloat16),
        in_specs=[VMEM, VMEM],
        out_specs=VMEM,
        compiler_params=LIMIT,
    )(position, down)


def partial_of(widths, side, tokens, ranked, dtype):
    rows = tokens.shape[0] * tokens.shape[2] // 2
    return pl.pallas_call(
        functools.partial(partial_kernel, widths),
        out_shape=jax.ShapeDtypeStruct((rows, sum(widths)), dtype),
        in_specs=[SMEM, VMEM, VMEM],
        out_specs=VMEM,
        compiler_params=LIMIT,
        cost_estimate=pl.CostEstimate(
            flops=2 * rows * sum(widths) * tokens.shape[3],
            bytes_accessed=2 * 2**20,
            transcendentals=0,
        ),
    )(side, tokens, ranked)


def after(value, other):
    def nothing(value_ref, other_ref, out_ref):
        pass

    return pl.pallas_call(
        nothing,
        out_shape=jax.ShapeDtypeStruct(value.shape, value.dtype),
        in_specs=[pl.BlockSpec(memory_space=pl.ANY)] * 2,
        out_specs=pl.BlockSpec(memory_space=pl.ANY),
        input_output_aliases={0: 0},
    )(value, other)


def hidden_parts(widths, side, position, pairs, tokens):
    count = position.shape[1]
    rows = 2 * pairs.shape[0] * pairs.shape[2]
    features = tokens.shape[3]
    columns = sum(widths)
    return pl.pallas_call(
        functools.partial(hidden_kernel, widths),
        out_shape=(
            jax.ShapeDtypeStruct((count, features), jnp.bfloat16),
            jax.ShapeDtypeStruct((rows, columns), jnp.float32),
            jax.ShapeDtypeStruct((rows, columns), jnp.float32),
        ),
        in_specs=[SMEM] + [VMEM] * 3,
        out_specs=(VMEM,) * 3,
        scratch_shapes=[
            pltpu.VMEM((rows, columns), jnp.bfloat16),
            pltpu.VMEM((features, count), jnp.bfloat16),
        ],
        compiler_params=LIMIT,
        cost_estimate=pl.CostEstimate(
            flops=2 * features * count * (count + rows), bytes_accessed=8 * 2**20, transcendentals=0
        ),
    )(side, position, pairs, tokens)


def slopes_parts(widths, side, position, own_up, other_up, gate_rate, up_rate, tokens):
    count = position.shape[1]
    rows = 2 * own_up.shape[0]
    features = tokens.shape[3]
    columns = sum(widths)
    return pl.pallas_call(
        functools.partial(slopes_kernel, widths),
        out_shape=(jax.ShapeDtypeStruct((features, count), jnp.bfloat16),) * 2,
        in_specs=[SMEM] + [VMEM] * 6,
        out_specs=(VMEM,) * 2,
        scratch_shapes=[pltpu.VMEM((rows, columns), jnp.bfloat16)] * 2
        + [pltpu.VMEM((2 * features, count), jnp.bfloat16)],
        compiler_params=LIMIT,
        cost_estimate=pl.CostEstimate(
            flops=4 * features * count * (count + rows), bytes_accessed=8 * 2**20, transcendentals=0
        ),
    )(side, position, own_up, other_up, gate_rate, up_rate, tokens)


def per_device(
    ranks, down_weight, inputs, grad_out, gate_small, up_small, gate_mid, up_mid, gate_full, up_full
):
    n_dp = lax.axis_size("dp")
    n_tensor = lax.axis_size("tensor")
    chips = n_dp // 2
    side = (lax.axis_index("dp") % 2)[None]
    swap = [(item, item ^ 1) for item in range(n_dp)]
    by_core = [[2 * chip + side for chip in range(chips)] for side in range(2)]
    widths = tuple(padded(item.shape[1]) for item in (gate_small, gate_mid, gate_full))
    total = sum(widths)

    def copies_to_chips(piece):
        return lax.all_to_all(
            jnp.broadcast_to(piece[None], (chips,) + piece.shape),
            "dp",
            0,
            0,
            axis_index_groups=by_core,
            tiled=True,
        ).reshape(-1, piece.shape[1])

    own = jnp.concatenate([inputs, grad_out], axis=0)
    tokens = lax.all_to_all(
        jnp.broadcast_to(own[None], (n_tensor,) + own.shape), "tensor", 0, 0, tiled=True
    )

    given = ((gate_small, up_small), (gate_mid, up_mid), (gate_full, up_full))
    local = jnp.concatenate(
        [
            jnp.pad(item, ((0, 0), (0, width - item.shape[1])))
            for pair, width in zip(given, widths)
            for item in pair
        ],
        axis=1,
    )
    across = [(item, item ^ 2) for item in range(n_dp)]
    there = lax.ppermute(local, "dp", across)
    first = (lax.axis_index("dp") // 2) % 2 == 0
    two = jnp.concatenate([jnp.where(first, local, there), jnp.where(first, there, local)], axis=0)
    by_side = [
        [4 * row + 2 * half + core for row in range(n_dp // 4) for core in range(2)] for half in range(2)
    ]
    gathered = lax.all_gather(two, "dp", axis=0, axis_index_groups=by_side, tiled=True)
    pairs = gathered.reshape(n_dp // 4, 2, two.shape[0], two.shape[1])

    position = (ranks // n_tensor)[None, :]
    ranked = sort_rows(position, down_weight)

    sent = partial_of(widths, 1 - side, tokens, ranked, jnp.bfloat16)
    other = lax.ppermute(sent, "dp", swap)
    kept = partial_of(widths, side, tokens, ranked, jnp.float32)
    summed = (kept + other.astype(jnp.float32)).astype(jnp.bfloat16)

    pieces = lax.all_to_all(
        summed.reshape(chips, -1, total), "dp", 0, 0, axis_index_groups=by_core, tiled=True
    )
    reduced = jnp.sum(pieces.astype(jnp.float32), axis=0).astype(jnp.bfloat16)
    own_up = copies_to_chips(reduced)
    down_grad, gate_rate, up_rate = hidden_parts(
        widths, side, position, pairs, tokens
    )
    own_up = after(own_up, gate_rate)
    other_up = lax.ppermute(own_up, "dp", swap)

    gate_grad, up_grad = slopes_parts(
        widths, side, position, own_up, other_up, gate_rate, up_rate, tokens
    )
    return (down_grad, gate_grad, up_grad)


def solution(mesh):
    return jax.shard_map(
        per_device,
        mesh=mesh,
        in_specs=(
            P("tensor"),
            P("tensor", "dp"),
            P(None, "tensor", "dp"),
            P(None, "tensor", "dp"),
            P("dp", "tensor"),
            P("dp", "tensor"),
            P("dp", "tensor"),
            P("dp", "tensor"),
            P("dp", "tensor"),
            P("dp", "tensor"),
        ),
        out_specs=(P("tensor", "dp"), P("dp", "tensor"), P("dp", "tensor")),
        check_vma=False,
    )
```

time: 167 us -> 150 us (0.90)
  blocking collectives: 64.1 us -> 35.7 us
  waiting for transfers between devices: 49.3 us -> 31.8 us
  starting transfers between devices: 17 us -> 30.2 us
  Pallas kernels: 15.8 us -> 23 us
  local copies, waits for them, and re-layouts: 5.12 us -> 11.9 us
    all_gather x2 -> x1, waiting for transfers between devices: 31 us -> 0.02 us  [per_device(): lax.all_gather(two, 'dp', axis=0, axis_index_groups=by_side, tiled=True)]
    all_to_all x2 -> x1, blocking collectives: 64.1 us -> 35.7 us  [per_device(): lax.all_to_all(summed.reshape(chips, -1, total), 'dp', 0, 0, axis_index_g...]
    all_to_all x0 -> x1, waiting for transfers between devices: none -> 11.7 us  [copies_to_chips(): lax.all_to_all(jnp.broadcast_to(piece[None], (chips,) + piece.shape), 'dp...]
    ppermute x1 -> x3, starting transfers between devices: 5 us -> 16.4 us  [the longest x1 5.57 us: per_device(): other_up = lax.ppermute(own_up, 'dp', swap)]
    pallas_call x1 -> x3, Pallas kernels: 11.7 us -> 18.9 us  [the longest x1 9.53 us: slopes_parts(): pl.pallas_call(functools.partial(slopes_kernel, widths), out_shape=(jax.S...]
    unnamed x27 -> x17, local copies, waits for them, and re-layouts: 4.06 us -> 9.28 us
    all_to_all x0 -> x1, starting transfers between devices: none -> 3.62 us  [copies_to_chips(): lax.all_to_all(jnp.broadcast_to(piece[None], (chips,) + piece.shape), 'dp...]
    ppermute x1 -> x3, waiting for transfers between devices: 1.31 us -> 3.46 us  [the longest x1 2.15 us: per_device(): other_up = lax.ppermute(own_up, 'dp', swap)]
  transfers between devices with their start and end apart: 4 -> 6, of which waited for: 4 -> 4; matrix products, arithmetic and copies ran while one was open for 0% -> 2% of each run, Pallas kernels for 2% -> 9%
where the time goes in v2:
time: 150 us; the launch traced here: 149 us
  blocking collectives  35.7 us (24%)
  waiting for transfers between devices  31.8 us (21%)
  starting transfers between devices  30.2 us (20%)
  Pallas kernels  23 us (15%)
  between operations  14.2 us (9%)
  local copies, waits for them, and re-layouts  11.9 us (8%)
  other arithmetic  1.76 us (1%)
    all_to_all x1, blocking collectives, per_device(): lax.all_to_all(summed.reshape(chips, -1, total), 'dp', 0, 0, axis_index_g...  35.7 us
    all_to_all x1, waiting for transfers between devices, per_device(): lax.all_to_all(jnp.broadcast_to(own[None], (n_tensor,) + own.shape), 'ten...  16.6 us
    all_to_all x1, waiting for transfers between devices, copies_to_chips(): lax.all_to_all(jnp.broadcast_to(piece[None], (chips,) + piece.shape), 'dp...  11.7 us
    all_to_all x1, starting transfers between devices, per_device(): lax.all_to_all(jnp.broadcast_to(own[None], (n_tensor,) + own.shape), 'ten...  10.2 us
    pallas_call x1, Pallas kernels, slopes_parts(): pl.pallas_call(functools.partial(slopes_kernel, widths), out_shape=(jax.S...  9.53 us
    pallas_call x1, Pallas kernels, hidden_parts(): pl.pallas_call(functools.partial(hidden_kernel, widths), out_shape=(jax.S...  9.35 us
    unnamed x17, local copies, waits for them, and re-layouts  9.28 us
    ppermute x1, starting transfers between devices, per_device(): other_up = lax.ppermute(own_up, 'dp', swap)  5.57 us
  transfers between devices with their start and end apart: 6, of which 4 were waited for; matrix products, arithmetic and copies ran while one was open for 2% of the time, Pallas kernels for 9%

profile of v2, /device:TPU:1, one launch (start us, length us, event | category | flops | bytes accessed | tf_op | source)
XLA Modules:
  0.0 148.6 jit_solution(13537081636491072427)
XLA Ops:
  7.2 0.7 constant_dynamic-update-slice_fusion.5
  7.9 0.7 constant_dynamic-update-slice_fusion.4
  8.6 0.7 constant_dynamic-update-slice_fusion.3
  9.3 0.7 constant_dynamic-update-slice_fusion.2
  10.0 0.8 constant_dynamic-update-slice_fusion.1
  10.8 0.8 constant_dynamic-update-slice_fusion
  11.5 5.5 %collective-permute-start = (bf16[8,6400]{1,0:T(8,128)(2,1)S(1)}, bf16[8,6400]{1,0:T(8,128)(2,1)S(1)}, u32[]{:S(2)}, u32[]{:S(2)}) collective-permute-start(bf16[8,6400]{1,0:T(8,128)(2,1)S(1)} %constant_dynamic-update-slice_fusion), channel_id=1, source_target_pairs={{0,32},{16,48},{32,0},{48,16},{64,96},{80,112},{96,64},{112,80},{1... | collective-permute-start | bytes 307208 | tf_op jit(solution)/shard_map/ppermute | solution.py:271
  17.0 0.8 pad_maximum_fusion.1
  17.8 0.0 copy-start.5
  17.8 0.0 copy-start.4
  17.8 1.0 broadcast_in_dim.20
  18.7 10.2 %all-to-all-start = ((bf16[16,6,16,256]{3,2,1,0:T(8,128)(2,1)}), bf16[16,6,16,256]{3,2,1,0:T(8,128)(2,1)S(1)}, u32[]{:S(2)}, u32[]{:S(2)}) async-start(bf16[16,6,16,256]{3,2,1,0:T(8,128)(2,1)} %broadcast_in_dim.20), calls=%async_computation | async-start | bytes 1572864 | tf_op jit(solution)/shard_map/all_to_all | solution.py:257
  28.9 0.0 all-gather.2.cloned.1.call-start
  29.0 0.0 collective-permute-done
  29.0 0.7 pad_maximum_fusion
  29.7 0.0 all-gather.2.cloned.1.call-update
  29.8 0.0 copy-done.5
  29.8 0.0 copy-done.4
  29.8 2.9 %shard_map.122.ranked = bf16[1792,256]{1,0:T(8,128)(2,1)S(1)} custom-call(s32[1,1792]{1,0:T(1,128)S(1)} %broadcast_in_dim.9.position, bf16[1792,256]{1,0:T(8,128)(2,1)S(1)} %copy-done.4), custom_call_target="tpu_custom_call" | custom-call | tf_op jit(solution)/shard_map/pallas_call | solution.py:152
  32.7 16.6 %all-to-all-done.tokens = bf16[16,6,16,256]{3,2,1,0:T(8,128)(2,1)S(1)} async-done(((bf16[16,6,16,256]{3,2,1,0:T(8,128)(2,1)}), bf16[16,6,16,256]{3,2,1,0:T(8,128)(2,1)S(1)}, u32[]{:S(2)}, u32[]{:S(2)}) %all-to-all-start) | async-done | bytes 786464 | tf_op jit(solution)/shard_map/all_to_all | solution.py:257
  49.3 0.6 shard_map.124
  50.0 5.3 %collective-permute-start.1 = (bf16[128,3200]{1,0:T(8,128)(2,1)S(1)}, bf16[128,3200]{1,0:T(8,128)(2,1)S(1)}, u32[]{:S(2)}, u32[]{:S(2)}) collective-permute-start(bf16[128,3200]{1,0:T(8,128)(2,1)S(1)} %shard_map.124), channel_id=1, source_target_pairs={{0,16},{16,0},{32,48},{48,32},{64,80},{80,64},{96,112},{112,96},{1... | collective-permute-start | bytes 2457608 | tf_op jit(solution)/shard_map/ppermute | solution.py:284
  55.3 0.6 shard_map.123
  55.9 1.3 collective-permute-done.1
  57.2 0.1 fusion
  57.4 35.7 %all_to_all.15 = bf16[16,8,3200]{2,1,0:T(8,128)(2,1)S(1)} all-to-all(bf16[16,8,3200]{2,1,0:T(8,128)(2,1)S(1)} %fusion), channel_id=1, replica_groups={{0,32,64,96,128,160,192,224,256,288,320,352,384,416,448,480},{16,48,80,..., dimensions={0} | all-to-all | bytes 1638400 | tf_op jit(solution)/shard_map/all_to_all | solution.py:288
  93.1 0.1 reduce_sum.12
  93.2 0.9 broadcast_in_dim.21
  94.1 3.6 %all-to-all-start.2 = ((bf16[16,8,3200]{2,1,0:T(8,128)(2,1)}), bf16[16,8,3200]{2,1,0:T(8,128)(2,1)S(1)}, u32[]{:S(2)}, u32[]{:S(2)}) async-start(bf16[16,8,3200]{2,1,0:T(8,128)(2,1)} %broadcast_in_dim.21), calls=%async_computation.2 | async-start | bytes 1638400 | tf_op jit(solution)/shard_map/all_to_all | solution.py:247
  97.8 0.0 all-gather.2.cloned.1.call-done
  97.8 9.4 %shard_map.121 = (bf16[1792,256]{1,0:T(8,128)(2,1)}, f32[256,3200]{1,0:T(8,128)S(1)}, f32[256,3200]{1,0:T(8,128)}) custom-call(s32[1]{0:T(128)} %bitcast.side, s32[1,1792]{1,0:T(1,128)S(1)} %broadcast_in_dim.9.position, bf16[8,2,16,6400]{3,2,1,0:T(8,128)(2,1)} %bitcast.6, bf16[16,6,16,256]{3,2,1,0:T(8,128)(2,1)S(1)} %all-to-all-done.tokens), custom_call_target="tpu_custom_call" | custom-call | flops 1879048192 | bytes 8388608 | tf_op jit(solution)/shard_map/pallas_call | solution.py:195
  107.1 0.0 copy-start.2
  107.1 1.7 %copy-done.2 = f32[256,3200]{1,0:T(8,128)} copy-done((f32[256,3200]{1,0:T(8,128)}, f32[256,3200]{1,0:T(8,128)S(1)}, u32[]{:S(2)}) %copy-start.2) | copy-done | bytes 3276824
  108.9 11.7 %all-to-all-done.2 = bf16[16,8,3200]{2,1,0:T(8,128)(2,1)S(1)} async-done(((bf16[16,8,3200]{2,1,0:T(8,128)(2,1)}), bf16[16,8,3200]{2,1,0:T(8,128)(2,1)S(1)}, u32[]{:S(2)}, u32[]{:S(2)}) %all-to-all-start.2) | async-done | bytes 819232 | tf_op jit(solution)/shard_map/all_to_all | solution.py:247
  120.5 0.0 copy-start
  120.5 0.9 copy-done
  121.4 5.6 %collective-permute-start.2 = (bf16[128,3200]{1,0:T(8,128)(2,1)}, bf16[128,3200]{1,0:T(8,128)(2,1)S(1)}, u32[]{:S(2)}, u32[]{:S(2)}) collective-permute-start(bf16[128,3200]{1,0:T(8,128)(2,1)} %shard_map.125.own_up), channel_id=1, source_target_pairs={{0,16},{16,0},{32,48},{48,32},{64,80},{80,64},{96,112},{112,96},{1... | collective-permute-start | bytes 2457608 | tf_op jit(solution)/shard_map/ppermute | solution.py:297
  127.0 2.1 %collective-permute-done.2.other_up = bf16[128,3200]{1,0:T(8,128)(2,1)S(1)} collective-permute-done((bf16[128,3200]{1,0:T(8,128)(2,1)}, bf16[128,3200]{1,0:T(8,128)(2,1)S(1)}, u32[]{:S(2)}, u32[]{:S(2)}) %collective-permute-start.2) | collective-permute-done | bytes 819232 | tf_op jit(solution)/shard_map/ppermute | solution.py:297
  129.2 0.0 copy-start.1
  129.2 1.1 copy-done.1
  130.3 0.0 copy-start.3
  130.3 1.9 %copy-done.3 = f32[256,3200]{1,0:T(8,128)S(1)} copy-done((f32[256,3200]{1,0:T(8,128)S(1)}, f32[256,3200]{1,0:T(8,128)}, u32[]{:S(2)}) %copy-start.3) | copy-done | bytes 3276824
  132.2 9.5 %shard_map.126 = (bf16[256,1792]{1,0:T(8,128)(2,1)}, bf16[256,1792]{1,0:T(8,128)(2,1)}) custom-call(s32[1]{0:T(128)} %bitcast.side, s32[1,1792]{1,0:T(1,128)S(1)} %broadcast_in_dim.9.position, bf16[128,3200]{1,0:T(8,128)(2,1)S(1)} %copy-done.1, bf16[128,3200]{1,0:T(8,128)(2,1)S(1)} %collective-permute-done.2.other_up, f32[256,3200]{1,0:T(8,128)S(1)} %copy-done.3, ...), custom_call_target="tpu_custom_call" | custom-call | flops 3758096384 | bytes 8388608 | tf_op jit(solution)/shard_map/pallas_call | solution.py:220
  (4 shorter events, 0.0 us)
Async XLA Ops:
  11.5 17.5 %collective-permute-start = (bf16[8,6400]{1,0:T(8,128)(2,1)S(1)}, bf16[8,6400]{1,0:T(8,128)(2,1)S(1)}, u32[]{:S(2)}, u32[]{:S(2)}) collective-permute-start(bf16[8,6400]{1,0:T(8,128)(2,1)S(1)} %constant_dynamic-update-slice_fusion), channel_id=1, source_target_pairs={{0,32},{16,48},{32,0},{48,16},{64,96},{80,112},{96,64},{112,80},{1... | collective-permute-start | bytes 307208 | tf_op jit(solution)/shard_map/ppermute | solution.py:271
  17.8 12.0 %copy-start.5 = (s32[1792]{0:T(1024)S(1)}, s32[1792]{0:T(1024)}, u32[]{:S(2)}) copy-start(s32[1792]{0:T(1024)} %param.10) | copy-start | bytes 21508
  17.8 12.0 %copy-start.4 = (bf16[1792,256]{1,0:T(8,128)(2,1)S(1)}, bf16[1792,256]{1,0:T(8,128)(2,1)}, u32[]{:S(2)}) copy-start(bf16[1792,256]{1,0:T(8,128)(2,1)} %down.1) | copy-start | bytes 2752516
  18.7 30.6 %all-to-all-start = ((bf16[16,6,16,256]{3,2,1,0:T(8,128)(2,1)}), bf16[16,6,16,256]{3,2,1,0:T(8,128)(2,1)S(1)}, u32[]{:S(2)}, u32[]{:S(2)}) async-start(bf16[16,6,16,256]{3,2,1,0:T(8,128)(2,1)} %broadcast_in_dim.20), calls=%async_computation | async-start | bytes 1572864 | tf_op jit(solution)/shard_map/all_to_all | solution.py:257
  28.9 68.9 %all-gather.2.cloned.1.call-start = ((), (), s32[]{:S(2)}) async-start(), calls=%async_computation.3 | async-start | bytes 3481600 | tf_op jit(solution)/shard_map/all_gather | solution.py:277
  50.0 7.3 %collective-permute-start.1 = (bf16[128,3200]{1,0:T(8,128)(2,1)S(1)}, bf16[128,3200]{1,0:T(8,128)(2,1)S(1)}, u32[]{:S(2)}, u32[]{:S(2)}) collective-permute-start(bf16[128,3200]{1,0:T(8,128)(2,1)S(1)} %shard_map.124), channel_id=1, source_target_pairs={{0,16},{16,0},{32,48},{48,32},{64,80},{80,64},{96,112},{112,96},{1... | collective-permute-start | bytes 2457608 | tf_op jit(solution)/shard_map/ppermute | solution.py:284
  94.1 26.4 %all-to-all-start.2 = ((bf16[16,8,3200]{2,1,0:T(8,128)(2,1)}), bf16[16,8,3200]{2,1,0:T(8,128)(2,1)S(1)}, u32[]{:S(2)}, u32[]{:S(2)}) async-start(bf16[16,8,3200]{2,1,0:T(8,128)(2,1)} %broadcast_in_dim.21), calls=%async_computation.2 | async-start | bytes 1638400 | tf_op jit(solution)/shard_map/all_to_all | solution.py:247
  107.1 1.7 %copy-start.2 = (f32[256,3200]{1,0:T(8,128)}, f32[256,3200]{1,0:T(8,128)S(1)}, u32[]{:S(2)}) copy-start(f32[256,3200]{1,0:T(8,128)S(1)} %get-tuple-element.9.other_ref.gate_rate) | copy-start | bytes 9830404
  120.5 0.9 copy-start
  121.4 7.7 %collective-permute-start.2 = (bf16[128,3200]{1,0:T(8,128)(2,1)}, bf16[128,3200]{1,0:T(8,128)(2,1)S(1)}, u32[]{:S(2)}, u32[]{:S(2)}) collective-permute-start(bf16[128,3200]{1,0:T(8,128)(2,1)} %shard_map.125.own_up), channel_id=1, source_target_pairs={{0,16},{16,0},{32,48},{48,32},{64,80},{80,64},{96,112},{112,96},{1... | collective-permute-start | bytes 2457608 | tf_op jit(solution)/shard_map/ppermute | solution.py:297
  129.2 1.1 copy-start.1
  130.3 1.9 %copy-start.3 = (f32[256,3200]{1,0:T(8,128)S(1)}, f32[256,3200]{1,0:T(8,128)}, u32[]{:S(2)}) copy-start(f32[256,3200]{1,0:T(8,128)} %copy-done.2) | copy-start | bytes 9830404
Sparse Core Ops, SparseCore 0:
  32.4 52.0 all-gather.1

commit v3 on v0

v3 whole, which is shorter than its diff:
```python
import functools

import jax
import jax.numpy as jnp
from jax import lax
from jax.experimental import pallas as pl
from jax.experimental.pallas import tpu as pltpu
from jax.sharding import PartitionSpec as P

VMEM = pl.BlockSpec(memory_space=pltpu.VMEM)
ANY = pl.BlockSpec(memory_space=pl.ANY)
SMEM = pl.BlockSpec(memory_space=pltpu.SMEM)
LIMIT = pltpu.CompilerParams(vmem_limit_bytes=20 * 1024 * 1024)
FULL = pltpu.CompilerParams(vmem_limit_bytes=50 * 1024 * 1024)
TILE = 256
STEP = 128


def padded(width):
    return -(-width // 128) * 128


def call(kernel, out_shape, *args, scratch=(), scalars=0, flops=0):
    many = isinstance(out_shape, tuple)
    return pl.pallas_call(
        kernel,
        out_shape=out_shape,
        in_specs=[SMEM] * scalars + [VMEM] * (len(args) - scalars),
        out_specs=(VMEM,) * len(out_shape) if many else VMEM,
        scratch_shapes=list(scratch),
        compiler_params=LIMIT,
        cost_estimate=pl.CostEstimate(flops=flops, bytes_accessed=2**20, transcendentals=0),
    )(*args)


def shaped(shape, dtype=jnp.bfloat16):
    return jax.ShapeDtypeStruct(shape, dtype)


def after(value, other):
    def nothing(value_ref, other_ref, out_ref):
        pass

    return pl.pallas_call(
        nothing,
        out_shape=shaped(value.shape, value.dtype),
        in_specs=[VMEM, VMEM],
        out_specs=VMEM,
        input_output_aliases={0: 0},
        compiler_params=LIMIT,
    )(value, other)


def start_kernel(*refs):
    far, copies, packed = refs[:8], refs[8], refs[9]
    near, sems = refs[10:18], refs[18]
    moves = [
        pltpu.make_async_copy(source, target, sems.at[index])
        for index, (source, target) in enumerate(zip(far, near))
    ]
    for move in moves:
        move.start()
    for move in moves[:6]:
        move.wait()
    offset = 0
    for array in near[:6]:
        width = array.shape[1]
        wide = padded(width)
        if wide != width:
            packed[:, offset : offset + wide] = jnp.zeros((packed.shape[0], wide), packed.dtype)
        packed[:, offset : offset + width] = array[...]
        offset += wide
    for move in moves[6:]:
        move.wait()
    count = near[6].shape[0]

    @pl.loop(0, copies.shape[0])
    def _(place):
        copies[place, :count] = near[6][...]
        copies[place, count:] = near[7][...]


def sort_kernel(position, down, ranked, chosen):
    count = down.shape[0]

    @pl.loop(0, count // TILE)
    def _(block):
        here = pl.ds(pl.multiple_of(block * TILE, TILE), TILE)
        rows = lax.broadcasted_iota(jnp.int32, (TILE, count), 0) + block * TILE
        ones = (rows == position[...]).astype(jnp.float32).astype(jnp.bfloat16)
        chosen[here, :] = ones
        ranked[here, :] = jnp.dot(ones, down[...], preferred_element_type=jnp.float32).astype(
            jnp.bfloat16
        )


def split_sides(block, side):
    rows = block.shape[1] // 2
    pair = block.astype(jnp.float32).reshape(block.shape[0], 2, rows, block.shape[2])
    own = jnp.where(side == 0, pair[:, 0], pair[:, 1])
    other = jnp.where(side == 0, pair[:, 1], pair[:, 0])
    flat = (block.shape[0] * rows, block.shape[2])
    return own.reshape(flat), other.reshape(flat)


def partial_kernel(widths, side, tokens, ranked, out):
    offset = 0
    for index, width in enumerate(widths):
        left, _ = split_sides(tokens[:, 3 + index], side[0])
        out[:, offset : offset + width] = lax.dot_general(
            left.astype(jnp.bfloat16),
            ranked[:width],
            (((1,), (1,)), ((), ())),
            preferred_element_type=jnp.float32,
        ).astype(out.dtype)
        offset += width


def banded(widths, across, stacked, stored, low_row):
    bounds = (0,) + widths
    features, tokens = across.shape[0], across.shape[1] // 3
    for band in range(3):
        low, high = bounds[band], bounds[band + 1]
        stored[low_row : low_row + features, low:high] = jnp.dot(
            across[:, band * tokens :],
            stacked[band * tokens :, low:high],
            preferred_element_type=jnp.float32,
        ).astype(jnp.bfloat16)


def hidden_kernel(
    widths, side, chosen, pairs, tokens, down_grad, rates, turned, hidden, totals, turned_out
):
    count = chosen.shape[0]
    rows = pairs.shape[0] * pairs.shape[2]
    offset = 0
    for index, width in enumerate(widths):

        @pl.loop(0, width // STEP)
        def _(block, index=index, offset=offset, width=width):
            start = pl.multiple_of(block * STEP, STEP)
            for half, which in ((0, side[0]), (1, 1 - side[0])):
                gate = pairs[:, which, :, pl.ds(2 * offset + start, STEP)].astype(jnp.float32)
                up = pairs[:, which, :, pl.ds(2 * offset + width + start, STEP)].astype(jnp.float32)
                gate = gate.reshape(rows, STEP)
                up = up.reshape(rows, STEP)
                sigmoid = jax.nn.sigmoid(gate)
                active = gate * sigmoid
                low = (2 * index + half) * rows
                hidden[low : low + rows, pl.ds(start, STEP)] = (active * up).astype(jnp.bfloat16)
                place = pl.ds(offset + start, STEP)
                rates[0, half * rows : (half + 1) * rows, place] = up * (
                    sigmoid * (1.0 + gate * (1.0 - sigmoid))
                )
                rates[1, half * rows : (half + 1) * rows, place] = active

        offset += width

    for index in range(6):
        own, other = split_sides(tokens[:, index], side[0])
        target = turned if index < 3 else turned_out
        low = (index % 3) * 2 * rows
        target[:, low : low + 2 * rows] = jnp.concatenate([own, other], axis=0).T.astype(jnp.bfloat16)

    banded(widths, turned_out, hidden, totals, 0)

    @pl.loop(0, count // TILE)
    def _(block):
        here = pl.ds(pl.multiple_of(block * TILE, TILE), TILE)
        moved = jnp.dot(totals[...], chosen[:, here], preferred_element_type=jnp.float32)
        down_grad[here, :] = moved.T.astype(jnp.bfloat16)


def slopes_kernel(
    widths,
    chosen_far,
    own_up,
    other_up,
    rates_far,
    turned,
    gate_grad,
    up_grad,
    chosen,
    rates,
    gates,
    ups,
    totals,
    rate_sems,
    chosen_sems,
):
    count = chosen.shape[0]
    features = turned.shape[0]
    rows = own_up.shape[0]
    blocks = count // TILE
    starts = (0, widths[0], widths[0] + widths[1])

    def rate_copy(index):
        place = pl.ds(starts[index], widths[index])
        return pltpu.make_async_copy(
            rates_far.at[:, :, place], rates.at[:, :, place], rate_sems.at[index]
        )

    def chosen_copy(block):
        here = pl.ds(block * TILE, TILE)
        return pltpu.make_async_copy(
            chosen_far.at[here, :], chosen.at[here, :], chosen_sems.at[block]
        )

    for index in range(3):
        rate_copy(index).start()
    for block in range(blocks):
        chosen_copy(block).start()

    for index, width in enumerate(widths):
        offset = starts[index]
        rate_copy(index).wait()

        @pl.loop(0, width // STEP)
        def _(block, index=index, offset=offset):
            start = pl.multiple_of(block * STEP, STEP)
            place = pl.ds(pl.multiple_of(offset + start, STEP), STEP)
            for half, above in enumerate((own_up, other_up)):
                upstream = above[:, place].astype(jnp.float32)
                source = slice(half * rows, (half + 1) * rows)
                low = (2 * index + half) * rows
                gates[low : low + rows, pl.ds(start, STEP)] = (
                    upstream * rates[0, source, place]
                ).astype(jnp.bfloat16)
                ups[low : low + rows, pl.ds(start, STEP)] = (
                    upstream * rates[1, source, place]
                ).astype(jnp.bfloat16)

    banded(widths, turned, gates, totals, 0)
    banded(widths, turned, ups, totals, features)
    for block in range(blocks):
        chosen_copy(block).wait()

    @pl.loop(0, blocks)
    def _(block):
        here = pl.ds(pl.multiple_of(block * TILE, TILE), TILE)
        moved = jnp.dot(totals[...], chosen[:, here], preferred_element_type=jnp.float32)
        gate_grad[:, here] = moved[:features].astype(jnp.bfloat16)
        up_grad[:, here] = moved[features:].astype(jnp.bfloat16)


def per_device(
    ranks, down_weight, inputs, grad_out, gate_small, up_small, gate_mid, up_mid, gate_full, up_full
):
    n_dp = lax.axis_size("dp")
    n_tensor = lax.axis_size("tensor")
    n_rows = n_dp // 4
    count, features = down_weight.shape
    widths = tuple(padded(item.shape[1]) for item in (gate_small, gate_mid, gate_full))
    total = sum(widths)
    side = (lax.axis_index("dp") % 2)[None]
    core_swap = [(item, item ^ 1) for item in range(n_dp)]
    x_swap = [(item, item ^ 2) for item in range(n_dp)]
    by_place = [[4 * row + place for row in range(n_rows)] for place in range(4)]
    by_half = [
        [4 * row + 2 * half + core for row in range(n_rows) for core in range(2)] for half in range(2)
    ]

    def over_rows(blocks):
        return lax.all_to_all(blocks, "dp", 0, 0, axis_index_groups=by_place, tiled=True)

    given = (gate_small, up_small, gate_mid, up_mid, gate_full, up_full, inputs, grad_out)
    copies, local = pl.pallas_call(
        start_kernel,
        out_shape=(
            shaped((n_tensor, 6) + inputs.shape[1:]),
            shaped((gate_small.shape[0], 2 * total)),
        ),
        in_specs=[ANY] * len(given),
        out_specs=(VMEM, VMEM),
        scratch_shapes=[pltpu.VMEM(item.shape, item.dtype) for item in given]
        + [pltpu.SemaphoreType.DMA((len(given),))],
        compiler_params=FULL,
    )(*given)
    tokens = lax.all_to_all(copies, "tensor", 0, 0, tiled=True)

    position = (ranks // n_tensor)[None, :]
    ranked, chosen = call(
        sort_kernel, (shaped(down_weight.shape), shaped((count, count))), position, down_weight
    )

    there = lax.ppermute(local, "dp", x_swap)
    first = (lax.axis_index("dp") // 2) % 2 == 0
    two = jnp.concatenate([jnp.where(first, local, there), jnp.where(first, there, local)], axis=0)
    gathered = lax.all_gather(two, "dp", axis=0, axis_index_groups=by_half, tiled=True)
    pairs = gathered.reshape(n_rows, 2, two.shape[0], two.shape[1])

    rows = tokens.shape[0] * tokens.shape[2] // 2
    partial = functools.partial(partial_kernel, widths)
    sent = call(partial, shaped((rows, total)), 1 - side, tokens, ranked, scalars=1)
    other = lax.ppermute(sent, "dp", core_swap)
    kept = call(partial, shaped((rows, total), jnp.float32), side, tokens, ranked, scalars=1)
    summed = (kept + other.astype(jnp.float32)).astype(jnp.bfloat16)

    pieces = over_rows(summed.reshape(n_rows, -1, total))
    mine = jnp.sum(pieces.astype(jnp.float32), axis=0)
    theirs = lax.ppermute(mine.astype(jnp.bfloat16), "dp", x_swap)
    reduced = (mine + theirs.astype(jnp.float32)).astype(jnp.bfloat16)
    own_up = over_rows(jnp.broadcast_to(reduced[None], (n_rows,) + reduced.shape)).reshape(rows, total)

    down_grad, rates, turned = call(
        functools.partial(hidden_kernel, widths),
        (
            shaped((count, features)),
            shaped((2, 2 * rows, total), jnp.float32),
            shaped((features, 6 * rows)),
        ),
        side,
        chosen,
        pairs,
        tokens,
        scalars=1,
        scratch=(
            pltpu.VMEM((6 * rows, count), jnp.bfloat16),
            pltpu.VMEM((features, count), jnp.bfloat16),
            pltpu.VMEM((features, 6 * rows), jnp.bfloat16),
        ),
        flops=2 * features * count * (count + rows),
    )
    own_up = after(own_up, turned)
    other_up = lax.ppermute(own_up, "dp", core_swap)
    gate_grad, up_grad = pl.pallas_call(
        functools.partial(slopes_kernel, widths),
        out_shape=(shaped((features, count)),) * 2,
        in_specs=[ANY, VMEM, VMEM, ANY, VMEM],
        out_specs=(VMEM,) * 2,
        scratch_shapes=[
            pltpu.VMEM((count, count), jnp.bfloat16),
            pltpu.VMEM((2, 2 * rows, total), jnp.float32),
            pltpu.VMEM((6 * rows, count), jnp.bfloat16),
            pltpu.VMEM((6 * rows, count), jnp.bfloat16),
            pltpu.VMEM((2 * features, count), jnp.bfloat16),
            pltpu.SemaphoreType.DMA((3,)),
            pltpu.SemaphoreType.DMA((count // TILE,)),
        ],
        compiler_params=FULL,
        cost_estimate=pl.CostEstimate(
            flops=4 * features * count * (count + rows), bytes_accessed=2**24, transcendentals=0
        ),
    )(chosen, own_up, other_up, rates, turned)
    return (down_grad, gate_grad, up_grad)


def solution(mesh):
    return jax.shard_map(
        per_device,
        mesh=mesh,
        in_specs=(
            P("tensor"),
            P("tensor", "dp"),
            P(None, "tensor", "dp"),
            P(None, "tensor", "dp"),
            P("dp", "tensor"),
            P("dp", "tensor"),
            P("dp", "tensor"),
            P("dp", "tensor"),
            P("dp", "tensor"),
            P("dp", "tensor"),
        ),
        out_specs=(P("tensor", "dp"), P("dp", "tensor"), P("dp", "tensor")),
        check_vma=False,
    )
```

time: 749 us -> 152 us (0.20)
  blocking collectives: 432 us -> 33.9 us
  waiting for transfers between devices: 235 us -> 29.8 us
  starting transfers between devices: 0.12 us -> 30.8 us
  Pallas kernels: 0 us -> 24.3 us
  local copies, waits for them, and re-layouts: 35.9 us -> 16.9 us
  matrix products: 17.5 us -> 0 us
  other arithmetic: 13.7 us -> 1.03 us
    all_gather x11 -> x0, blocking collectives: 432 us -> none  [the longest x6 251 us: per_device(): lax.all_gather(for_sending(tuple(local_slopes)), 'dp', axis=0, tiled=True)]
    unnamed x4 -> x1, waiting for transfers between devices: 149 us -> 0.02 us
    reduce_scatter x2 -> x0, waiting for transfers between devices: 86.7 us -> none  [per_device(): upstream = lax.psum_scatter(partials, 'dp', scatter_dimension=0, tiled=True)]
    all_to_all x0 -> x1, blocking collectives: none -> 33.9 us  [over_rows(): lax.all_to_all(blocks, 'dp', 0, 0, axis_index_groups=by_place, tiled=True)]
    pallas_call x0 -> x7, Pallas kernels: none -> 24.3 us  [the longest x1 11.9 us: per_device(): pl.pallas_call(functools.partial(slopes_kernel, widths), out_shape=(shape...]
    all_to_all x0 -> x2, waiting for transfers between devices: none -> 23.4 us  [the longest x1 13.6 us: per_device(): tokens = lax.all_to_all(copies, 'tensor', 0, 0, tiled=True)]
    gather x4 -> x0, local copies, waits for them, and re-layouts: 23 us -> none  [the longest x1 6.06 us: per_device(): gate_grad = jnp.take(gate_total, position, axis=1).astype(jnp.bfloat16)]
    dot_general x15 -> x0, matrix products: 17.5 us -> none  [the longest x12 14.4 us: rows_product(): lax.dot_general(left, right, (((0,), (0,)), ((), ())), preferred_element_...]
  transfers between devices with their start and end apart: 3 -> 7, of which waited for: 2 -> 5; matrix products, arithmetic and copies ran while one was open for 3% -> 1% of each run, Pallas kernels for 0% -> 7%
where the time goes in v3:
time: 152 us; the launch traced here: 151 us
  blocking collectives  33.9 us (22%)
  starting transfers between devices  30.8 us (20%)
  waiting for transfers between devices  29.8 us (20%)
  Pallas kernels  24.3 us (16%)
  local copies, waits for them, and re-layouts  16.9 us (11%)
  between operations  14.3 us (9%)
    all_to_all x1, blocking collectives, over_rows(): lax.all_to_all(blocks, 'dp', 0, 0, axis_index_groups=by_place, tiled=True)  33.9 us
    unnamed x28, local copies, waits for them, and re-layouts  16 us
    all_to_all x1, waiting for transfers between devices, per_device(): tokens = lax.all_to_all(copies, 'tensor', 0, 0, tiled=True)  13.6 us
    pallas_call x1, Pallas kernels, per_device(): pl.pallas_call(functools.partial(slopes_kernel, widths), out_shape=(shape...  11.9 us
    pallas_call x4, Pallas kernels, call(): pl.pallas_call(kernel, out_shape=out_shape, in_specs=[SMEM] * scalars + [...  11.2 us
    all_to_all x1, starting transfers between devices, per_device(): tokens = lax.all_to_all(copies, 'tensor', 0, 0, tiled=True)  10.2 us
    all_to_all x1, waiting for transfers between devices, over_rows(): lax.all_to_all(blocks, 'dp', 0, 0, axis_index_groups=by_place, tiled=True)  9.8 us
    ppermute x1, starting transfers between devices, per_device(): there = lax.ppermute(local, 'dp', x_swap)  5.48 us
  transfers between devices with their start and end apart: 7, of which 5 were waited for; matrix products, arithmetic and copies ran while one was open for 1% of the time, Pallas kernels for 7%

profile of v3, /device:TPU:1, one launch (start us, length us, event | category | flops | bytes accessed | tf_op | source)
XLA Modules:
  0.0 151.1 jit_solution(1050166054089374799)
XLA Ops:
  7.2 0.0 copy-start.5
  7.2 0.7 copy-done.5
  7.9 0.0 copy-start.6
  7.9 0.7 copy-done.6
  8.7 0.0 copy-start.7
  8.7 0.7 copy-done.7
  9.4 0.0 copy-start.8
  9.4 0.7 copy-done.8
  10.1 0.0 copy-start.9
  10.1 0.7 copy-done.9
  10.9 0.0 copy-start.10
  10.9 0.7 copy-done.10
  11.6 0.7 copy-done.11
  12.3 0.7 copy-done.12
  13.0 1.2 shard_map.122
  14.2 5.5 %collective-permute-start = (bf16[8,6400]{1,0:T(8,128)(2,1)S(1)}, bf16[8,6400]{1,0:T(8,128)(2,1)S(1)}, u32[]{:S(2)}, u32[]{:S(2)}) collective-permute-start(bf16[8,6400]{1,0:T(8,128)(2,1)S(1)} %get-tuple-element.13), channel_id=1, source_target_pairs={{0,32},{16,48},{32,0},{48,16},{64,96},{80,112},{96,64},{112,80},{1... | collective-permute-start | bytes 307208 | tf_op jit(solution)/shard_map/ppermute | solution.py:286
  19.7 10.2 %all-to-all-start = ((bf16[16,6,16,256]{3,2,1,0:T(8,128)(2,1)}), bf16[16,6,16,256]{3,2,1,0:T(8,128)(2,1)S(1)}, u32[]{:S(2)}, u32[]{:S(2)}) async-start(bf16[16,6,16,256]{3,2,1,0:T(8,128)(2,1)} %get-tuple-element.14), calls=%async_computation | async-start | bytes 1572864 | tf_op jit(solution)/shard_map/all_to_all | solution.py:279
  29.9 0.0 all-gather.2.cloned.1.call-start
  30.0 0.0 collective-permute-done
  30.0 0.7 pad_maximum_fusion
  30.7 0.0 all-gather.2.cloned.1.call-update
  30.7 0.0 copy-done.13
  30.8 0.0 copy-done.4
  30.8 3.2 %shard_map.121 = (bf16[1792,256]{1,0:T(8,128)(2,1)S(1)}, bf16[1792,1792]{1,0:T(8,128)(2,1)S(1)}) custom-call(s32[1,1792]{1,0:T(1,128)S(1)} %broadcast_in_dim.13.position, bf16[1792,256]{1,0:T(8,128)(2,1)S(1)} %copy-done.4), custom_call_target="tpu_custom_call" | custom-call | bytes 1048576 | tf_op jit(solution)/shard_map/pallas_call | solution.py:25
  34.0 0.0 copy-start
  34.0 2.7 %copy-done = bf16[1792,1792]{1,0:T(8,128)(2,1)} copy-done((bf16[1792,1792]{1,0:T(8,128)(2,1)}, bf16[1792,1792]{1,0:T(8,128)(2,1)S(1)}, u32[]{:S(2)}) %copy-start) | copy-done | bytes 6422552
  36.7 13.6 %all-to-all-done.tokens = bf16[16,6,16,256]{3,2,1,0:T(8,128)(2,1)S(1)} async-done(((bf16[16,6,16,256]{3,2,1,0:T(8,128)(2,1)}), bf16[16,6,16,256]{3,2,1,0:T(8,128)(2,1)S(1)}, u32[]{:S(2)}, u32[]{:S(2)}) %all-to-all-start) | async-done | bytes 786464 | tf_op jit(solution)/shard_map/all_to_all | solution.py:279
  50.3 0.6 shard_map.125
  50.9 5.3 %collective-permute-start.1 = (bf16[128,3200]{1,0:T(8,128)(2,1)S(1)}, bf16[128,3200]{1,0:T(8,128)(2,1)S(1)}, u32[]{:S(2)}, u32[]{:S(2)}) collective-permute-start(bf16[128,3200]{1,0:T(8,128)(2,1)S(1)} %shard_map.125), channel_id=1, source_target_pairs={{0,16},{16,0},{32,48},{48,32},{64,80},{80,64},{96,112},{112,96},{1... | collective-permute-start | bytes 2457608 | tf_op jit(solution)/shard_map/ppermute | solution.py:295
  56.3 0.6 shard_map.124
  56.9 1.3 collective-permute-done.1
  58.2 0.1 add_convert_fusion
  58.3 33.9 %all_to_all.15 = bf16[8,16,3200]{2,1,0:T(8,128)(2,1)S(1)} all-to-all(bf16[8,16,3200]{2,1,0:T(8,128)(2,1)S(1)} %bitcast.6), channel_id=1, replica_groups={{0,64,128,192,256,320,384,448},{16,80,144,208,272,336,400,464},{32,96,1..., dimensions={0} | all-to-all | bytes 1638400 | tf_op jit(solution)/shard_map/all_to_all | solution.py:264
  92.3 0.1 convert_reduce_fusion
  92.4 3.8 %collective-permute-start.2 = (bf16[16,3200]{1,0:T(8,128)(2,1)S(1)}, bf16[16,3200]{1,0:T(8,128)(2,1)S(1)}, u32[]{:S(2)}, u32[]{:S(2)}) collective-permute-start(bf16[16,3200]{1,0:T(8,128)(2,1)S(1)} %convert_element_type.21), channel_id=1, source_target_pairs={{0,32},{16,48},{32,0},{48,16},{64,96},{80,112},{96,64},{112,80},{1... | collective-permute-start | bytes 307208 | tf_op jit(solution)/shard_map/ppermute | solution.py:301
  96.2 3.1 %collective-permute-done.2 = bf16[16,3200]{1,0:T(8,128)(2,1)S(1)} collective-permute-done((bf16[16,3200]{1,0:T(8,128)(2,1)S(1)}, bf16[16,3200]{1,0:T(8,128)(2,1)S(1)}, u32[]{:S(2)}, u32[]{:S(2)}) %collective-permute-start.2) | collective-permute-done | bytes 102432 | tf_op jit(solution)/shard_map/ppermute | solution.py:301
  99.4 0.9 broadcast_in_dim.14
  100.3 3.5 %all-to-all-start.2 = ((bf16[8,16,3200]{2,1,0:T(8,128)(2,1)}), bf16[8,16,3200]{2,1,0:T(8,128)(2,1)S(1)}, u32[]{:S(2)}, u32[]{:S(2)}) async-start(bf16[8,16,3200]{2,1,0:T(8,128)(2,1)} %broadcast_in_dim.14), calls=%async_computation.2 | async-start | bytes 1638400 | tf_op jit(solution)/shard_map/all_to_all | solution.py:264
  103.9 0.0 all-gather.2.cloned.1.call-done
  103.9 0.0 copy-start.1
  103.9 2.8 %copy-done.1 = bf16[1792,1792]{1,0:T(8,128)(2,1)S(1)} copy-done((bf16[1792,1792]{1,0:T(8,128)(2,1)S(1)}, bf16[1792,1792]{1,0:T(8,128)(2,1)}, u32[]{:S(2)}) %copy-start.1) | copy-done | bytes 6422552
  106.7 1.9 %copy-done.3 = bf16[256,6400]{1,0:T(8,128)(2,1)S(1)} copy-done((bf16[256,6400]{1,0:T(8,128)(2,1)S(1)}, bf16[256,6400]{1,0:T(8,128)(2,1)}, u32[]{:S(2)}) %copy-start.3) | copy-done | bytes 3276824
  108.7 6.8 %shard_map.123 = (bf16[1792,256]{1,0:T(8,128)(2,1)}, f32[2,256,3200]{2,1,0:T(8,128)S(1)}, bf16[256,768]{1,0:T(8,128)(2,1)S(1)}) custom-call(s32[1]{0:T(128)} %bitcast.side, bf16[1792,1792]{1,0:T(8,128)(2,1)S(1)} %copy-done.1, bf16[8,2,16,6400]{3,2,1,0:T(8,128)(2,1)S(1)} %bitcast.5, bf16[16,6,16,256]{3,2,1,0:T(8,128)(2,1)S(1)} %all-to-all-done.tokens), custom_call_target="tpu_custom_call" | custom-call | flops 1761607680 | bytes 1048576 | tf_op jit(solution)/shard_map/pallas_call | solution.py:25
  115.4 2.7 %copy-done.2 = f32[2,256,3200]{2,1,0:T(8,128)} copy-done((f32[2,256,3200]{2,1,0:T(8,128)}, f32[2,256,3200]{2,1,0:T(8,128)S(1)}, u32[]{:S(2)}) %copy-start.2) | copy-done | bytes 6553624
  118.2 9.8 %all-to-all-done.2 = bf16[8,16,3200]{2,1,0:T(8,128)(2,1)S(1)} async-done(((bf16[8,16,3200]{2,1,0:T(8,128)(2,1)}), bf16[8,16,3200]{2,1,0:T(8,128)(2,1)S(1)}, u32[]{:S(2)}, u32[]{:S(2)}) %all-to-all-start.2) | async-done | bytes 819232 | tf_op jit(solution)/shard_map/all_to_all | solution.py:264
  128.0 2.5 %collective-permute-start.3 = (bf16[128,3200]{1,0:T(8,128)(2,1)S(1)}, bf16[128,3200]{1,0:T(8,128)(2,1)S(1)}, u32[]{:S(2)}, u32[]{:S(2)}) collective-permute-start(bf16[128,3200]{1,0:T(8,128)(2,1)S(1)} %shard_map.126.own_up), channel_id=1, source_target_pairs={{0,16},{16,0},{32,48},{48,32},{64,80},{80,64},{96,112},{112,96},{1... | collective-permute-start | bytes 2457608 | tf_op jit(solution)/shard_map/ppermute | solution.py:325
  130.5 1.9 %collective-permute-done.3.other_up = bf16[128,3200]{1,0:T(8,128)(2,1)S(1)} collective-permute-done((bf16[128,3200]{1,0:T(8,128)(2,1)S(1)}, bf16[128,3200]{1,0:T(8,128)(2,1)S(1)}, u32[]{:S(2)}, u32[]{:S(2)}) %collective-permute-start.3) | collective-permute-done | bytes 819232 | tf_op jit(solution)/shard_map/ppermute | solution.py:325
  132.4 11.9 %shard_map.127 = (bf16[256,1792]{1,0:T(8,128)(2,1)}, bf16[256,1792]{1,0:T(8,128)(2,1)}) custom-call(bf16[1792,1792]{1,0:T(8,128)(2,1)} %copy-done, bf16[128,3200]{1,0:T(8,128)(2,1)S(1)} %shard_map.126.own_up, bf16[128,3200]{1,0:T(8,128)(2,1)S(1)} %collective-permute-done.3.other_up, f32[2,256,3200]{2,1,0:T(8,128)} %copy-done.2, ...), custom_call_target="tpu_custom_call" | custom-call | flops 3523215360 | bytes 16777216 | tf_op jit(solution)/shard_map/pallas_call | solution.py:326
  (12 shorter events, 0.1 us)
Async XLA Ops:
  7.2 0.7 copy-start.5
  7.9 0.7 copy-start.6
  8.7 0.7 copy-start.7
  9.4 0.7 copy-start.8
  10.1 0.7 copy-start.9
  10.9 0.7 copy-start.10
  11.6 0.7 copy-start.11
  12.3 0.7 copy-start.12
  13.0 17.8 %copy-start.13 = (s32[1792]{0:T(1024)S(1)}, s32[1792]{0:T(1024)}, u32[]{:S(2)}) copy-start(s32[1792]{0:T(1024)} %param.10) | copy-start | bytes 21508
  13.0 17.8 %copy-start.4 = (bf16[1792,256]{1,0:T(8,128)(2,1)S(1)}, bf16[1792,256]{1,0:T(8,128)(2,1)}, u32[]{:S(2)}) copy-start(bf16[1792,256]{1,0:T(8,128)(2,1)} %down.1) | copy-start | bytes 2752516
  14.2 15.8 %collective-permute-start = (bf16[8,6400]{1,0:T(8,128)(2,1)S(1)}, bf16[8,6400]{1,0:T(8,128)(2,1)S(1)}, u32[]{:S(2)}, u32[]{:S(2)}) collective-permute-start(bf16[8,6400]{1,0:T(8,128)(2,1)S(1)} %get-tuple-element.13), channel_id=1, source_target_pairs={{0,32},{16,48},{32,0},{48,16},{64,96},{80,112},{96,64},{112,80},{1... | collective-permute-start | bytes 307208 | tf_op jit(solution)/shard_map/ppermute | solution.py:286
  19.7 30.6 %all-to-all-start = ((bf16[16,6,16,256]{3,2,1,0:T(8,128)(2,1)}), bf16[16,6,16,256]{3,2,1,0:T(8,128)(2,1)S(1)}, u32[]{:S(2)}, u32[]{:S(2)}) async-start(bf16[16,6,16,256]{3,2,1,0:T(8,128)(2,1)} %get-tuple-element.14), calls=%async_computation | async-start | bytes 1572864 | tf_op jit(solution)/shard_map/all_to_all | solution.py:279
  29.9 74.0 %all-gather.2.cloned.1.call-start = ((), (), s32[]{:S(2)}) async-start(), calls=%async_computation.3 | async-start | bytes 3481600 | tf_op jit(solution)/shard_map/all_gather | solution.py:289
  34.0 2.7 %copy-start = (bf16[1792,1792]{1,0:T(8,128)(2,1)}, bf16[1792,1792]{1,0:T(8,128)(2,1)S(1)}, u32[]{:S(2)}) copy-start(bf16[1792,1792]{1,0:T(8,128)(2,1)S(1)} %get-tuple-element.12.chosen.chosen_far) | copy-start | bytes 19267588
  50.9 7.3 %collective-permute-start.1 = (bf16[128,3200]{1,0:T(8,128)(2,1)S(1)}, bf16[128,3200]{1,0:T(8,128)(2,1)S(1)}, u32[]{:S(2)}, u32[]{:S(2)}) collective-permute-start(bf16[128,3200]{1,0:T(8,128)(2,1)S(1)} %shard_map.125), channel_id=1, source_target_pairs={{0,16},{16,0},{32,48},{48,32},{64,80},{80,64},{96,112},{112,96},{1... | collective-permute-start | bytes 2457608 | tf_op jit(solution)/shard_map/ppermute | solution.py:295
  92.4 6.9 %collective-permute-start.2 = (bf16[16,3200]{1,0:T(8,128)(2,1)S(1)}, bf16[16,3200]{1,0:T(8,128)(2,1)S(1)}, u32[]{:S(2)}, u32[]{:S(2)}) collective-permute-start(bf16[16,3200]{1,0:T(8,128)(2,1)S(1)} %convert_element_type.21), channel_id=1, source_target_pairs={{0,32},{16,48},{32,0},{48,16},{64,96},{80,112},{96,64},{112,80},{1... | collective-permute-start | bytes 307208 | tf_op jit(solution)/shard_map/ppermute | solution.py:301
  100.3 27.7 %all-to-all-start.2 = ((bf16[8,16,3200]{2,1,0:T(8,128)(2,1)}), bf16[8,16,3200]{2,1,0:T(8,128)(2,1)S(1)}, u32[]{:S(2)}, u32[]{:S(2)}) async-start(bf16[8,16,3200]{2,1,0:T(8,128)(2,1)} %broadcast_in_dim.14), calls=%async_computation.2 | async-start | bytes 1638400 | tf_op jit(solution)/shard_map/all_to_all | solution.py:264
  103.9 2.8 %copy-start.1 = (bf16[1792,1792]{1,0:T(8,128)(2,1)S(1)}, bf16[1792,1792]{1,0:T(8,128)(2,1)}, u32[]{:S(2)}) copy-start(bf16[1792,1792]{1,0:T(8,128)(2,1)} %copy-done) | copy-start | bytes 19267588
  106.7 1.9 %copy-start.3 = (bf16[256,6400]{1,0:T(8,128)(2,1)S(1)}, bf16[256,6400]{1,0:T(8,128)(2,1)}, u32[]{:S(2)}) copy-start(bf16[256,6400]{1,0:T(8,128)(2,1)} %all-gather.2.cloned.1.call-done) | copy-start | bytes 9830404
  115.4 2.7 %copy-start.2 = (f32[2,256,3200]{2,1,0:T(8,128)}, f32[2,256,3200]{2,1,0:T(8,128)S(1)}, u32[]{:S(2)}) copy-start(f32[2,256,3200]{2,1,0:T(8,128)S(1)} %get-tuple-element.18.rates_far) | copy-start | bytes 19660804
  128.0 4.4 %collective-permute-start.3 = (bf16[128,3200]{1,0:T(8,128)(2,1)S(1)}, bf16[128,3200]{1,0:T(8,128)(2,1)S(1)}, u32[]{:S(2)}, u32[]{:S(2)}) collective-permute-start(bf16[128,3200]{1,0:T(8,128)(2,1)S(1)} %shard_map.126.own_up), channel_id=1, source_target_pairs={{0,16},{16,0},{32,48},{48,32},{64,80},{80,64},{96,112},{112,96},{1... | collective-permute-start | bytes 2457608 | tf_op jit(solution)/shard_map/ppermute | solution.py:325
Sparse Core Ops, SparseCore 0:
  33.4 53.1 all-gather.1

commit v4 on v3

v4 whole, which is shorter than its diff:
```python
import functools

import jax
import jax.numpy as jnp
from jax import lax
from jax.experimental import pallas as pl
from jax.experimental.pallas import tpu as pltpu
from jax.sharding import PartitionSpec as P

VMEM = pl.BlockSpec(memory_space=pltpu.VMEM)
ANY = pl.BlockSpec(memory_space=pl.ANY)
SMEM = pl.BlockSpec(memory_space=pltpu.SMEM)
LIMIT = pltpu.CompilerParams(vmem_limit_bytes=20 * 1024 * 1024)
FULL = pltpu.CompilerParams(vmem_limit_bytes=60 * 1024 * 1024)
TILE = 256
WEIGHT = 60
STEP = 128


def padded(width):
    return -(-width // 128) * 128


def call(kernel, out_shape, *args, scratch=(), scalars=0, flops=0):
    many = isinstance(out_shape, tuple)
    return pl.pallas_call(
        kernel,
        out_shape=out_shape,
        in_specs=[SMEM] * scalars + [VMEM] * (len(args) - scalars),
        out_specs=(VMEM,) * len(out_shape) if many else VMEM,
        scratch_shapes=list(scratch),
        compiler_params=LIMIT,
        cost_estimate=pl.CostEstimate(flops=flops, bytes_accessed=2**20, transcendentals=0),
    )(*args)


def shaped(shape, dtype=jnp.bfloat16):
    return jax.ShapeDtypeStruct(shape, dtype)


def after(value, other):
    def nothing(value_ref, other_ref, out_ref):
        pass

    return pl.pallas_call(
        nothing,
        out_shape=shaped(value.shape, value.dtype),
        in_specs=[VMEM, VMEM],
        out_specs=VMEM,
        input_output_aliases={0: 0},
        compiler_params=LIMIT,
    )(value, other)


def start_kernel(*refs):
    far, copies, packed = refs[:8], refs[8], refs[9]
    near, sems = refs[10:18], refs[18]
    moves = [
        pltpu.make_async_copy(source, target, sems.at[index])
        for index, (source, target) in enumerate(zip(far, near))
    ]
    for move in moves:
        move.start()
    for move in moves[:6]:
        move.wait()
    offset = 0
    for array in near[:6]:
        width = array.shape[1]
        wide = padded(width)
        if wide != width:
            packed[:, offset : offset + wide] = jnp.zeros((packed.shape[0], wide), packed.dtype)
        packed[:, offset : offset + width] = array[...]
        offset += wide
    for move in moves[6:]:
        move.wait()
    count = near[6].shape[0]

    @pl.loop(0, copies.shape[0])
    def _(place):
        copies[place, :count] = near[6][...]
        copies[place, count:] = near[7][...]


def sort_kernel(position, down, ranked, chosen):
    count = down.shape[0]

    @pl.loop(0, count // TILE)
    def _(block):
        here = pl.ds(pl.multiple_of(block * TILE, TILE), TILE)
        rows = lax.broadcasted_iota(jnp.int32, (TILE, count), 0) + block * TILE
        ones = (rows == position[...]).astype(jnp.float32).astype(jnp.bfloat16)
        chosen[here, :] = ones
        ranked[here, :] = jnp.dot(ones, down[...], preferred_element_type=jnp.float32).astype(
            jnp.bfloat16
        )


def pick(pair, place):
    return jnp.where(place == 0, pair[0], pair[1])


def group_of(block, core, half):
    places, rows, features = block.shape
    apart = block.astype(jnp.float32).reshape(places // 2, 2, 2, rows // 2, features)
    mine = pick((apart[:, 0], apart[:, 1]), half)
    return pick((mine[:, 0], mine[:, 1]), core).reshape(places * rows // 4, features)


def partial_kernel(widths, where, tokens, ranked, *rest):
    out = rest[-1]
    offset = 0
    for index, width in enumerate(widths):
        left = group_of(tokens[:, 3 + index], where[0], where[1])
        out[:, offset : offset + width] = lax.dot_general(
            left.astype(jnp.bfloat16),
            ranked[:width],
            (((1,), (1,)), ((), ())),
            preferred_element_type=jnp.float32,
        ).astype(out.dtype)
        offset += width


def banded(widths, across, stacked):
    bounds = (0,) + widths
    tokens = across.shape[1] // 3
    for band in range(3):
        low, high = bounds[band], bounds[band + 1]
        yield slice(low, high), jnp.dot(
            across[:, band * tokens :],
            stacked[band * tokens :, low:high],
            preferred_element_type=jnp.float32,
        )


def hidden_kernel(
    widths, where, chosen, pairs, tokens, down_grad, rates, turned, flag, hidden, totals, turned_out
):
    flag[...] = jnp.zeros_like(flag)
    count = chosen.shape[0]
    features = tokens.shape[3]
    rows = pairs.shape[0] * 8
    offset = 0
    for index, width in enumerate(widths):

        @pl.loop(0, width // STEP)
        def _(block, index=index, offset=offset, width=width):
            start = pl.multiple_of(block * STEP, STEP)
            for core in range(2):
                which = jnp.where(core == 0, where[0], 1 - where[0])
                gates = pairs[:, which, :, pl.ds(2 * offset + start, STEP)].astype(jnp.float32)
                ups = pairs[:, which, :, pl.ds(2 * offset + width + start, STEP)].astype(jnp.float32)
                gates = gates.reshape(-1, 2, 8, STEP)
                ups = ups.reshape(-1, 2, 8, STEP)
                for half in range(2):
                    gate = gates[:, half].reshape(rows, STEP)
                    up = ups[:, half].reshape(rows, STEP)
                    sigmoid = jax.nn.sigmoid(gate)
                    active = gate * sigmoid
                    group = (2 * half + core) * rows
                    low = 4 * index * rows + group
                    hidden[low : low + rows, pl.ds(start, STEP)] = (active * up).astype(jnp.bfloat16)
                    place = pl.ds(pl.multiple_of(offset + start, STEP), STEP)
                    rates[0, group : group + rows, place] = up * (
                        sigmoid * (1.0 + gate * (1.0 - sigmoid))
                    )
                    rates[1, group : group + rows, place] = active

        offset += width

    for index in range(6):
        block = tokens[:, index]
        for half in range(2):
            pair = [
                group_of(block, jnp.where(core == 0, where[0], 1 - where[0]), (where[1] + half) % 2)
                for core in range(2)
            ]
            flipped = jnp.concatenate(pair, axis=0).T.astype(jnp.bfloat16)
            if index < 3:
                turned[half, :, 2 * index * rows : 2 * (index + 1) * rows] = flipped
            else:
                low = (4 * (index - 3) + 2 * half) * rows
                turned_out[:, low : low + 2 * rows] = flipped

    for columns, product in banded(widths, turned_out, hidden):
        totals[:, columns] = product.astype(jnp.bfloat16)

    @pl.loop(0, count // TILE)
    def _(block):
        here = pl.ds(pl.multiple_of(block * TILE, TILE), TILE)
        moved = jnp.dot(totals[...], chosen[:, here], preferred_element_type=jnp.float32)
        down_grad[here, :] = moved.T.astype(jnp.bfloat16)


def slopes_of(widths, half, first, second, rates, gates, ups):
    rows = first.shape[0]
    offset = 0
    for index, width in enumerate(widths):

        @pl.loop(0, width // STEP)
        def _(block, index=index, offset=offset):
            start = pl.multiple_of(block * STEP, STEP)
            place = pl.ds(pl.multiple_of(offset + start, STEP), STEP)
            for core, above in enumerate((first, second)):
                upstream = above[:, place].astype(jnp.float32)
                source = slice((2 * half + core) * rows, (2 * half + core + 1) * rows)
                low = (2 * index + core) * rows
                gates[low : low + rows, pl.ds(start, STEP)] = (
                    upstream * rates[0, source, place]
                ).astype(jnp.bfloat16)
                ups[low : low + rows, pl.ds(start, STEP)] = (
                    upstream * rates[1, source, place]
                ).astype(jnp.bfloat16)

        offset += width


def first_kernel(widths, first, second, rates, turned, sums, gates, ups):
    features = turned.shape[1]
    slopes_of(widths, 0, first, second, rates, gates, ups)
    for place, array in enumerate((gates, ups)):
        for columns, product in banded(widths, turned[0], array):
            sums[place * features : (place + 1) * features, columns] = product


def second_kernel(
    widths, chosen, first, second, rates, turned, sums, gate_grad, up_grad, gates, ups, totals
):
    count = chosen.shape[0]
    features = turned.shape[1]
    slopes_of(widths, 1, first, second, rates, gates, ups)
    for place, array in enumerate((gates, ups)):
        for columns, product in banded(widths, turned[1], array):
            low = slice(place * features, (place + 1) * features)
            totals[low, columns] = (sums[low, columns] + product).astype(jnp.bfloat16)

    @pl.loop(0, count // TILE)
    def _(block):
        here = pl.ds(pl.multiple_of(block * TILE, TILE), TILE)
        moved = jnp.dot(totals[...], chosen[:, here], preferred_element_type=jnp.float32)
        gate_grad[:, here] = moved[:features].astype(jnp.bfloat16)
        up_grad[:, here] = moved[features:].astype(jnp.bfloat16)


def per_device(
    ranks, down_weight, inputs, grad_out, gate_small, up_small, gate_mid, up_mid, gate_full, up_full
):
    n_dp = lax.axis_size("dp")
    n_tensor = lax.axis_size("tensor")
    n_rows = n_dp // 4
    count, features = down_weight.shape
    widths = tuple(padded(item.shape[1]) for item in (gate_small, gate_mid, gate_full))
    total = sum(widths)
    place = lax.axis_index("dp")
    core, half = place % 2, (place // 2) % 2
    core_swap = [(item, item ^ 1) for item in range(n_dp)]
    x_swap = [(item, item ^ 2) for item in range(n_dp)]
    by_place = [[4 * row + place for row in range(n_rows)] for place in range(4)]
    by_half = [
        [4 * row + 2 * half + core for row in range(n_rows) for core in range(2)] for half in range(2)
    ]

    def over_rows(blocks):
        return lax.all_to_all(blocks, "dp", 0, 0, axis_index_groups=by_place, tiled=True)

    given = (gate_small, up_small, gate_mid, up_mid, gate_full, up_full, inputs, grad_out)
    copies, local = pl.pallas_call(
        start_kernel,
        out_shape=(
            shaped((n_tensor, 6) + inputs.shape[1:]),
            shaped((gate_small.shape[0], 2 * total)),
        ),
        in_specs=[ANY] * len(given),
        out_specs=(VMEM, VMEM),
        scratch_shapes=[pltpu.VMEM(item.shape, item.dtype) for item in given]
        + [pltpu.SemaphoreType.DMA((len(given),))],
        compiler_params=FULL,
    )(*given)
    tokens = lax.all_to_all(copies, "tensor", 0, 0, tiled=True)

    position = (ranks // n_tensor)[None, :]
    ranked, chosen = call(
        sort_kernel,
        (shaped(down_weight.shape), shaped((count, count))),
        position,
        down_weight,
        flops=2 * count * count * features,
    )

    there = lax.ppermute(local, "dp", x_swap)
    two = jnp.concatenate([local, there], axis=0)
    gathered = lax.all_gather(two, "dp", axis=0, axis_index_groups=by_half, tiled=True)
    pairs = gathered.reshape(n_rows, 2, two.shape[0], two.shape[1])

    rows = tokens.shape[0] * tokens.shape[2] // 4

    def partial(core, half, dtype, *behind):
        return call(
            functools.partial(partial_kernel, widths),
            shaped((rows, total), dtype),
            jnp.stack([core, half]),
            tokens,
            ranked,
            *behind,
            scalars=1,
            flops=2 * WEIGHT * rows * total * features,
        )

    def core_sum(half, *behind):
        sent = partial(1 - core, half, jnp.bfloat16, *behind)
        other = lax.ppermute(sent, "dp", core_swap)
        return partial(core, half, jnp.float32) + other.astype(jnp.float32), sent

    across, behind = core_sum(1 - half)
    far = lax.ppermute(across.astype(jnp.bfloat16), "dp", x_swap)
    summed = (core_sum(half, behind)[0] + far.astype(jnp.float32)).astype(jnp.bfloat16)
    pieces = over_rows(summed.reshape(n_rows, -1, total))
    reduced = jnp.sum(pieces.astype(jnp.float32), axis=0).astype(jnp.bfloat16)
    near = over_rows(jnp.broadcast_to(reduced[None], (n_rows,) + reduced.shape)).reshape(rows, total)

    down_grad, rates, turned, flag = call(
        functools.partial(hidden_kernel, widths),
        (
            shaped((count, features)),
            shaped((2, 4 * rows, total), jnp.float32),
            shaped((2, features, 6 * rows)),
            shaped((8, 128), jnp.float32),
        ),
        jnp.stack([core, half]),
        chosen,
        pairs,
        tokens,
        scalars=1,
        scratch=(
            pltpu.VMEM((12 * rows, count), jnp.bfloat16),
            pltpu.VMEM((features, count), jnp.bfloat16),
            pltpu.VMEM((features, 12 * rows), jnp.bfloat16),
        ),
        flops=2 * features * count * (count + rows),
    )
    near = after(near, flag)
    beyond = lax.ppermute(near, "dp", x_swap)
    near_other = lax.ppermute(near, "dp", core_swap)
    halves = (pltpu.VMEM((6 * rows, count), jnp.bfloat16),) * 2
    sums = call(
        functools.partial(first_kernel, widths),
        shaped((2 * features, count), jnp.float32),
        near,
        near_other,
        rates,
        turned,
        scratch=halves,
        flops=4 * features * count * rows,
    )
    beyond = after(beyond, sums)
    beyond_other = lax.ppermute(beyond, "dp", core_swap)
    gate_grad, up_grad = call(
        functools.partial(second_kernel, widths),
        (shaped((features, count)),) * 2,
        chosen,
        beyond,
        beyond_other,
        rates,
        turned,
        sums,
        scratch=halves + (pltpu.VMEM((2 * features, count), jnp.bfloat16),),
        flops=4 * features * count * (count + rows),
    )
    return (down_grad, gate_grad, up_grad)


def solution(mesh):
    return jax.shard_map(
        per_device,
        mesh=mesh,
        in_specs=(
            P("tensor"),
            P("tensor", "dp"),
            P(None, "tensor", "dp"),
            P(None, "tensor", "dp"),
            P("dp", "tensor"),
            P("dp", "tensor"),
            P("dp", "tensor"),
            P("dp", "tensor"),
            P("dp", "tensor"),
            P("dp", "tensor"),
        ),
        out_specs=(P("tensor", "dp"), P("dp", "tensor"), P("dp", "tensor")),
        check_vma=False,
    )
```

time: 152 us -> 148 us (0.974)
  blocking collectives: 33.9 us -> 19.9 us
  starting transfers between devices: 30.8 us -> 41.1 us
  waiting for transfers between devices: 29.8 us -> 26.9 us
  other arithmetic: 1.03 us -> 2.78 us
    all_to_all x1, blocking collectives: 33.9 us -> 19.9 us  [over_rows(): lax.all_to_all(blocks, 'dp', 0, 0, axis_index_groups=by_place, tiled=True)]
    pallas_call x4 -> x8, Pallas kernels: 11.2 us -> 23.3 us  [call(): pl.pallas_call(kernel, out_shape=out_shape, in_specs=[SMEM] * scalars + [...]
    pallas_call x1 -> x0, Pallas kernels: 11.9 us -> none  [per_device(): pl.pallas_call(functools.partial(slopes_kernel, widths), out_shape=(shape...]
    ppermute x3 -> x6, starting transfers between devices: 11.6 us -> 22 us  [the longest x2 7.25 us: core_sum(): other = lax.ppermute(sent, 'dp', core_swap)]
    all_to_all x1, waiting for transfers between devices: 9.8 us -> 0.01 us  [over_rows(): lax.all_to_all(blocks, 'dp', 0, 0, axis_index_groups=by_place, tiled=True)]
    ppermute x3 -> x6, waiting for transfers between devices: 6.36 us -> 16.1 us  [the longest x1 9.11 us: per_device(): far = lax.ppermute(across.astype(jnp.bfloat16), 'dp', x_swap)]
    all_to_all x1, waiting for transfers between devices: 13.6 us -> 10.7 us  [per_device(): tokens = lax.all_to_all(copies, 'tensor', 0, 0, tiled=True)]
    unnamed x28 -> x22, local copies, waits for them, and re-layouts: 16 us -> 16 us
  transfers between devices with their start and end apart: 7 -> 10, of which waited for: 5 -> 4; matrix products, arithmetic and copies ran while one was open for 1% -> 2% of each run, Pallas kernels for 7% -> 11%
where the time goes in v4:
time: 148 us; the launch traced here: 147 us
  starting transfers between devices  41.1 us (28%)
  waiting for transfers between devices  26.9 us (18%)
  Pallas kernels  25.3 us (17%)
  blocking collectives  19.9 us (13%)
  local copies, waits for them, and re-layouts  16.8 us (11%)
  between operations  14.2 us (10%)
  other arithmetic  2.78 us (2%)
    pallas_call x8, Pallas kernels, call(): pl.pallas_call(kernel, out_shape=out_shape, in_specs=[SMEM] * scalars + [...  23.3 us
    all_to_all x1, blocking collectives, over_rows(): lax.all_to_all(blocks, 'dp', 0, 0, axis_index_groups=by_place, tiled=True)  19.9 us
    unnamed x22, local copies, waits for them, and re-layouts  16 us
    all_to_all x1, waiting for transfers between devices, per_device(): tokens = lax.all_to_all(copies, 'tensor', 0, 0, tiled=True)  10.7 us
    all_to_all x1, starting transfers between devices, per_device(): tokens = lax.all_to_all(copies, 'tensor', 0, 0, tiled=True)  10.2 us
    ppermute x1, waiting for transfers between devices, per_device(): far = lax.ppermute(across.astype(jnp.bfloat16), 'dp', x_swap)  9.11 us
    ppermute x2, starting transfers between devices, core_sum(): other = lax.ppermute(sent, 'dp', core_swap)  7.25 us
    ppermute x1, waiting for transfers between devices, per_device(): beyond = lax.ppermute(near, 'dp', x_swap)  5.66 us
  transfers between devices with their start and end apart: 10, of which 4 were waited for; matrix products, arithmetic and copies ran while one was open for 2% of the time, Pallas kernels for 11%

profile of v4, /device:TPU:1, one launch (start us, length us, event | category | flops | bytes accessed | tf_op | source)
XLA Modules:
  0.0 146.9 jit_solution(14498409817500745860)
XLA Ops:
  7.2 1.9 %shard_map.122 = (bf16[16,6,16,256]{3,2,1,0:T(8,128)(2,1)}, bf16[8,6400]{1,0:T(8,128)(2,1)}) custom-call(bf16[8,448]{1,0:T(8,128)(2,1)} %refs_0_.1, bf16[8,448]{1,0:T(8,128)(2,1)} %refs_1_.1, bf16[8,896]{1,0:T(8,128)(2,1)} %refs_2_.1, bf16[8,896]{1,0:T(8,128)(2,1)} %refs_3_.1, bf16[8,1792]{1,0:T(8,128)(2,1)} %refs_4_.1, bf16[8,1792]{1,0:T(8,128)(2,1)} %refs_5_.1, ...), custom_call_target="tpu_custom_call" | custom-call | tf_op jit(solution)/shard_map/pallas_call | solution.py:266
  9.1 5.5 %collective-permute-start = (bf16[8,6400]{1,0:T(8,128)(2,1)}, bf16[8,6400]{1,0:T(8,128)(2,1)S(1)}, u32[]{:S(2)}, u32[]{:S(2)}) collective-permute-start(bf16[8,6400]{1,0:T(8,128)(2,1)} %get-tuple-element.14), channel_id=1, source_target_pairs={{0,32},{16,48},{32,0},{48,16},{64,96},{80,112},{96,64},{112,80},{1... | collective-permute-start | bytes 307208 | tf_op jit(solution)/shard_map/ppermute | solution.py:289
  14.6 10.2 %all-to-all-start = ((bf16[16,6,16,256]{3,2,1,0:T(8,128)(2,1)}), bf16[16,6,16,256]{3,2,1,0:T(8,128)(2,1)S(1)}, u32[]{:S(2)}, u32[]{:S(2)}) async-start(bf16[16,6,16,256]{3,2,1,0:T(8,128)(2,1)} %get-tuple-element.15), calls=%async_computation | async-start | bytes 1572864 | tf_op jit(solution)/shard_map/all_to_all | solution.py:278
  24.8 0.0 all-gather.2.cloned.1.call-start
  24.8 0.0 collective-permute-done
  24.8 1.6 %pad_maximum_fusion = bf16[16,6400]{1,0:T(8,128)(2,1)} fusion(bf16[8,6400]{1,0:T(8,128)(2,1)S(1)} %collective-permute-done, bf16[8,6400]{1,0:T(8,128)(2,1)} %get-tuple-element.14), kind=kLoop, calls=%fused_computation.3 | loop fusion | flops 409600 | bytes 409600 | tf_op jit(solution)/shard_map/concatenate | solution.py:290
  26.4 0.0 all-gather.2.cloned.1.call-update
  26.5 0.7 add_select_fusion
  27.2 0.1 pad_add_fusion.1.where
  27.2 0.1 pad_add_fusion.2.where
  27.3 0.1 pad_add_fusion
  27.4 1.2 copy-done.8
  28.6 3.2 %shard_map.121 = (bf16[1792,256]{1,0:T(8,128)(2,1)S(1)}, bf16[1792,1792]{1,0:T(8,128)(2,1)S(1)}) custom-call(s32[1,1792]{1,0:T(1,128)S(1)} %broadcast_in_dim.4.position, bf16[1792,256]{1,0:T(8,128)(2,1)S(1)} %copy-done.8), custom_call_target="tpu_custom_call" | custom-call | flops 1644167168 | bytes 1048576 | tf_op jit(solution)/shard_map/pallas_call | solution.py:26
  31.8 2.7 %copy-done.3 = bf16[1792,1792]{1,0:T(8,128)(2,1)} copy-done((bf16[1792,1792]{1,0:T(8,128)(2,1)}, bf16[1792,1792]{1,0:T(8,128)(2,1)S(1)}, u32[]{:S(2)}) %copy-start.3) | copy-done | bytes 6422552
  34.5 10.7 %all-to-all-done.tokens = bf16[16,6,16,256]{3,2,1,0:T(8,128)(2,1)S(1)} async-done(((bf16[16,6,16,256]{3,2,1,0:T(8,128)(2,1)}), bf16[16,6,16,256]{3,2,1,0:T(8,128)(2,1)S(1)}, u32[]{:S(2)}, u32[]{:S(2)}) %all-to-all-start) | async-done | bytes 786464 | tf_op jit(solution)/shard_map/all_to_all | solution.py:278
  45.2 1.2 shard_map.125.rest_0_
  46.4 5.3 %collective-permute-start.2 = (bf16[64,3200]{1,0:T(8,128)(2,1)S(1)}, bf16[64,3200]{1,0:T(8,128)(2,1)S(1)}, u32[]{:S(2)}, u32[]{:S(2)}) collective-permute-start(bf16[64,3200]{1,0:T(8,128)(2,1)S(1)} %shard_map.125.rest_0_), channel_id=1, source_target_pairs={{0,16},{16,0},{32,48},{48,32},{64,80},{80,64},{96,112},{112,96},{1... | collective-permute-start | bytes 1228808 | tf_op jit(solution)/shard_map/ppermute | solution.py:310
  51.7 1.2 shard_map.126
  52.9 1.9 %collective-permute-start.1 = (bf16[64,3200]{1,0:T(8,128)(2,1)S(1)}, bf16[64,3200]{1,0:T(8,128)(2,1)S(1)}, u32[]{:S(2)}, u32[]{:S(2)}) collective-permute-start(bf16[64,3200]{1,0:T(8,128)(2,1)S(1)} %shard_map.126), channel_id=1, source_target_pairs={{0,16},{16,0},{32,48},{48,32},{64,80},{80,64},{96,112},{112,96},{1... | collective-permute-start | bytes 1228808 | tf_op jit(solution)/shard_map/ppermute | solution.py:310
  54.8 1.2 shard_map.127
  56.0 0.0 collective-permute-done.2
  56.0 0.1 add_convert_fusion.1
  56.0 3.6 %collective-permute-start.3 = (bf16[64,3200]{1,0:T(8,128)(2,1)S(1)}, bf16[64,3200]{1,0:T(8,128)(2,1)S(1)}, u32[]{:S(2)}, u32[]{:S(2)}) collective-permute-start(bf16[64,3200]{1,0:T(8,128)(2,1)S(1)} %add_convert_fusion.1), channel_id=1, source_target_pairs={{0,32},{16,48},{32,0},{48,16},{64,96},{80,112},{96,64},{112,80},{1... | collective-permute-start | bytes 1228808 | tf_op jit(solution)/shard_map/ppermute | solution.py:314
  59.7 1.2 shard_map.124
  60.9 0.0 collective-permute-done.1
  60.9 9.1 %collective-permute-done.3 = bf16[64,3200]{1,0:T(8,128)(2,1)S(1)} collective-permute-done((bf16[64,3200]{1,0:T(8,128)(2,1)S(1)}, bf16[64,3200]{1,0:T(8,128)(2,1)S(1)}, u32[]{:S(2)}, u32[]{:S(2)}) %collective-permute-start.3) | collective-permute-done | bytes 409632 | tf_op jit(solution)/shard_map/ppermute | solution.py:314
  70.0 0.1 fusion
  70.1 19.9 %all_to_all.15 = bf16[8,8,3200]{2,1,0:T(8,128)(2,1)S(1)} all-to-all(bf16[8,8,3200]{2,1,0:T(8,128)(2,1)S(1)} %fusion), channel_id=1, replica_groups={{0,64,128,192,256,320,384,448},{16,80,144,208,272,336,400,464},{32,96,1..., dimensions={0} | all-to-all | bytes 819200 | tf_op jit(solution)/shard_map/all_to_all | solution.py:263
  90.0 0.1 reduce_sum.12
  90.0 0.8 broadcast_in_dim.10
  90.8 3.5 %all-to-all-start.2 = ((bf16[8,8,3200]{2,1,0:T(8,128)(2,1)}), bf16[8,8,3200]{2,1,0:T(8,128)(2,1)S(1)}, u32[]{:S(2)}, u32[]{:S(2)}) async-start(bf16[8,8,3200]{2,1,0:T(8,128)(2,1)} %broadcast_in_dim.10), calls=%async_computation.2 | async-start | bytes 819200 | tf_op jit(solution)/shard_map/all_to_all | solution.py:263
  94.3 0.0 all-gather.2.cloned.1.call-done
  94.3 2.8 %copy-done.4 = bf16[1792,1792]{1,0:T(8,128)(2,1)S(1)} copy-done((bf16[1792,1792]{1,0:T(8,128)(2,1)S(1)}, bf16[1792,1792]{1,0:T(8,128)(2,1)}, u32[]{:S(2)}) %copy-start.4) | copy-done | bytes 6422552
  97.1 1.9 %copy-done.5 = bf16[256,6400]{1,0:T(8,128)(2,1)S(1)} copy-done((bf16[256,6400]{1,0:T(8,128)(2,1)S(1)}, bf16[256,6400]{1,0:T(8,128)(2,1)}, u32[]{:S(2)}) %copy-start.5) | copy-done | bytes 3276824
  99.1 7.4 %shard_map.123 = (bf16[1792,256]{1,0:T(8,128)(2,1)}, f32[2,256,3200]{2,1,0:T(8,128)S(1)}, bf16[2,256,384]{2,1,0:T(8,128)(2,1)S(1)}, f32[8,128]{1,0:T(8,128)S(1)}) custom-call(s32[2]{0:T(128)S(1)} %pad_add_fusion.1.where, bf16[1792,1792]{1,0:T(8,128)(2,1)S(1)} %copy-done.4, bf16[8,2,16,6400]{3,2,1,0:T(8,128)(2,1)S(1)} %bitcast.11, ...), custom_call_target="tpu_custom_call" | custom-call | flops 1702887424 | bytes 1048576 | tf_op jit(solution)/shard_map/pallas_call | solution.py:26
  106.4 2.7 %copy-done = f32[2,256,3200]{2,1,0:T(8,128)} copy-done((f32[2,256,3200]{2,1,0:T(8,128)}, f32[2,256,3200]{2,1,0:T(8,128)S(1)}, u32[]{:S(2)}) %copy-start) | copy-done | bytes 6553624
  109.2 0.7 copy-done.6
  109.9 0.0 all-to-all-done.2
  109.9 4.7 %collective-permute-start.5 = (bf16[64,3200]{1,0:T(8,128)(2,1)S(1)}, bf16[64,3200]{1,0:T(8,128)(2,1)S(1)}, u32[]{:S(2)}, u32[]{:S(2)}) collective-permute-start(bf16[64,3200]{1,0:T(8,128)(2,1)S(1)} %shard_map.128.first), channel_id=1, source_target_pairs={{0,16},{16,0},{32,48},{48,32},{64,80},{80,64},{96,112},{112,96},{1... | collective-permute-start | bytes 1228808 | tf_op jit(solution)/shard_map/ppermute | solution.py:342
  114.6 3.7 %collective-permute-start.4 = (bf16[64,3200]{1,0:T(8,128)(2,1)S(1)}, bf16[64,3200]{1,0:T(8,128)(2,1)S(1)}, u32[]{:S(2)}, u32[]{:S(2)}) collective-permute-start(bf16[64,3200]{1,0:T(8,128)(2,1)S(1)} %shard_map.128.first), channel_id=1, source_target_pairs={{0,32},{16,48},{32,0},{48,16},{64,96},{80,112},{96,64},{112,80},{1... | collective-permute-start | bytes 1228808 | tf_op jit(solution)/shard_map/ppermute | solution.py:341
  118.3 0.0 collective-permute-done.5.second
  118.3 2.9 %copy-done.1 = f32[2,256,3200]{2,1,0:T(8,128)S(1)} copy-done((f32[2,256,3200]{2,1,0:T(8,128)S(1)}, f32[2,256,3200]{2,1,0:T(8,128)}, u32[]{:S(2)}) %copy-start.1) | copy-done | bytes 6553624
  121.2 1.0 copy-done.7
  122.2 1.2 shard_map.129.other_ref.sums
  123.4 5.7 %collective-permute-done.4.value_ref = bf16[64,3200]{1,0:T(8,128)(2,1)S(1)} collective-permute-done((bf16[64,3200]{1,0:T(8,128)(2,1)S(1)}, bf16[64,3200]{1,0:T(8,128)(2,1)S(1)}, u32[]{:S(2)}, u32[]{:S(2)}) %collective-permute-start.4) | collective-permute-done | bytes 409632 | tf_op jit(solution)/shard_map/ppermute | solution.py:341
  129.1 2.7 %collective-permute-start.6 = (bf16[64,3200]{1,0:T(8,128)(2,1)S(1)}, bf16[64,3200]{1,0:T(8,128)(2,1)S(1)}, u32[]{:S(2)}, u32[]{:S(2)}) collective-permute-start(bf16[64,3200]{1,0:T(8,128)(2,1)S(1)} %shard_map.130.first), channel_id=1, source_target_pairs={{0,16},{16,0},{32,48},{48,32},{64,80},{80,64},{96,112},{112,96},{1... | collective-permute-start | bytes 1228808 | tf_op jit(solution)/shard_map/ppermute | solution.py:355
  131.8 1.4 collective-permute-done.6.second
  133.1 6.9 %shard_map.131 = (bf16[256,1792]{1,0:T(8,128)(2,1)}, bf16[256,1792]{1,0:T(8,128)(2,1)}) custom-call(bf16[1792,1792]{1,0:T(8,128)(2,1)S(1)} %bitcast.9, bf16[64,3200]{1,0:T(8,128)(2,1)S(1)} %shard_map.130.first, bf16[64,3200]{1,0:T(8,128)(2,1)S(1)} %collective-permute-done.6.second, f32[2,256,3200]{2,1,0:T(8,128)S(1)} %copy-done.2, ...), custom_call_target="tpu_custom_call" | custom-call | flops 3405774848 | bytes 1048576 | tf_op jit(solution)/shard_map/pallas_call | solution.py:26
  (18 shorter events, 0.0 us)
Async XLA Ops:
  9.1 15.7 %collective-permute-start = (bf16[8,6400]{1,0:T(8,128)(2,1)}, bf16[8,6400]{1,0:T(8,128)(2,1)S(1)}, u32[]{:S(2)}, u32[]{:S(2)}) collective-permute-start(bf16[8,6400]{1,0:T(8,128)(2,1)} %get-tuple-element.14), channel_id=1, source_target_pairs={{0,32},{16,48},{32,0},{48,16},{64,96},{80,112},{96,64},{112,80},{1... | collective-permute-start | bytes 307208 | tf_op jit(solution)/shard_map/ppermute | solution.py:289
  14.6 30.6 %all-to-all-start = ((bf16[16,6,16,256]{3,2,1,0:T(8,128)(2,1)}), bf16[16,6,16,256]{3,2,1,0:T(8,128)(2,1)S(1)}, u32[]{:S(2)}, u32[]{:S(2)}) async-start(bf16[16,6,16,256]{3,2,1,0:T(8,128)(2,1)} %get-tuple-element.15), calls=%async_computation | async-start | bytes 1572864 | tf_op jit(solution)/shard_map/all_to_all | solution.py:278
  24.8 69.5 %all-gather.2.cloned.1.call-start = ((), (), s32[]{:S(2)}) async-start(), calls=%async_computation.3 | async-start | bytes 3481600 | tf_op jit(solution)/shard_map/all_gather | solution.py:291
  27.4 1.2 copy-start.8
  31.8 2.7 %copy-start.3 = (bf16[1792,1792]{1,0:T(8,128)(2,1)}, bf16[1792,1792]{1,0:T(8,128)(2,1)S(1)}, u32[]{:S(2)}) copy-start(bf16[1792,1792]{1,0:T(8,128)(2,1)S(1)} %get-tuple-element.13.chosen) | copy-start | bytes 19267588
  46.4 9.6 %collective-permute-start.2 = (bf16[64,3200]{1,0:T(8,128)(2,1)S(1)}, bf16[64,3200]{1,0:T(8,128)(2,1)S(1)}, u32[]{:S(2)}, u32[]{:S(2)}) collective-permute-start(bf16[64,3200]{1,0:T(8,128)(2,1)S(1)} %shard_map.125.rest_0_), channel_id=1, source_target_pairs={{0,16},{16,0},{32,48},{48,32},{64,80},{80,64},{96,112},{112,96},{1... | collective-permute-start | bytes 1228808 | tf_op jit(solution)/shard_map/ppermute | solution.py:310
  52.9 8.0 %collective-permute-start.1 = (bf16[64,3200]{1,0:T(8,128)(2,1)S(1)}, bf16[64,3200]{1,0:T(8,128)(2,1)S(1)}, u32[]{:S(2)}, u32[]{:S(2)}) collective-permute-start(bf16[64,3200]{1,0:T(8,128)(2,1)S(1)} %shard_map.126), channel_id=1, source_target_pairs={{0,16},{16,0},{32,48},{48,32},{64,80},{80,64},{96,112},{112,96},{1... | collective-permute-start | bytes 1228808 | tf_op jit(solution)/shard_map/ppermute | solution.py:310
  56.0 13.9 %collective-permute-start.3 = (bf16[64,3200]{1,0:T(8,128)(2,1)S(1)}, bf16[64,3200]{1,0:T(8,128)(2,1)S(1)}, u32[]{:S(2)}, u32[]{:S(2)}) collective-permute-start(bf16[64,3200]{1,0:T(8,128)(2,1)S(1)} %add_convert_fusion.1), channel_id=1, source_target_pairs={{0,32},{16,48},{32,0},{48,16},{64,96},{80,112},{96,64},{112,80},{1... | collective-permute-start | bytes 1228808 | tf_op jit(solution)/shard_map/ppermute | solution.py:314
  90.8 19.1 %all-to-all-start.2 = ((bf16[8,8,3200]{2,1,0:T(8,128)(2,1)}), bf16[8,8,3200]{2,1,0:T(8,128)(2,1)S(1)}, u32[]{:S(2)}, u32[]{:S(2)}) async-start(bf16[8,8,3200]{2,1,0:T(8,128)(2,1)} %broadcast_in_dim.10), calls=%async_computation.2 | async-start | bytes 819200 | tf_op jit(solution)/shard_map/all_to_all | solution.py:263
  94.3 2.8 %copy-start.4 = (bf16[1792,1792]{1,0:T(8,128)(2,1)S(1)}, bf16[1792,1792]{1,0:T(8,128)(2,1)}, u32[]{:S(2)}) copy-start(bf16[1792,1792]{1,0:T(8,128)(2,1)} %copy-done.3) | copy-start | bytes 19267588
  97.1 1.9 %copy-start.5 = (bf16[256,6400]{1,0:T(8,128)(2,1)S(1)}, bf16[256,6400]{1,0:T(8,128)(2,1)}, u32[]{:S(2)}) copy-start(bf16[256,6400]{1,0:T(8,128)(2,1)} %all-gather.2.cloned.1.call-done) | copy-start | bytes 9830404
  99.1 34.1 %slice-start = ((s8[6422528]{0:T(1024)(128)(4,1)}), s8[2228224]{0:T(1024)(128)(4,1)S(1)}, s32[]{:S(2)}) async-start(s8[6422528]{0:T(1024)(128)(4,1)} %bitcast.8), calls=%async_computation.4 | async-start | bytes 4456448
  106.4 2.7 %copy-start = (f32[2,256,3200]{2,1,0:T(8,128)}, f32[2,256,3200]{2,1,0:T(8,128)S(1)}, u32[]{:S(2)}) copy-start(f32[2,256,3200]{2,1,0:T(8,128)S(1)} %get-tuple-element.19.rates) | copy-start | bytes 19660804
  109.2 0.7 copy-start.6
  109.9 8.4 %collective-permute-start.5 = (bf16[64,3200]{1,0:T(8,128)(2,1)S(1)}, bf16[64,3200]{1,0:T(8,128)(2,1)S(1)}, u32[]{:S(2)}, u32[]{:S(2)}) collective-permute-start(bf16[64,3200]{1,0:T(8,128)(2,1)S(1)} %shard_map.128.first), channel_id=1, source_target_pairs={{0,16},{16,0},{32,48},{48,32},{64,80},{80,64},{96,112},{112,96},{1... | collective-permute-start | bytes 1228808 | tf_op jit(solution)/shard_map/ppermute | solution.py:342
  114.6 14.5 %collective-permute-start.4 = (bf16[64,3200]{1,0:T(8,128)(2,1)S(1)}, bf16[64,3200]{1,0:T(8,128)(2,1)S(1)}, u32[]{:S(2)}, u32[]{:S(2)}) collective-permute-start(bf16[64,3200]{1,0:T(8,128)(2,1)S(1)} %shard_map.128.first), channel_id=1, source_target_pairs={{0,32},{16,48},{32,0},{48,16},{64,96},{80,112},{96,64},{112,80},{1... | collective-permute-start | bytes 1228808 | tf_op jit(solution)/shard_map/ppermute | solution.py:341
  118.3 2.9 %copy-start.1 = (f32[2,256,3200]{2,1,0:T(8,128)S(1)}, f32[2,256,3200]{2,1,0:T(8,128)}, u32[]{:S(2)}) copy-start(f32[2,256,3200]{2,1,0:T(8,128)} %copy-done) | copy-start | bytes 19660804
  121.2 1.0 copy-start.7
  122.2 10.9 %copy-start.2 = (f32[2,256,3200]{2,1,0:T(8,128)S(1)}, f32[2,256,3200]{2,1,0:T(8,128)}, u32[]{:S(2)}) copy-start(f32[2,256,3200]{2,1,0:T(8,128)} %copy-done) | copy-start | bytes 19660804
  122.2 10.9 %slice-start.1 = ((s8[6422528]{0:T(1024)(128)(4,1)}), s8[4194304]{0:T(1024)(128)(4,1)S(1)}, s32[]{:S(2)}) async-start(s8[6422528]{0:T(1024)(128)(4,1)} %bitcast.8), calls=%async_computation.5 | async-start | bytes 8388608
  129.1 4.1 %collective-permute-start.6 = (bf16[64,3200]{1,0:T(8,128)(2,1)S(1)}, bf16[64,3200]{1,0:T(8,128)(2,1)S(1)}, u32[]{:S(2)}, u32[]{:S(2)}) collective-permute-start(bf16[64,3200]{1,0:T(8,128)(2,1)S(1)} %shard_map.130.first), channel_id=1, source_target_pairs={{0,16},{16,0},{32,48},{48,32},{64,80},{80,64},{96,112},{112,96},{1... | collective-permute-start | bytes 1228808 | tf_op jit(solution)/shard_map/ppermute | solution.py:355
Sparse Core Ops, SparseCore 0:
  28.3 45.0 all-gather.1

commit v5 on v4

--- a/solution.py
+++ b/solution.py
@@ -13,7 +13,7 @@
 LIMIT = pltpu.CompilerParams(vmem_limit_bytes=20 * 1024 * 1024)
 FULL = pltpu.CompilerParams(vmem_limit_bytes=60 * 1024 * 1024)
 TILE = 256
-WEIGHT = 60
+WEIGHT = 110
 STEP = 128
 
 
@@ -81,8 +81,9 @@
         copies[place, count:] = near[7][...]
 
 
-def sort_kernel(position, down, ranked, chosen):
-    count = down.shape[0]
+def sort_kernel(position, down, down_far, ranked, chosen, flag):
+    flag[...] = jnp.zeros_like(flag)
+    count, features = down.shape
 
     @pl.loop(0, count // TILE)
     def _(block):
@@ -90,9 +91,10 @@
         rows = lax.broadcasted_iota(jnp.int32, (TILE, count), 0) + block * TILE
         ones = (rows == position[...]).astype(jnp.float32).astype(jnp.bfloat16)
         chosen[here, :] = ones
-        ranked[here, :] = jnp.dot(ones, down[...], preferred_element_type=jnp.float32).astype(
-            jnp.bfloat16
-        )
+        for low, source in ((0, down), (features, down_far)):
+            ranked[here, low : low + features] = jnp.dot(
+                ones, source[...], preferred_element_type=jnp.float32
+            ).astype(jnp.bfloat16)
 
 
 def pick(pair, place):
@@ -106,16 +108,26 @@
     return pick((mine[:, 0], mine[:, 1]), core).reshape(places * rows // 4, features)
 
 
-def partial_kernel(widths, where, tokens, ranked, *rest):
+def split_kernel(where, tokens, flag, sent, kept):
+    rows = sent.shape[1] // 2
+    for index in range(3):
+        block = tokens[:, 3 + index]
+        for half in range(2):
+            for out, core in ((sent, 1 - where[0]), (kept, where[0])):
+                out[index, half * rows : (half + 1) * rows, :] = group_of(
+                    block, core, (where[1] + half) % 2
+                ).astype(jnp.bfloat16)
+
+
+def partial_kernel(widths, half, kept, other, ranked, *rest):
     out = rest[-1]
+    rows = out.shape[0]
     offset = 0
     for index, width in enumerate(widths):
-        left = group_of(tokens[:, 3 + index], where[0], where[1])
+        here = slice(half * rows, (half + 1) * rows)
+        left = jnp.concatenate([kept[index, here, :], other[index, here, :]], axis=1)
         out[:, offset : offset + width] = lax.dot_general(
-            left.astype(jnp.bfloat16),
-            ranked[:width],
-            (((1,), (1,)), ((), ())),
-            preferred_element_type=jnp.float32,
+            left, ranked[:width], (((1,), (1,)), ((), ())), preferred_element_type=jnp.float32
         ).astype(out.dtype)
         offset += width
 
@@ -132,12 +144,8 @@
         )
 
 
-def hidden_kernel(
-    widths, where, chosen, pairs, tokens, down_grad, rates, turned, flag, hidden, totals, turned_out
-):
+def rates_kernel(widths, where, pairs, hidden, rates, flag):
     flag[...] = jnp.zeros_like(flag)
-    count = chosen.shape[0]
-    features = tokens.shape[3]
     rows = pairs.shape[0] * 8
     offset = 0
     for index, width in enumerate(widths):
@@ -167,6 +175,11 @@
 
         offset += width
 
+
+def down_kernel(widths, where, chosen, hidden, tokens, down_grad, turned, flag, totals, turned_out):
+    flag[...] = jnp.zeros_like(flag)
+    count = chosen.shape[0]
+    rows = turned.shape[2] // 6
     for index in range(6):
         block = tokens[:, index]
         for half in range(2):
@@ -278,12 +291,15 @@
     tokens = lax.all_to_all(copies, "tensor", 0, 0, tiled=True)
 
     position = (ranks // n_tensor)[None, :]
-    ranked, chosen = call(
+    down_far = lax.ppermute(down_weight, "dp", core_swap)
+    flag_shape = shaped((8, 128), jnp.float32)
+    ranked, chosen, flag = call(
         sort_kernel,
-        (shaped(down_weight.shape), shaped((count, count))),
+        (shaped((count, 2 * features)), shaped((count, count)), flag_shape),
         position,
         down_weight,
-        flops=2 * count * count * features,
+        down_far,
+        flops=4 * count * count * features,
     )
 
     there = lax.ppermute(local, "dp", x_swap)
@@ -293,45 +309,48 @@
 
     rows = tokens.shape[0] * tokens.shape[2] // 4
 
-    def partial(core, half, dtype, *behind):
+    where = jnp.stack([core, half])
+    sent, kept = call(
+        split_kernel, (shaped((3, 2 * rows, features)),) * 2, where, tokens, flag, scalars=1
+    )
+    other = lax.ppermute(sent, "dp", core_swap)
+
+    def partial(half, dtype, *behind):
         return call(
-            functools.partial(partial_kernel, widths),
+            functools.partial(partial_kernel, widths, half),
             shaped((rows, total), dtype),
-            jnp.stack([core, half]),
-            tokens,
+            kept,
+            other,
             ranked,
             *behind,
-            scalars=1,
-            flops=2 * WEIGHT * rows * total * features,
+            flops=4 * WEIGHT * rows * total * features,
         )
 
-    def core_sum(half, *behind):
-        sent = partial(1 - core, half, jnp.bfloat16, *behind)
-        other = lax.ppermute(sent, "dp", core_swap)
-        return partial(core, half, jnp.float32) + other.astype(jnp.float32), sent
-
-    across, behind = core_sum(1 - half)
-    far = lax.ppermute(across.astype(jnp.bfloat16), "dp", x_swap)
-    summed = (core_sum(half, behind)[0] + far.astype(jnp.float32)).astype(jnp.bfloat16)
+    across = partial(1, jnp.bfloat16)
+    far = lax.ppermute(across, "dp", x_swap)
+    summed = (partial(0, jnp.float32, across) + far.astype(jnp.float32)).astype(jnp.bfloat16)
     pieces = over_rows(summed.reshape(n_rows, -1, total))
+    hidden, rates, flag = call(
+        functools.partial(rates_kernel, widths),
+        (shaped((12 * rows, count)), shaped((2, 4 * rows, total), jnp.float32), flag_shape),
+        where,
+        pairs,
+        scalars=1,
+        flops=2 * features * count * count,
+    )
+    pieces = after(pieces, flag)
     reduced = jnp.sum(pieces.astype(jnp.float32), axis=0).astype(jnp.bfloat16)
     near = over_rows(jnp.broadcast_to(reduced[None], (n_rows,) + reduced.shape)).reshape(rows, total)
 
-    down_grad, rates, turned, flag = call(
-        functools.partial(hidden_kernel, widths),
-        (
-            shaped((count, features)),
-            shaped((2, 4 * rows, total), jnp.float32),
-            shaped((2, features, 6 * rows)),
-            shaped((8, 128), jnp.float32),
-        ),
-        jnp.stack([core, half]),
+    down_grad, turned, flag = call(
+        functools.partial(down_kernel, widths),
+        (shaped((count, features)), shaped((2, features, 6 * rows)), flag_shape),
+        where,
         chosen,
-        pairs,
+        hidden,
         tokens,
         scalars=1,
         scratch=(
-            pltpu.VMEM((12 * rows, count), jnp.bfloat16),
             pltpu.VMEM((features, count), jnp.bfloat16),
             pltpu.VMEM((features, 12 * rows), jnp.bfloat16),
         ),

time: 148 us -> 145 us (0.980)
  blocking collectives: 19.9 us -> 0 us
  local copies, waits for them, and re-layouts: 16.8 us -> 27.6 us
  starting transfers between devices: 41.1 us -> 51.9 us
  waiting for transfers between devices: 26.9 us -> 22 us
    all_to_all x1 -> x0, blocking collectives: 19.9 us -> none  [over_rows(): lax.all_to_all(blocks, 'dp', 0, 0, axis_index_groups=by_place, tiled=True)]
    unnamed x22 -> x38, local copies, waits for them, and re-layouts: 16 us -> 26.8 us
    all_to_all x1, waiting for transfers between devices: 10.7 us -> 1.04 us  [per_device(): tokens = lax.all_to_all(copies, 'tensor', 0, 0, tiled=True)]
    all_to_all x1 -> x2, starting transfers between devices: 3.46 us -> 10.3 us  [over_rows(): lax.all_to_all(blocks, 'dp', 0, 0, axis_index_groups=by_place, tiled=True)]
    all_gather x1, waiting for transfers between devices: 0.02 us -> 3.9 us  [per_device(): lax.all_gather(two, 'dp', axis=0, axis_index_groups=by_half, tiled=True)]
    all_to_all x1, starting transfers between devices: 10.2 us -> 11.9 us  [per_device(): tokens = lax.all_to_all(copies, 'tensor', 0, 0, tiled=True)]
    ppermute x3, starting transfers between devices: 10.9 us -> 12.5 us  [the longest x1 4.99 us: per_device(): other = lax.ppermute(sent, 'dp', core_swap)]
  transfers between devices with their start and end apart: 10 -> 11, of which waited for: 4 -> 7; matrix products, arithmetic and copies ran while one was open for 2% -> 2% of each run, Pallas kernels for 11% -> 11%
where the time goes in v5:
time: 145 us; the launch traced here: 144 us
  starting transfers between devices  51.9 us (36%)
  local copies, waits for them, and re-layouts  27.6 us (19%)
  Pallas kernels  25.4 us (18%)
  waiting for transfers between devices  22 us (15%)
  between operations  14.2 us (10%)
  other arithmetic  3.25 us (2%)
    unnamed x38, local copies, waits for them, and re-layouts  26.8 us
    pallas_call x8, Pallas kernels, call(): pl.pallas_call(kernel, out_shape=out_shape, in_specs=[SMEM] * scalars + [...  23.5 us
    all_to_all x1, starting transfers between devices, per_device(): tokens = lax.all_to_all(copies, 'tensor', 0, 0, tiled=True)  11.9 us
    all_to_all x2, starting transfers between devices, over_rows(): lax.all_to_all(blocks, 'dp', 0, 0, axis_index_groups=by_place, tiled=True)  10.3 us
    ppermute x1, waiting for transfers between devices, per_device(): far = lax.ppermute(across, 'dp', x_swap)  8.62 us
    ppermute x1, starting transfers between devices, per_device(): near_other = lax.ppermute(near, 'dp', core_swap)  5.59 us
    ppermute x1, starting transfers between devices, per_device(): other = lax.ppermute(sent, 'dp', core_swap)  4.99 us
    ppermute x1, waiting for transfers between devices, per_device(): beyond = lax.ppermute(near, 'dp', x_swap)  4.85 us
  transfers between devices with their start and end apart: 11, of which 7 were waited for; matrix products, arithmetic and copies ran while one was open for 2% of the time, Pallas kernels for 11%

profile of v5, /device:TPU:1, one launch (start us, length us, event | category | flops | bytes accessed | tf_op | source)
XLA Modules:
  0.0 144.4 jit_solution(6288293327318767124)
XLA Ops:
  7.2 1.9 %shard_map.122 = (bf16[16,6,16,256]{3,2,1,0:T(8,128)(2,1)}, bf16[8,6400]{1,0:T(8,128)(2,1)}) custom-call(bf16[8,448]{1,0:T(8,128)(2,1)} %refs_0_.1, bf16[8,448]{1,0:T(8,128)(2,1)} %refs_1_.1, bf16[8,896]{1,0:T(8,128)(2,1)} %refs_2_.1, bf16[8,896]{1,0:T(8,128)(2,1)} %refs_3_.1, bf16[8,1792]{1,0:T(8,128)(2,1)} %refs_4_.1, bf16[8,1792]{1,0:T(8,128)(2,1)} %refs_5_.1, ...), custom_call_target="tpu_custom_call" | custom-call | tf_op jit(solution)/shard_map/pallas_call | solution.py:279
  9.1 11.9 %all-to-all-start = ((bf16[16,6,16,256]{3,2,1,0:T(8,128)(2,1)}), bf16[16,6,16,256]{3,2,1,0:T(8,128)(2,1)S(1)}, u32[]{:S(2)}, u32[]{:S(2)}) async-start(bf16[16,6,16,256]{3,2,1,0:T(8,128)(2,1)} %get-tuple-element.21), calls=%async_computation | async-start | bytes 1572864 | tf_op jit(solution)/shard_map/all_to_all | solution.py:291
  21.1 4.4 %collective-permute-start.1 = (bf16[8,6400]{1,0:T(8,128)(2,1)}, bf16[8,6400]{1,0:T(8,128)(2,1)S(1)}, u32[]{:S(2)}, u32[]{:S(2)}) collective-permute-start(bf16[8,6400]{1,0:T(8,128)(2,1)} %get-tuple-element.19), channel_id=1, source_target_pairs={{0,32},{16,48},{32,0},{48,16},{64,96},{80,112},{96,64},{112,80},{1... | collective-permute-start | bytes 307208 | tf_op jit(solution)/shard_map/ppermute | solution.py:305
  25.4 3.1 %collective-permute-start = (bf16[1792,256]{1,0:T(8,128)(2,1)}, bf16[1792,256]{1,0:T(8,128)(2,1)S(1)}, u32[]{:S(2)}, u32[]{:S(2)}) collective-permute-start(bf16[1792,256]{1,0:T(8,128)(2,1)} %down.1), channel_id=1, source_target_pairs={{0,16},{16,0},{32,48},{48,32},{64,80},{80,64},{96,112},{112,96},{1... | collective-permute-start | bytes 2752520 | tf_op jit(solution)/shard_map/ppermute | solution.py:294
  28.6 0.7 add_select_fusion
  29.3 0.1 pad_add_fusion.where
  29.4 1.6 %pad_maximum_fusion = bf16[16,6400]{1,0:T(8,128)(2,1)} fusion(bf16[8,6400]{1,0:T(8,128)(2,1)S(1)} %collective-permute-done.1, bf16[8,6400]{1,0:T(8,128)(2,1)} %get-tuple-element.19), kind=kLoop, calls=%fused_computation.2 | loop fusion | flops 409600 | bytes 409600 | tf_op jit(solution)/shard_map/concatenate | solution.py:306
  31.0 1.2 copy-done.14
  32.2 4.6 %shard_map.121 = (bf16[1792,512]{1,0:T(8,128)(2,1)S(1)}, bf16[1792,1792]{1,0:T(8,128)(2,1)S(1)}, f32[8,128]{1,0:T(8,128)S(1)}) custom-call(s32[1,1792]{1,0:T(1,128)S(1)} %broadcast_in_dim.4.position, bf16[1792,256]{1,0:T(8,128)(2,1)S(1)} %copy-done.14, bf16[1792,256]{1,0:T(8,128)(2,1)S(1)} %collective-permute-done.down_far), custom_call_target="tpu_custom_call" | custom-call | flops 3288334336 | bytes 1048576 | tf_op jit(solution)/shard_map/pallas_call | solution.py:26
  36.8 2.7 %copy-done.2 = bf16[1792,1792]{1,0:T(8,128)(2,1)} copy-done((bf16[1792,1792]{1,0:T(8,128)(2,1)}, bf16[1792,1792]{1,0:T(8,128)(2,1)S(1)}, u32[]{:S(2)}) %copy-start.2) | copy-done | bytes 6422552
  39.5 1.3 copy-done.15
  40.8 1.0 all-to-all-done.tokens
  41.8 0.7 shard_map.125
  42.5 5.0 %collective-permute-start.2 = (bf16[3,128,256]{2,1,0:T(8,128)(2,1)S(1)}, bf16[3,128,256]{2,1,0:T(8,128)(2,1)S(1)}, u32[]{:S(2)}, u32[]{:S(2)}) collective-permute-start(bf16[3,128,256]{2,1,0:T(8,128)(2,1)S(1)} %get-tuple-element.25), channel_id=1, source_target_pairs={{0,16},{16,0},{32,48},{48,32},{64,80},{80,64},{96,112},{112,96},{1... | collective-permute-start | bytes 589832 | tf_op jit(solution)/shard_map/ppermute | solution.py:316
  47.5 1.0 collective-permute-done.2.other
  48.5 1.5 %copy-done.16 = bf16[1792,512]{1,0:T(8,128)(2,1)S(1)} copy-done((bf16[1792,512]{1,0:T(8,128)(2,1)S(1)}, bf16[1792,512]{1,0:T(8,128)(2,1)}, u32[]{:S(2)}) %copy-start.16) | copy-done | bytes 1835032
  50.0 1.1 shard_map.126.rest_0_
  51.1 4.4 %collective-permute-start.3 = (bf16[64,3200]{1,0:T(8,128)(2,1)S(1)}, bf16[64,3200]{1,0:T(8,128)(2,1)S(1)}, u32[]{:S(2)}, u32[]{:S(2)}) collective-permute-start(bf16[64,3200]{1,0:T(8,128)(2,1)S(1)} %shard_map.126.rest_0_), channel_id=1, source_target_pairs={{0,32},{16,48},{32,0},{48,16},{64,96},{80,112},{96,64},{112,80},{1... | collective-permute-start | bytes 1228808 | tf_op jit(solution)/shard_map/ppermute | solution.py:330
  55.5 1.1 shard_map.127
  56.6 8.6 %collective-permute-done.3 = bf16[64,3200]{1,0:T(8,128)(2,1)S(1)} collective-permute-done((bf16[64,3200]{1,0:T(8,128)(2,1)S(1)}, bf16[64,3200]{1,0:T(8,128)(2,1)S(1)}, u32[]{:S(2)}, u32[]{:S(2)}) %collective-permute-start.3) | collective-permute-done | bytes 409632 | tf_op jit(solution)/shard_map/ppermute | solution.py:330
  65.2 0.8 fusion
  66.0 6.9 %all-to-all-start.1 = ((bf16[8,8,3200]{2,1,0:T(8,128)(2,1)}), bf16[8,8,3200]{2,1,0:T(8,128)(2,1)S(1)}, u32[]{:S(2)}, u32[]{:S(2)}) async-start(bf16[8,8,3200]{2,1,0:T(8,128)(2,1)} %fusion), calls=%async_computation.1 | async-start | bytes 819200 | tf_op jit(solution)/shard_map/all_to_all | solution.py:276
  72.9 3.9 %all-gather.2.cloned.1.call-done = bf16[256,6400]{1,0:T(8,128)(2,1)} async-done(((bf16[16,6400]{1,0:T(8,128)(2,1)}), bf16[256,6400]{1,0:T(8,128)(2,1)}) %all-gather.2.cloned.1.call-update) | async-done | bytes 3276816 | tf_op jit(solution)/shard_map/all_gather | solution.py:307
  76.8 1.9 %copy-done.13 = bf16[256,6400]{1,0:T(8,128)(2,1)S(1)} copy-done((bf16[256,6400]{1,0:T(8,128)(2,1)S(1)}, bf16[256,6400]{1,0:T(8,128)(2,1)}, u32[]{:S(2)}) %copy-start.13) | copy-done | bytes 3276824
  78.7 2.3 %shard_map.123 = (bf16[768,1792]{1,0:T(8,128)(2,1)S(1)}, f32[2,256,3200]{2,1,0:T(8,128)S(1)}, f32[8,128]{1,0:T(8,128)S(1)}) custom-call(s32[2]{0:T(128)S(1)} %pad_add_fusion.where, bf16[8,2,16,6400]{3,2,1,0:T(8,128)(2,1)S(1)} %bitcast.9), custom_call_target="tpu_custom_call" | custom-call | flops 1644167168 | bytes 1048576 | tf_op jit(solution)/shard_map/pallas_call | solution.py:26
  81.1 2.8 %copy-done = f32[2,256,3200]{2,1,0:T(8,128)} copy-done((f32[2,256,3200]{2,1,0:T(8,128)}, f32[2,256,3200]{2,1,0:T(8,128)S(1)}, u32[]{:S(2)}) %copy-start) | copy-done | bytes 6553624
  83.8 1.5 %copy-done.5 = bf16[768,1792]{1,0:T(8,128)(2,1)} copy-done((bf16[768,1792]{1,0:T(8,128)(2,1)}, bf16[768,1792]{1,0:T(8,128)(2,1)S(1)}, u32[]{:S(2)}) %copy-start.5) | copy-done | bytes 2752536
  85.3 1.1 all-to-all-done.1.value_ref
  86.4 0.1 reduce_sum.12
  86.5 0.8 broadcast_in_dim.10
  87.3 3.5 %all-to-all-start.2 = ((bf16[8,8,3200]{2,1,0:T(8,128)(2,1)}), bf16[8,8,3200]{2,1,0:T(8,128)(2,1)S(1)}, u32[]{:S(2)}, u32[]{:S(2)}) async-start(bf16[8,8,3200]{2,1,0:T(8,128)(2,1)} %broadcast_in_dim.10), calls=%async_computation.2 | async-start | bytes 819200 | tf_op jit(solution)/shard_map/all_to_all | solution.py:276
  90.8 2.8 %copy-done.3 = bf16[1792,1792]{1,0:T(8,128)(2,1)S(1)} copy-done((bf16[1792,1792]{1,0:T(8,128)(2,1)S(1)}, bf16[1792,1792]{1,0:T(8,128)(2,1)}, u32[]{:S(2)}) %copy-start.3) | copy-done | bytes 6422552
  93.6 1.8 %copy-done.6 = bf16[768,1792]{1,0:T(8,128)(2,1)S(1)} copy-done((bf16[768,1792]{1,0:T(8,128)(2,1)S(1)}, bf16[768,1792]{1,0:T(8,128)(2,1)}, u32[]{:S(2)}) %copy-start.6) | copy-done | bytes 2752536
  95.4 0.6 copy-done.12
  96.0 5.6 %shard_map.124 = (bf16[1792,256]{1,0:T(8,128)(2,1)}, bf16[2,256,384]{2,1,0:T(8,128)(2,1)S(1)}, f32[8,128]{1,0:T(8,128)S(1)}) custom-call(s32[2]{0:T(128)S(1)} %copy-done.12, bf16[1792,1792]{1,0:T(8,128)(2,1)S(1)} %copy-done.3, bf16[768,1792]{1,0:T(8,128)(2,1)S(1)} %copy-done.6, bf16[16,6,16,256]{3,2,1,0:T(8,128)(2,1)S(1)} %all-to-all-done.tokens), custom_call_target="tpu_custom_call" | custom-call | flops 1702887424 | bytes 1048576 | tf_op jit(solution)/shard_map/pallas_call | solution.py:26
  101.6 0.7 copy-done.7
  102.3 0.6 copy-done.9
  103.0 0.7 copy-done.10
  103.6 5.6 %collective-permute-start.5 = (bf16[64,3200]{1,0:T(8,128)(2,1)S(1)}, bf16[64,3200]{1,0:T(8,128)(2,1)S(1)}, u32[]{:S(2)}, u32[]{:S(2)}) collective-permute-start(bf16[64,3200]{1,0:T(8,128)(2,1)S(1)} %shard_map.129.first), channel_id=1, source_target_pairs={{0,16},{16,0},{32,48},{48,32},{64,80},{80,64},{96,112},{112,96},{1... | collective-permute-start | bytes 1228808 | tf_op jit(solution)/shard_map/ppermute | solution.py:361
  109.2 4.5 %collective-permute-start.4 = (bf16[64,3200]{1,0:T(8,128)(2,1)S(1)}, bf16[64,3200]{1,0:T(8,128)(2,1)S(1)}, u32[]{:S(2)}, u32[]{:S(2)}) collective-permute-start(bf16[64,3200]{1,0:T(8,128)(2,1)S(1)} %shard_map.129.first), channel_id=1, source_target_pairs={{0,32},{16,48},{32,0},{48,16},{64,96},{80,112},{96,64},{112,80},{1... | collective-permute-start | bytes 1228808 | tf_op jit(solution)/shard_map/ppermute | solution.py:360
  113.8 2.9 %copy-done.1 = f32[2,256,3200]{2,1,0:T(8,128)S(1)} copy-done((f32[2,256,3200]{2,1,0:T(8,128)S(1)}, f32[2,256,3200]{2,1,0:T(8,128)}, u32[]{:S(2)}) %copy-start.1) | copy-done | bytes 6553624
  116.7 1.0 copy-done.8
  117.6 1.2 shard_map.130.other_ref.sums
  118.9 4.8 %collective-permute-done.4.value_ref = bf16[64,3200]{1,0:T(8,128)(2,1)S(1)} collective-permute-done((bf16[64,3200]{1,0:T(8,128)(2,1)S(1)}, bf16[64,3200]{1,0:T(8,128)(2,1)S(1)}, u32[]{:S(2)}, u32[]{:S(2)}) %collective-permute-start.4) | collective-permute-done | bytes 409632 | tf_op jit(solution)/shard_map/ppermute | solution.py:360
  123.7 2.7 %collective-permute-start.6 = (bf16[64,3200]{1,0:T(8,128)(2,1)S(1)}, bf16[64,3200]{1,0:T(8,128)(2,1)S(1)}, u32[]{:S(2)}, u32[]{:S(2)}) collective-permute-start(bf16[64,3200]{1,0:T(8,128)(2,1)S(1)} %shard_map.131.first), channel_id=1, source_target_pairs={{0,16},{16,0},{32,48},{48,32},{64,80},{80,64},{96,112},{112,96},{1... | collective-permute-start | bytes 1228808 | tf_op jit(solution)/shard_map/ppermute | solution.py:374
  126.4 1.4 collective-permute-done.6.second
  127.8 2.8 %copy-done.4 = bf16[1792,1792]{1,0:T(8,128)(2,1)S(1)} copy-done((bf16[1792,1792]{1,0:T(8,128)(2,1)S(1)}, bf16[1792,1792]{1,0:T(8,128)(2,1)}, u32[]{:S(2)}) %copy-start.4) | copy-done | bytes 6422552
  130.6 6.9 %shard_map.132 = (bf16[256,1792]{1,0:T(8,128)(2,1)}, bf16[256,1792]{1,0:T(8,128)(2,1)}) custom-call(bf16[1792,1792]{1,0:T(8,128)(2,1)S(1)} %copy-done.4, bf16[64,3200]{1,0:T(8,128)(2,1)S(1)} %shard_map.131.first, bf16[64,3200]{1,0:T(8,128)(2,1)S(1)} %collective-permute-done.6.second, f32[2,256,3200]{2,1,0:T(8,128)S(1)} %bitcast.7, ...), custom_call_target="tpu_custom_call" | custom-call | flops 3405774848 | bytes 1048576 | tf_op jit(solution)/shard_map/pallas_call | solution.py:26
  (33 shorter events, 0.2 us)
Async XLA Ops:
  9.1 32.7 %all-to-all-start = ((bf16[16,6,16,256]{3,2,1,0:T(8,128)(2,1)}), bf16[16,6,16,256]{3,2,1,0:T(8,128)(2,1)S(1)}, u32[]{:S(2)}, u32[]{:S(2)}) async-start(bf16[16,6,16,256]{3,2,1,0:T(8,128)(2,1)} %get-tuple-element.21), calls=%async_computation | async-start | bytes 1572864 | tf_op jit(solution)/shard_map/all_to_all | solution.py:291
  21.0 55.8 %all-gather.2.cloned.1.call-start = ((), (), s32[]{:S(2)}) async-start(), calls=%async_computation.3 | async-start | bytes 3481600 | tf_op jit(solution)/shard_map/all_gather | solution.py:307
  21.1 8.3 %collective-permute-start.1 = (bf16[8,6400]{1,0:T(8,128)(2,1)}, bf16[8,6400]{1,0:T(8,128)(2,1)S(1)}, u32[]{:S(2)}, u32[]{:S(2)}) collective-permute-start(bf16[8,6400]{1,0:T(8,128)(2,1)} %get-tuple-element.19), channel_id=1, source_target_pairs={{0,32},{16,48},{32,0},{48,16},{64,96},{80,112},{96,64},{112,80},{1... | collective-permute-start | bytes 307208 | tf_op jit(solution)/shard_map/ppermute | solution.py:305
  25.4 5.6 %collective-permute-start = (bf16[1792,256]{1,0:T(8,128)(2,1)}, bf16[1792,256]{1,0:T(8,128)(2,1)S(1)}, u32[]{:S(2)}, u32[]{:S(2)}) collective-permute-start(bf16[1792,256]{1,0:T(8,128)(2,1)} %down.1), channel_id=1, source_target_pairs={{0,16},{16,0},{32,48},{48,32},{64,80},{80,64},{96,112},{112,96},{1... | collective-permute-start | bytes 2752520 | tf_op jit(solution)/shard_map/ppermute | solution.py:294
  29.4 47.4 %copy-start.11 = (s32[2]{0:T(128)}, s32[2]{0:T(128)S(1)}, u32[]{:S(2)}) copy-start(s32[2]{0:T(128)S(1)} %pad_add_fusion.where) | copy-start | bytes 28
  31.0 1.2 copy-start.14
  36.8 2.7 %copy-start.2 = (bf16[1792,1792]{1,0:T(8,128)(2,1)}, bf16[1792,1792]{1,0:T(8,128)(2,1)S(1)}, u32[]{:S(2)}) copy-start(bf16[1792,1792]{1,0:T(8,128)(2,1)S(1)} %get-tuple-element.18.chosen) | copy-start | bytes 19267588
  39.5 1.3 copy-start.15
  42.5 6.0 %collective-permute-start.2 = (bf16[3,128,256]{2,1,0:T(8,128)(2,1)S(1)}, bf16[3,128,256]{2,1,0:T(8,128)(2,1)S(1)}, u32[]{:S(2)}, u32[]{:S(2)}) collective-permute-start(bf16[3,128,256]{2,1,0:T(8,128)(2,1)S(1)} %get-tuple-element.25), channel_id=1, source_target_pairs={{0,16},{16,0},{32,48},{48,32},{64,80},{80,64},{96,112},{112,96},{1... | collective-permute-start | bytes 589832 | tf_op jit(solution)/shard_map/ppermute | solution.py:316
  48.5 1.5 %copy-start.16 = (bf16[1792,512]{1,0:T(8,128)(2,1)S(1)}, bf16[1792,512]{1,0:T(8,128)(2,1)}, u32[]{:S(2)}) copy-start(bf16[1792,512]{1,0:T(8,128)(2,1)} %copy-done.15) | copy-start | bytes 5505028
  51.1 14.1 %collective-permute-start.3 = (bf16[64,3200]{1,0:T(8,128)(2,1)S(1)}, bf16[64,3200]{1,0:T(8,128)(2,1)S(1)}, u32[]{:S(2)}, u32[]{:S(2)}) collective-permute-start(bf16[64,3200]{1,0:T(8,128)(2,1)S(1)} %shard_map.126.rest_0_), channel_id=1, source_target_pairs={{0,32},{16,48},{32,0},{48,16},{64,96},{80,112},{96,64},{112,80},{1... | collective-permute-start | bytes 1228808 | tf_op jit(solution)/shard_map/ppermute | solution.py:330
  66.0 20.4 %all-to-all-start.1 = ((bf16[8,8,3200]{2,1,0:T(8,128)(2,1)}), bf16[8,8,3200]{2,1,0:T(8,128)(2,1)S(1)}, u32[]{:S(2)}, u32[]{:S(2)}) async-start(bf16[8,8,3200]{2,1,0:T(8,128)(2,1)} %fusion), calls=%async_computation.1 | async-start | bytes 819200 | tf_op jit(solution)/shard_map/all_to_all | solution.py:276
  76.8 1.9 %copy-start.13 = (bf16[256,6400]{1,0:T(8,128)(2,1)S(1)}, bf16[256,6400]{1,0:T(8,128)(2,1)}, u32[]{:S(2)}) copy-start(bf16[256,6400]{1,0:T(8,128)(2,1)} %all-gather.2.cloned.1.call-done) | copy-start | bytes 9830404
  81.0 2.8 %copy-start = (f32[2,256,3200]{2,1,0:T(8,128)}, f32[2,256,3200]{2,1,0:T(8,128)S(1)}, u32[]{:S(2)}) copy-start(f32[2,256,3200]{2,1,0:T(8,128)S(1)} %get-tuple-element.29.rates) | copy-start | bytes 19660804
  83.8 1.5 %copy-start.5 = (bf16[768,1792]{1,0:T(8,128)(2,1)}, bf16[768,1792]{1,0:T(8,128)(2,1)S(1)}, u32[]{:S(2)}) copy-start(bf16[768,1792]{1,0:T(8,128)(2,1)S(1)} %get-tuple-element.20.hidden) | copy-start | bytes 8257540
  87.3 15.7 %all-to-all-start.2 = ((bf16[8,8,3200]{2,1,0:T(8,128)(2,1)}), bf16[8,8,3200]{2,1,0:T(8,128)(2,1)S(1)}, u32[]{:S(2)}, u32[]{:S(2)}) async-start(bf16[8,8,3200]{2,1,0:T(8,128)(2,1)} %broadcast_in_dim.10), calls=%async_computation.2 | async-start | bytes 819200 | tf_op jit(solution)/shard_map/all_to_all | solution.py:276
  90.7 2.8 %copy-start.3 = (bf16[1792,1792]{1,0:T(8,128)(2,1)S(1)}, bf16[1792,1792]{1,0:T(8,128)(2,1)}, u32[]{:S(2)}) copy-start(bf16[1792,1792]{1,0:T(8,128)(2,1)} %copy-done.2) | copy-start | bytes 19267588
  93.6 1.8 %copy-start.6 = (bf16[768,1792]{1,0:T(8,128)(2,1)S(1)}, bf16[768,1792]{1,0:T(8,128)(2,1)}, u32[]{:S(2)}) copy-start(bf16[768,1792]{1,0:T(8,128)(2,1)} %copy-done.5) | copy-start | bytes 8257540
  95.3 0.6 copy-start.12
  96.0 31.8 %slice-start = ((s8[6553600]{0:T(1024)(128)(4,1)}), s8[2359296]{0:T(1024)(128)(4,1)S(1)}, s32[]{:S(2)}) async-start(s8[6553600]{0:T(1024)(128)(4,1)} %bitcast.6), calls=%async_computation.4 | async-start | bytes 4718592
  101.6 0.7 copy-start.7
  102.3 0.6 copy-start.9
  103.0 0.7 copy-start.10
  103.6 10.1 %collective-permute-start.5 = (bf16[64,3200]{1,0:T(8,128)(2,1)S(1)}, bf16[64,3200]{1,0:T(8,128)(2,1)S(1)}, u32[]{:S(2)}, u32[]{:S(2)}) collective-permute-start(bf16[64,3200]{1,0:T(8,128)(2,1)S(1)} %shard_map.129.first), channel_id=1, source_target_pairs={{0,16},{16,0},{32,48},{48,32},{64,80},{80,64},{96,112},{112,96},{1... | collective-permute-start | bytes 1228808 | tf_op jit(solution)/shard_map/ppermute | solution.py:361
  109.2 14.5 %collective-permute-start.4 = (bf16[64,3200]{1,0:T(8,128)(2,1)S(1)}, bf16[64,3200]{1,0:T(8,128)(2,1)S(1)}, u32[]{:S(2)}, u32[]{:S(2)}) collective-permute-start(bf16[64,3200]{1,0:T(8,128)(2,1)S(1)} %shard_map.129.first), channel_id=1, source_target_pairs={{0,32},{16,48},{32,0},{48,16},{64,96},{80,112},{96,64},{112,80},{1... | collective-permute-start | bytes 1228808 | tf_op jit(solution)/shard_map/ppermute | solution.py:360
  113.8 2.9 %copy-start.1 = (f32[2,256,3200]{2,1,0:T(8,128)S(1)}, f32[2,256,3200]{2,1,0:T(8,128)}, u32[]{:S(2)}) copy-start(f32[2,256,3200]{2,1,0:T(8,128)} %copy-done) | copy-start | bytes 19660804
  116.7 1.0 copy-start.8
  117.6 10.1 %slice-start.1 = ((s8[6553600]{0:T(1024)(128)(4,1)}), s8[4194304]{0:T(1024)(128)(4,1)S(1)}, s32[]{:S(2)}) async-start(s8[6553600]{0:T(1024)(128)(4,1)} %bitcast.6), calls=%async_computation.5 | async-start | bytes 8388608
  123.7 4.1 %collective-permute-start.6 = (bf16[64,3200]{1,0:T(8,128)(2,1)S(1)}, bf16[64,3200]{1,0:T(8,128)(2,1)S(1)}, u32[]{:S(2)}, u32[]{:S(2)}) collective-permute-start(bf16[64,3200]{1,0:T(8,128)(2,1)S(1)} %shard_map.131.first), channel_id=1, source_target_pairs={{0,16},{16,0},{32,48},{48,32},{64,80},{80,64},{96,112},{112,96},{1... | collective-permute-start | bytes 1228808 | tf_op jit(solution)/shard_map/ppermute | solution.py:374
  127.8 2.8 %copy-start.4 = (bf16[1792,1792]{1,0:T(8,128)(2,1)S(1)}, bf16[1792,1792]{1,0:T(8,128)(2,1)}, u32[]{:S(2)}) copy-start(bf16[1792,1792]{1,0:T(8,128)(2,1)} %copy-done.2) | copy-start | bytes 19267588
Sparse Core Ops, SparseCore 0:
  31.1 45.6 all-gather.1

commit v6 on v5

v6 whole, which is shorter than its diff:
```python
import functools

import jax
import jax.numpy as jnp
from jax import lax
from jax.experimental import pallas as pl
from jax.experimental.pallas import tpu as pltpu
from jax.sharding import PartitionSpec as P

VMEM = pl.BlockSpec(memory_space=pltpu.VMEM)
ANY = pl.BlockSpec(memory_space=pl.ANY)
SMEM = pl.BlockSpec(memory_space=pltpu.SMEM)
LIMIT = pltpu.CompilerParams(vmem_limit_bytes=20 * 1024 * 1024)
FULL = pltpu.CompilerParams(vmem_limit_bytes=60 * 1024 * 1024)
TILE = 256
WEIGHT = 85
REDUCE = 58
STEP = 128


def padded(width):
    return -(-width // 128) * 128


def call(kernel, out_shape, *args, scratch=(), scalars=0, flops=0):
    many = isinstance(out_shape, tuple)
    return pl.pallas_call(
        kernel,
        out_shape=out_shape,
        in_specs=[SMEM] * scalars + [VMEM] * (len(args) - scalars),
        out_specs=(VMEM,) * len(out_shape) if many else VMEM,
        scratch_shapes=list(scratch),
        compiler_params=LIMIT,
        cost_estimate=pl.CostEstimate(flops=flops, bytes_accessed=2**20, transcendentals=0),
    )(*args)


def shaped(shape, dtype=jnp.bfloat16):
    return jax.ShapeDtypeStruct(shape, dtype)


def after(value, other):
    def nothing(value_ref, other_ref, out_ref):
        pass

    return pl.pallas_call(
        nothing,
        out_shape=shaped(value.shape, value.dtype),
        in_specs=[VMEM, ANY],
        out_specs=VMEM,
        input_output_aliases={0: 0},
        compiler_params=LIMIT,
    )(value, other)


def start_kernel(*refs):
    far, copies, packed = refs[:8], refs[8], refs[9]
    near, sems = refs[10:18], refs[18]
    moves = [
        pltpu.make_async_copy(source, target, sems.at[index])
        for index, (source, target) in enumerate(zip(far, near))
    ]
    for move in moves:
        move.start()
    for move in moves[:6]:
        move.wait()
    offset = 0
    for array in near[:6]:
        width = array.shape[1]
        wide = padded(width)
        if wide != width:
            packed[:, offset : offset + wide] = jnp.zeros((packed.shape[0], wide), packed.dtype)
        packed[:, offset : offset + width] = array[...]
        offset += wide
    for move in moves[6:]:
        move.wait()
    count = near[6].shape[0]

    @pl.loop(0, copies.shape[0])
    def _(place):
        copies[place, :count] = near[6][...]
        copies[place, count:] = near[7][...]


def ones_where(rows, columns):
    return (rows == columns).astype(jnp.float32).astype(jnp.bfloat16)


def sort_kernel(position, down, ranked, flag):
    flag[...] = jnp.zeros_like(flag)
    count = down.shape[0]

    @pl.loop(0, count // TILE)
    def _(block):
        here = pl.ds(pl.multiple_of(block * TILE, TILE), TILE)
        rows = lax.broadcasted_iota(jnp.int32, (TILE, count), 0) + block * TILE
        ranked[here, :] = jnp.dot(
            ones_where(rows, position[...]), down[...], preferred_element_type=jnp.float32
        ).astype(jnp.bfloat16)


def own_place():
    place = lax.axis_index("dp")
    return place % 2, (place // 2) % 2


def pick(pair, place):
    return jnp.where(place == 0, pair[0], pair[1])


def group_of(block, core, half):
    places, rows, features = block.shape
    apart = block.astype(jnp.float32).reshape(places // 2, 2, 2, rows // 2, features)
    mine = pick((apart[:, 0], apart[:, 1]), half)
    return pick((mine[:, 0], mine[:, 1]), core).reshape(places * rows // 4, features)


def split_kernel(tokens, flag, sent, kept):
    own_core, own_half = own_place()
    rows = sent.shape[1] // 2
    for index in range(3):
        block = tokens[:, 3 + index]
        for half in range(2):
            for out, core in ((sent, 1 - own_core), (kept, own_core)):
                out[index, half * rows : (half + 1) * rows, :] = group_of(
                    block, core, (own_half + half) % 2
                ).astype(jnp.bfloat16)


def partial_kernel(widths, half, kept, other, ranked, ranked_far, *rest):
    out = rest[-1]
    rows = out.shape[0]
    offset = 0
    for index, width in enumerate(widths):
        here = slice(half * rows, (half + 1) * rows)
        total = None
        for left, right in ((kept, ranked), (other, ranked_far)):
            term = lax.dot_general(
                left[index, here, :],
                right[:width],
                (((1,), (1,)), ((), ())),
                preferred_element_type=jnp.float32,
            )
            total = term if total is None else total + term
        out[:, offset : offset + width] = total.astype(out.dtype)
        offset += width


def banded(widths, across, stacked):
    bounds = (0,) + widths
    tokens = across.shape[1] // 3
    for band in range(3):
        low, high = bounds[band], bounds[band + 1]
        yield slice(low, high), jnp.dot(
            across[:, band * tokens :],
            stacked[band * tokens :, low:high],
            preferred_element_type=jnp.float32,
        )


def rates_kernel(
    widths, parts, pairs, hidden, rates, near, hidden_near, rates_near, in_sems, out_sems
):
    own_core, _ = own_place()
    rows = pairs.shape[0] * 8
    starts = (0, widths[0], widths[0] + widths[1])

    def loads(number):
        index, low, size = parts[number]
        for which in range(2):
            place = pl.ds(2 * starts[index] + which * widths[index] + low, size)
            yield pltpu.make_async_copy(
                pairs.at[:, :, :, place], near.at[:, :, :, place], in_sems.at[number, which]
            )

    def stores(number):
        index, low, size = parts[number]
        place = pl.ds(starts[index] + low, size)
        yield pltpu.make_async_copy(
            rates_near.at[:, :, place], rates.at[:, :, place], out_sems.at[number, 0]
        )
        spot = (pl.ds(4 * index * rows, 4 * rows), pl.ds(low, size))
        yield pltpu.make_async_copy(hidden_near.at[spot], hidden.at[spot], out_sems.at[number, 1])

    for number in range(len(parts)):
        for copy in loads(number):
            copy.start()
    for number, (index, low, size) in enumerate(parts):
        for copy in loads(number):
            copy.wait()
        offset, width = starts[index], widths[index]

        @pl.loop(0, size // STEP)
        def _(block, index=index, low=low, offset=offset, width=width):
            start = pl.multiple_of(low + block * STEP, STEP)
            gate_place = pl.ds(pl.multiple_of(2 * offset + start, STEP), STEP)
            up_place = pl.ds(pl.multiple_of(2 * offset + width + start, STEP), STEP)
            for core in range(2):
                which = jnp.where(core == 0, own_core, 1 - own_core)
                gates = near[:, which, :, gate_place].astype(jnp.float32).reshape(-1, 2, 8, STEP)
                ups = near[:, which, :, up_place].astype(jnp.float32).reshape(-1, 2, 8, STEP)
                for half in range(2):
                    gate = gates[:, half].reshape(rows, STEP)
                    up = ups[:, half].reshape(rows, STEP)
                    sigmoid = jax.nn.sigmoid(gate)
                    active = gate * sigmoid
                    group = (2 * half + core) * rows
                    row = 4 * index * rows + group
                    hidden_near[row : row + rows, pl.ds(start, STEP)] = (active * up).astype(
                        jnp.bfloat16
                    )
                    place = pl.ds(pl.multiple_of(offset + start, STEP), STEP)
                    rates_near[0, group : group + rows, place] = up * (
                        sigmoid * (1.0 + gate * (1.0 - sigmoid))
                    )
                    rates_near[1, group : group + rows, place] = active

        for copy in stores(number):
            copy.start()
    for number in range(len(parts)):
        for copy in stores(number):
            copy.wait()


def reduce_kernel(pieces, rates, out):
    total = pieces[0].astype(jnp.float32)
    for place in range(1, pieces.shape[0]):
        total = total + pieces[place].astype(jnp.float32)
    total = total.astype(jnp.bfloat16)
    for place in range(out.shape[0]):
        out[place] = total


def turn(tokens, index, half):
    own_core, own_half = own_place()
    pair = [
        group_of(tokens[:, index], jnp.where(core == 0, own_core, 1 - own_core), (own_half + half) % 2)
        for core in range(2)
    ]
    return jnp.concatenate(pair, axis=0).T.astype(jnp.bfloat16)


def down_kernel(widths, position, hidden_far, tokens, down_grad, flag, hidden, totals, turned, sems):
    flag[...] = jnp.zeros_like(flag)
    count = position.shape[1]
    rows = hidden.shape[0] // 12

    def load(index):
        spot = (pl.ds(4 * index * rows, 4 * rows), pl.ds(0, widths[index]))
        return pltpu.make_async_copy(hidden_far.at[spot], hidden.at[spot], sems.at[index])

    for index in range(3):
        load(index).start()
    for index in range(3):
        for half in range(2):
            low = (4 * index + 2 * half) * rows
            turned[:, low : low + 2 * rows] = turn(tokens, 3 + index, half)
    for index in range(3):
        load(index).wait()
    for columns, product in banded(widths, turned, hidden):
        totals[:, columns] = product.astype(jnp.bfloat16)

    @pl.loop(0, count // TILE)
    def _(block):
        here = pl.ds(pl.multiple_of(block * TILE, TILE), TILE)
        ranks_here = lax.broadcasted_iota(jnp.int32, (count, TILE), 0)
        moved = jnp.dot(
            totals[...],
            ones_where(ranks_here, position[:, here]),
            preferred_element_type=jnp.float32,
        )
        down_grad[here, :] = moved.T.astype(jnp.bfloat16)


def slopes_of(widths, first, second, rates, gates, ups):
    rows = first.shape[0]
    offset = 0
    for index, width in enumerate(widths):

        @pl.loop(0, width // STEP)
        def _(block, index=index, offset=offset):
            start = pl.multiple_of(block * STEP, STEP)
            place = pl.ds(pl.multiple_of(offset + start, STEP), STEP)
            for core, above in enumerate((first, second)):
                upstream = above[:, place].astype(jnp.float32)
                source = slice(core * rows, (core + 1) * rows)
                low = (2 * index + core) * rows
                gates[low : low + rows, pl.ds(start, STEP)] = (
                    upstream * rates[0, source, place]
                ).astype(jnp.bfloat16)
                ups[low : low + rows, pl.ds(start, STEP)] = (
                    upstream * rates[1, source, place]
                ).astype(jnp.bfloat16)

        offset += width


def first_kernel(
    widths,
    position,
    first,
    second,
    rates_far,
    tokens,
    sums,
    chosen,
    rates_second,
    turned_second,
    rates,
    turned,
    gates,
    ups,
    sems,
):
    count = position.shape[1]
    features = tokens.shape[3]
    rows = first.shape[0]
    copies = [
        pltpu.make_async_copy(
            rates_far.at[:, pl.ds(2 * half * rows, 2 * rows), :], target, sems.at[half]
        )
        for half, target in enumerate((rates, rates_second))
    ]
    for copy in copies:
        copy.start()
    for index in range(3):
        here = slice(2 * index * rows, 2 * (index + 1) * rows)
        turned[:, here] = turn(tokens, index, 0)
        turned_second[:, here] = turn(tokens, index, 1)

    @pl.loop(0, count // TILE)
    def _(block):
        here = pl.ds(pl.multiple_of(block * TILE, TILE), TILE)
        chosen[here, :] = ones_where(
            lax.broadcasted_iota(jnp.int32, (TILE, count), 0) + block * TILE, position[...]
        )

    copies[0].wait()
    slopes_of(widths, first, second, rates, gates, ups)
    for place, array in enumerate((gates, ups)):
        for columns, product in banded(widths, turned, array):
            sums[place * features : (place + 1) * features, columns] = product
    copies[1].wait()


def second_kernel(
    widths,
    chosen,
    first,
    second,
    rates,
    turned,
    sums,
    gate_grad,
    up_grad,
    gates,
    ups,
    totals,
    staged,
    sems,
):
    count = chosen.shape[0]
    features = turned.shape[0]
    slopes_of(widths, first, second, rates, gates, ups)
    for place, array in enumerate((gates, ups)):
        for columns, product in banded(widths, turned, array):
            low = slice(place * features, (place + 1) * features)
            totals[low, columns] = (sums[low, columns] + product).astype(jnp.bfloat16)

    def stores(block):
        here = pl.ds(block * TILE, TILE)
        for place, target in enumerate((gate_grad, up_grad)):
            yield pltpu.make_async_copy(
                staged.at[pl.ds(place * features, features), here],
                target.at[:, here],
                sems.at[block, place],
            )

    for block in range(count // TILE):
        here = slice(block * TILE, (block + 1) * TILE)
        staged[:, here] = jnp.dot(
            totals[...], chosen[:, here], preferred_element_type=jnp.float32
        ).astype(jnp.bfloat16)
        for copy in stores(block):
            copy.start()
    for block in range(count // TILE):
        for copy in stores(block):
            copy.wait()


def per_device(
    ranks, down_weight, inputs, grad_out, gate_small, up_small, gate_mid, up_mid, gate_full, up_full
):
    n_dp = lax.axis_size("dp")
    n_tensor = lax.axis_size("tensor")
    n_rows = n_dp // 4
    count, features = down_weight.shape
    widths = tuple(padded(item.shape[1]) for item in (gate_small, gate_mid, gate_full))
    total = sum(widths)
    core_swap = [(item, item ^ 1) for item in range(n_dp)]
    x_swap = [(item, item ^ 2) for item in range(n_dp)]
    by_place = [[4 * row + place for row in range(n_rows)] for place in range(4)]
    by_half = [
        [4 * row + 2 * half + core for row in range(n_rows) for core in range(2)] for half in range(2)
    ]

    def over_rows(blocks):
        return lax.all_to_all(blocks, "dp", 0, 0, axis_index_groups=by_place, tiled=True)

    given = (gate_small, up_small, gate_mid, up_mid, gate_full, up_full, inputs, grad_out)
    copies, local = pl.pallas_call(
        start_kernel,
        out_shape=(
            shaped((n_tensor, 6) + inputs.shape[1:]),
            shaped((gate_small.shape[0], 2 * total)),
        ),
        in_specs=[ANY] * len(given),
        out_specs=(VMEM, VMEM),
        scratch_shapes=[pltpu.VMEM(item.shape, item.dtype) for item in given]
        + [pltpu.SemaphoreType.DMA((len(given),))],
        compiler_params=FULL,
    )(*given)
    tokens = lax.all_to_all(copies, "tensor", 0, 0, tiled=True)

    position = (ranks // n_tensor)[None, :]
    flag_shape = shaped((8, 128), jnp.float32)
    ranked, flag = call(
        sort_kernel,
        (shaped((count, features)), flag_shape),
        position,
        down_weight,
        flops=2 * count * count * features,
    )
    ranked_far = lax.ppermute(ranked, "dp", core_swap)

    there = lax.ppermute(local, "dp", x_swap)
    two = jnp.concatenate([local, there], axis=0)
    gathered = lax.all_gather(two, "dp", axis=0, axis_index_groups=by_half, tiled=True)
    pairs = gathered.reshape(n_rows, 2, two.shape[0], two.shape[1])

    rows = tokens.shape[0] * tokens.shape[2] // 4

    sent, kept = call(split_kernel, (shaped((3, 2 * rows, features)),) * 2, tokens, flag)
    other = lax.ppermute(sent, "dp", core_swap)

    def partial(half, dtype, *behind):
        return call(
            functools.partial(partial_kernel, widths, half),
            shaped((rows, total), dtype),
            kept,
            other,
            ranked,
            ranked_far,
            *behind,
            flops=4 * WEIGHT * rows * total * features,
        )

    across = partial(1, jnp.bfloat16)
    far = lax.ppermute(across, "dp", x_swap)
    summed = (partial(0, jnp.float32, across) + far.astype(jnp.float32)).astype(jnp.bfloat16)
    pieces = over_rows(summed.reshape(n_rows, -1, total))
    half_full = widths[2] // 2
    parts = ((2, 0, half_full), (2, half_full, half_full), (1, 0, widths[1]), (0, 0, widths[0]))
    hidden_shape, rates_shape = (12 * rows, count), (2, 4 * rows, total)
    hidden, rates = pl.pallas_call(
        functools.partial(rates_kernel, widths, parts),
        out_shape=(shaped(hidden_shape), shaped(rates_shape, jnp.float32)),
        in_specs=[ANY],
        out_specs=(ANY, ANY),
        scratch_shapes=[
            pltpu.VMEM(pairs.shape, jnp.bfloat16),
            pltpu.VMEM(hidden_shape, jnp.bfloat16),
            pltpu.VMEM(rates_shape, jnp.float32),
            pltpu.SemaphoreType.DMA((len(parts), 2)),
            pltpu.SemaphoreType.DMA((len(parts), 2)),
        ],
        compiler_params=FULL,
        cost_estimate=pl.CostEstimate(
            flops=2 * features * count * count, bytes_accessed=2**20, transcendentals=0
        ),
    )(pairs)
    reduced = pl.pallas_call(
        reduce_kernel,
        out_shape=shaped(pieces.shape),
        in_specs=[VMEM, ANY],
        out_specs=VMEM,
        compiler_params=pltpu.CompilerParams(vmem_limit_bytes=REDUCE * 1024 * 1024),
    )(pieces, rates)
    near = over_rows(reduced).reshape(rows, total)

    down_grad, flag = pl.pallas_call(
        functools.partial(down_kernel, widths),
        out_shape=(shaped((count, features)), flag_shape),
        in_specs=[VMEM, ANY, VMEM],
        out_specs=(VMEM, VMEM),
        scratch_shapes=[
            pltpu.VMEM(hidden_shape, jnp.bfloat16),
            pltpu.VMEM((features, count), jnp.bfloat16),
            pltpu.VMEM((features, 12 * rows), jnp.bfloat16),
            pltpu.SemaphoreType.DMA((3,)),
        ],
        compiler_params=LIMIT,
        cost_estimate=pl.CostEstimate(
            flops=2 * features * count * count, bytes_accessed=2**20, transcendentals=0
        ),
    )(position, hidden, tokens)
    near = after(near, flag)
    beyond = lax.ppermute(near, "dp", x_swap)
    near_other = lax.ppermute(near, "dp", core_swap)
    halves = [pltpu.VMEM((6 * rows, count), jnp.bfloat16)] * 2
    rates_half, turned_shape = (2, 2 * rows, total), (features, 6 * rows)
    sums, chosen, rates_second, turned = pl.pallas_call(
        functools.partial(first_kernel, widths),
        out_shape=(
            shaped((2 * features, count), jnp.float32),
            shaped((count, count)),
            shaped(rates_half, jnp.float32),
            shaped(turned_shape),
        ),
        in_specs=[VMEM, VMEM, VMEM, ANY, VMEM],
        out_specs=(VMEM,) * 4,
        scratch_shapes=[
            pltpu.VMEM(rates_half, jnp.float32),
            pltpu.VMEM(turned_shape, jnp.bfloat16),
            *halves,
            pltpu.SemaphoreType.DMA((2,)),
        ],
        compiler_params=pltpu.CompilerParams(vmem_limit_bytes=37 * 1024 * 1024),
        cost_estimate=pl.CostEstimate(
            flops=4 * features * count * rows, bytes_accessed=2**20, transcendentals=0
        ),
    )(position, near, near_other, rates, tokens)
    beyond = after(beyond, sums)
    beyond_other = lax.ppermute(beyond, "dp", core_swap)
    gate_grad, up_grad = pl.pallas_call(
        functools.partial(second_kernel, widths),
        out_shape=(shaped((features, count)),) * 2,
        in_specs=[VMEM] * 6,
        out_specs=(ANY, ANY),
        scratch_shapes=[
            *halves,
            pltpu.VMEM((2 * features, count), jnp.bfloat16),
            pltpu.VMEM((2 * features, count), jnp.bfloat16),
            pltpu.SemaphoreType.DMA((count // TILE, 2)),
        ],
        compiler_params=LIMIT,
        cost_estimate=pl.CostEstimate(
            flops=4 * features * count * (count + rows), bytes_accessed=2**20, transcendentals=0
        ),
    )(chosen, beyond, beyond_other, rates_second, turned, sums)
    return (down_grad, gate_grad, up_grad)


def solution(mesh):
    return jax.shard_map(
        per_device,
        mesh=mesh,
        in_specs=(
            P("tensor"),
            P("tensor", "dp"),
            P(None, "tensor", "dp"),
            P(None, "tensor", "dp"),
            P("dp", "tensor"),
            P("dp", "tensor"),
            P("dp", "tensor"),
            P("dp", "tensor"),
            P("dp", "tensor"),
            P("dp", "tensor"),
        ),
        out_specs=(P("tensor", "dp"), P("dp", "tensor"), P("dp", "tensor")),
        check_vma=False,
    )
```

time: 145 us -> 144 us (level)
  local copies, waits for them, and re-layouts: 27.6 us -> 3.7 us
  waiting for transfers between devices: 22 us -> 43.3 us
  Pallas kernels: 25.4 us -> 28.3 us
  starting transfers between devices: 51.9 us -> 50.2 us
    unnamed x38 -> x6, local copies, waits for them, and re-layouts: 26.8 us -> 3.69 us
    pallas_call x0 -> x5, Pallas kernels: none -> 21.1 us  [the longest x1 5.59 us: per_device(): pl.pallas_call(functools.partial(down_kernel, widths), out_shape=(shaped(...]
    pallas_call x8 -> x4, Pallas kernels: 23.5 us -> 5.24 us  [call(): pl.pallas_call(kernel, out_shape=out_shape, in_specs=[SMEM] * scalars + [...]
    all_to_all x2, waiting for transfers between devices: 1.14 us -> 13.3 us  [over_rows(): lax.all_to_all(blocks, 'dp', 0, 0, axis_index_groups=by_place, tiled=True)]
    all_to_all x1, waiting for transfers between devices: 1.04 us -> 10.8 us  [per_device(): tokens = lax.all_to_all(copies, 'tensor', 0, 0, tiled=True)]
    all_gather x1, waiting for transfers between devices: 3.9 us -> 0.01 us  [per_device(): lax.all_gather(two, 'dp', axis=0, axis_index_groups=by_half, tiled=True)]
    ppermute x1, waiting for transfers between devices: 4.85 us -> 7.41 us  [per_device(): beyond = lax.ppermute(near, 'dp', x_swap)]
    all_to_all x1, starting transfers between devices: 11.9 us -> 10.2 us  [per_device(): tokens = lax.all_to_all(copies, 'tensor', 0, 0, tiled=True)]
  transfers between devices with their start and end apart: 11 -> 11, of which waited for: 7 -> 7; matrix products, arithmetic and copies ran while one was open for 2% -> 2% of each run, Pallas kernels for 11% -> 13%
where the time goes in v6:
time: 144 us; the launch traced here: 143 us
  starting transfers between devices  50.2 us (35%)
  waiting for transfers between devices  43.3 us (30%)
  Pallas kernels  28.3 us (20%)
  between operations  14.2 us (10%)
  local copies, waits for them, and re-layouts  3.7 us (3%)
  other arithmetic  3.12 us (2%)
    all_to_all x2, waiting for transfers between devices, over_rows(): lax.all_to_all(blocks, 'dp', 0, 0, axis_index_groups=by_place, tiled=True)  13.3 us
    all_to_all x1, waiting for transfers between devices, per_device(): tokens = lax.all_to_all(copies, 'tensor', 0, 0, tiled=True)  10.8 us
    all_to_all x2, starting transfers between devices, over_rows(): lax.all_to_all(blocks, 'dp', 0, 0, axis_index_groups=by_place, tiled=True)  10.3 us
    all_to_all x1, starting transfers between devices, per_device(): tokens = lax.all_to_all(copies, 'tensor', 0, 0, tiled=True)  10.2 us
    ppermute x1, waiting for transfers between devices, per_device(): far = lax.ppermute(across, 'dp', x_swap)  9.32 us
    ppermute x1, waiting for transfers between devices, per_device(): beyond = lax.ppermute(near, 'dp', x_swap)  7.41 us
    ppermute x1, starting transfers between devices, per_device(): near_other = lax.ppermute(near, 'dp', core_swap)  5.59 us
    pallas_call x1, Pallas kernels, per_device(): pl.pallas_call(functools.partial(down_kernel, widths), out_shape=(shaped(...  5.59 us
  transfers between devices with their start and end apart: 11, of which 7 were waited for; matrix products, arithmetic and copies ran while one was open for 2% of the time, Pallas kernels for 13%

profile of v6, /device:TPU:1, one launch (start us, length us, event | category | flops | bytes accessed | tf_op | source)
XLA Modules:
  0.0 142.8 jit_solution(6798942227498387524)
XLA Ops:
  7.2 1.9 %shard_map.121 = (bf16[16,6,16,256]{3,2,1,0:T(8,128)(2,1)}, bf16[8,6400]{1,0:T(8,128)(2,1)}) custom-call(bf16[8,448]{1,0:T(8,128)(2,1)} %refs_0_.1, bf16[8,448]{1,0:T(8,128)(2,1)} %refs_1_.1, bf16[8,896]{1,0:T(8,128)(2,1)} %refs_2_.1, bf16[8,896]{1,0:T(8,128)(2,1)} %refs_3_.1, bf16[8,1792]{1,0:T(8,128)(2,1)} %refs_4_.1, bf16[8,1792]{1,0:T(8,128)(2,1)} %refs_5_.1, ...), custom_call_target="tpu_custom_call" | custom-call | tf_op jit(solution)/shard_map/pallas_call | solution.py:411
  9.1 5.5 %collective-permute-start = (bf16[8,6400]{1,0:T(8,128)(2,1)}, bf16[8,6400]{1,0:T(8,128)(2,1)S(1)}, u32[]{:S(2)}, u32[]{:S(2)}) collective-permute-start(bf16[8,6400]{1,0:T(8,128)(2,1)} %get-tuple-element.19), channel_id=1, source_target_pairs={{0,32},{16,48},{32,0},{48,16},{64,96},{80,112},{96,64},{112,80},{1... | collective-permute-start | bytes 307208 | tf_op jit(solution)/shard_map/ppermute | solution.py:436
  14.6 10.2 %all-to-all-start = ((bf16[16,6,16,256]{3,2,1,0:T(8,128)(2,1)}), bf16[16,6,16,256]{3,2,1,0:T(8,128)(2,1)S(1)}, u32[]{:S(2)}, u32[]{:S(2)}) async-start(bf16[16,6,16,256]{3,2,1,0:T(8,128)(2,1)} %get-tuple-element.21), calls=%async_computation | async-start | bytes 1572864 | tf_op jit(solution)/shard_map/all_to_all | solution.py:423
  24.8 0.0 all-gather.2.cloned.1.call-start
  24.8 0.0 collective-permute-done
  24.8 1.6 %pad_maximum_fusion = bf16[16,6400]{1,0:T(8,128)(2,1)} fusion(bf16[8,6400]{1,0:T(8,128)(2,1)S(1)} %collective-permute-done, bf16[8,6400]{1,0:T(8,128)(2,1)} %get-tuple-element.19), kind=kLoop, calls=%fused_computation.2 | loop fusion | flops 409600 | bytes 409600 | tf_op jit(solution)/shard_map/concatenate | solution.py:437
  26.4 0.0 all-gather.2.cloned.1.call-update
  26.5 0.7 add_select_fusion
  27.2 0.0 copy-start
  27.2 1.2 copy-done
  28.3 2.9 %shard_map.124 = (bf16[1792,256]{1,0:T(8,128)(2,1)S(1)}, f32[8,128]{1,0:T(8,128)S(1)}) custom-call(s32[1,1792]{1,0:T(1,128)S(1)} %broadcast_in_dim.3.position, bf16[1792,256]{1,0:T(8,128)(2,1)S(1)} %copy-done), custom_call_target="tpu_custom_call" | custom-call | flops 1644167168 | bytes 1048576 | tf_op jit(solution)/shard_map/pallas_call | solution.py:27
  31.2 3.1 %collective-permute-start.2 = (bf16[1792,256]{1,0:T(8,128)(2,1)S(1)}, bf16[1792,256]{1,0:T(8,128)(2,1)S(1)}, u32[]{:S(2)}, u32[]{:S(2)}) collective-permute-start(bf16[1792,256]{1,0:T(8,128)(2,1)S(1)} %get-tuple-element.26.ranked), channel_id=1, source_target_pairs={{0,16},{16,0},{32,48},{48,32},{64,80},{80,64},{96,112},{112,96},{1... | collective-permute-start | bytes 2752520 | tf_op jit(solution)/shard_map/ppermute | solution.py:434
  34.4 10.8 %all-to-all-done.tokens = bf16[16,6,16,256]{3,2,1,0:T(8,128)(2,1)S(1)} async-done(((bf16[16,6,16,256]{3,2,1,0:T(8,128)(2,1)}), bf16[16,6,16,256]{3,2,1,0:T(8,128)(2,1)S(1)}, u32[]{:S(2)}, u32[]{:S(2)}) %all-to-all-start) | async-done | bytes 786464 | tf_op jit(solution)/shard_map/all_to_all | solution.py:423
  45.2 0.1 shard_map.125
  45.4 5.3 %collective-permute-start.1 = (bf16[3,128,256]{2,1,0:T(8,128)(2,1)S(1)}, bf16[3,128,256]{2,1,0:T(8,128)(2,1)S(1)}, u32[]{:S(2)}, u32[]{:S(2)}) collective-permute-start(bf16[3,128,256]{2,1,0:T(8,128)(2,1)S(1)} %get-tuple-element.25), channel_id=1, source_target_pairs={{0,16},{16,0},{32,48},{48,32},{64,80},{80,64},{96,112},{112,96},{1... | collective-permute-start | bytes 589832 | tf_op jit(solution)/shard_map/ppermute | solution.py:444
  50.7 0.0 collective-permute-done.2.ranked_far
  50.7 1.0 collective-permute-done.1.other
  51.7 1.1 shard_map.126.rest_0_
  52.8 3.6 %collective-permute-start.3 = (bf16[64,3200]{1,0:T(8,128)(2,1)S(1)}, bf16[64,3200]{1,0:T(8,128)(2,1)S(1)}, u32[]{:S(2)}, u32[]{:S(2)}) collective-permute-start(bf16[64,3200]{1,0:T(8,128)(2,1)S(1)} %shard_map.126.rest_0_), channel_id=1, source_target_pairs={{0,32},{16,48},{32,0},{48,16},{64,96},{80,112},{96,64},{112,80},{1... | collective-permute-start | bytes 1228808 | tf_op jit(solution)/shard_map/ppermute | solution.py:459
  56.5 1.1 shard_map.127
  57.6 9.3 %collective-permute-done.3 = bf16[64,3200]{1,0:T(8,128)(2,1)S(1)} collective-permute-done((bf16[64,3200]{1,0:T(8,128)(2,1)S(1)}, bf16[64,3200]{1,0:T(8,128)(2,1)S(1)}, u32[]{:S(2)}, u32[]{:S(2)}) %collective-permute-start.3) | collective-permute-done | bytes 409632 | tf_op jit(solution)/shard_map/ppermute | solution.py:459
  66.9 0.8 fusion
  67.7 6.8 %all-to-all-start.1 = ((bf16[8,8,3200]{2,1,0:T(8,128)(2,1)}), bf16[8,8,3200]{2,1,0:T(8,128)(2,1)S(1)}, u32[]{:S(2)}, u32[]{:S(2)}) async-start(bf16[8,8,3200]{2,1,0:T(8,128)(2,1)} %fusion), calls=%async_computation.1 | async-start | bytes 819200 | tf_op jit(solution)/shard_map/all_to_all | solution.py:408
  74.6 0.0 all-gather.2.cloned.1.call-done
  74.6 5.0 %shard_map.122 = (bf16[768,1792]{1,0:T(8,128)(2,1)}, f32[2,256,3200]{2,1,0:T(8,128)}) custom-call(bf16[8,2,16,6400]{3,2,1,0:T(8,128)(2,1)} %bitcast.5), custom_call_target="tpu_custom_call" | custom-call | flops 1644167168 | bytes 1048576 | tf_op jit(solution)/shard_map/pallas_call | solution.py:465
  79.6 8.5 %all-to-all-done.1.pieces = bf16[8,8,3200]{2,1,0:T(8,128)(2,1)S(1)} async-done(((bf16[8,8,3200]{2,1,0:T(8,128)(2,1)}), bf16[8,8,3200]{2,1,0:T(8,128)(2,1)S(1)}, u32[]{:S(2)}, u32[]{:S(2)}) %all-to-all-start.1) | async-done | bytes 409632 | tf_op jit(solution)/shard_map/all_to_all | solution.py:408
  88.1 0.0 copy-start.2
  88.1 0.7 copy-done.2
  88.9 1.8 %shard_map.128 = bf16[8,8,3200]{2,1,0:T(8,128)(2,1)} custom-call(bf16[8,8,3200]{2,1,0:T(8,128)(2,1)} %copy-done.2, f32[2,256,3200]{2,1,0:T(8,128)} %get-tuple-element.27.rates.rates_far), custom_call_target="tpu_custom_call" | custom-call | tf_op jit(solution)/shard_map/pallas_call | solution.py:482
  90.7 3.5 %all-to-all-start.2 = ((bf16[8,8,3200]{2,1,0:T(8,128)(2,1)}), bf16[8,8,3200]{2,1,0:T(8,128)(2,1)S(1)}, u32[]{:S(2)}, u32[]{:S(2)}) async-start(bf16[8,8,3200]{2,1,0:T(8,128)(2,1)} %shard_map.128), calls=%async_computation.2 | async-start | bytes 819200 | tf_op jit(solution)/shard_map/all_to_all | solution.py:408
  94.1 0.0 copy-start.1
  94.2 1.8 %copy-done.1 = bf16[768,1792]{1,0:T(8,128)(2,1)S(1)} copy-done((bf16[768,1792]{1,0:T(8,128)(2,1)S(1)}, bf16[768,1792]{1,0:T(8,128)(2,1)}, u32[]{:S(2)}) %copy-start.1) | copy-done | bytes 2752536
  95.9 5.6 %shard_map.123 = (bf16[1792,256]{1,0:T(8,128)(2,1)}, f32[8,128]{1,0:T(8,128)S(1)}) custom-call(s32[1,1792]{1,0:T(1,128)S(1)} %broadcast_in_dim.3.position, bf16[768,1792]{1,0:T(8,128)(2,1)S(1)} %copy-done.1, bf16[16,6,16,256]{3,2,1,0:T(8,128)(2,1)S(1)} %all-to-all-done.tokens), custom_call_target="tpu_custom_call" | custom-call | flops 1644167168 | bytes 1048576 | tf_op jit(solution)/shard_map/pallas_call | solution.py:491
  101.5 4.8 %all-to-all-done.2 = bf16[8,8,3200]{2,1,0:T(8,128)(2,1)S(1)} async-done(((bf16[8,8,3200]{2,1,0:T(8,128)(2,1)}), bf16[8,8,3200]{2,1,0:T(8,128)(2,1)S(1)}, u32[]{:S(2)}, u32[]{:S(2)}) %all-to-all-start.2) | async-done | bytes 409632 | tf_op jit(solution)/shard_map/all_to_all | solution.py:408
  106.4 5.6 %collective-permute-start.4 = (bf16[64,3200]{1,0:T(8,128)(2,1)S(1)}, bf16[64,3200]{1,0:T(8,128)(2,1)S(1)}, u32[]{:S(2)}, u32[]{:S(2)}) collective-permute-start(bf16[64,3200]{1,0:T(8,128)(2,1)S(1)} %shard_map.129.first), channel_id=1, source_target_pairs={{0,16},{16,0},{32,48},{48,32},{64,80},{80,64},{96,112},{112,96},{1... | collective-permute-start | bytes 1228808 | tf_op jit(solution)/shard_map/ppermute | solution.py:509
  112.0 3.8 %collective-permute-start.5 = (bf16[64,3200]{1,0:T(8,128)(2,1)S(1)}, bf16[64,3200]{1,0:T(8,128)(2,1)S(1)}, u32[]{:S(2)}, u32[]{:S(2)}) collective-permute-start(bf16[64,3200]{1,0:T(8,128)(2,1)S(1)} %shard_map.129.first), channel_id=1, source_target_pairs={{0,32},{16,48},{32,0},{48,16},{64,96},{80,112},{96,64},{112,80},{1... | collective-permute-start | bytes 1228808 | tf_op jit(solution)/shard_map/ppermute | solution.py:508
  115.8 0.0 collective-permute-done.4.second
  115.8 3.2 %shard_map.130 = (f32[512,1792]{1,0:T(8,128)S(1)}, bf16[1792,1792]{1,0:T(8,128)(2,1)S(1)}, f32[2,128,3200]{2,1,0:T(8,128)S(1)}, bf16[256,384]{1,0:T(8,128)(2,1)S(1)}) custom-call(s32[1,1792]{1,0:T(1,128)S(1)} %broadcast_in_dim.3.position, bf16[64,3200]{1,0:T(8,128)(2,1)S(1)} %shard_map.129.first, bf16[64,3200]{1,0:T(8,128)(2,1)S(1)} %collective-permute-done.4.second, ...), custom_call_target="tpu_custom_call" | custom-call | flops 117440512 | bytes 1048576 | tf_op jit(solution)/shard_map/pallas_call | solution.py:512
  119.0 7.4 %collective-permute-done.5.value_ref = bf16[64,3200]{1,0:T(8,128)(2,1)S(1)} collective-permute-done((bf16[64,3200]{1,0:T(8,128)(2,1)S(1)}, bf16[64,3200]{1,0:T(8,128)(2,1)S(1)}, u32[]{:S(2)}, u32[]{:S(2)}) %collective-permute-start.5) | collective-permute-done | bytes 409632 | tf_op jit(solution)/shard_map/ppermute | solution.py:508
  126.4 2.7 %collective-permute-start.6 = (bf16[64,3200]{1,0:T(8,128)(2,1)S(1)}, bf16[64,3200]{1,0:T(8,128)(2,1)S(1)}, u32[]{:S(2)}, u32[]{:S(2)}) collective-permute-start(bf16[64,3200]{1,0:T(8,128)(2,1)S(1)} %shard_map.131.first), channel_id=1, source_target_pairs={{0,16},{16,0},{32,48},{48,32},{64,80},{80,64},{96,112},{112,96},{1... | collective-permute-start | bytes 1228808 | tf_op jit(solution)/shard_map/ppermute | solution.py:534
  129.1 1.4 collective-permute-done.6.second
  130.5 5.5 %shard_map.132 = (bf16[256,1792]{1,0:T(8,128)(2,1)}, bf16[256,1792]{1,0:T(8,128)(2,1)}) custom-call(bf16[1792,1792]{1,0:T(8,128)(2,1)S(1)} %get-tuple-element.29.chosen, bf16[64,3200]{1,0:T(8,128)(2,1)S(1)} %shard_map.131.first, bf16[64,3200]{1,0:T(8,128)(2,1)S(1)} %collective-permute-done.6.second, f32[2,128,3200]{2,1,0:T(8,128)S(1)} %get-tuple-element.31.rates, ...), custom_call_target="tpu_custom_call" | custom-call | flops 3405774848 | bytes 1048576 | tf_op jit(solution)/shard_map/pallas_call | solution.py:535
  (3 shorter events, 0.0 us)
Async XLA Ops:
  9.1 15.7 %collective-permute-start = (bf16[8,6400]{1,0:T(8,128)(2,1)}, bf16[8,6400]{1,0:T(8,128)(2,1)S(1)}, u32[]{:S(2)}, u32[]{:S(2)}) collective-permute-start(bf16[8,6400]{1,0:T(8,128)(2,1)} %get-tuple-element.19), channel_id=1, source_target_pairs={{0,32},{16,48},{32,0},{48,16},{64,96},{80,112},{96,64},{112,80},{1... | collective-permute-start | bytes 307208 | tf_op jit(solution)/shard_map/ppermute | solution.py:436
  14.6 30.6 %all-to-all-start = ((bf16[16,6,16,256]{3,2,1,0:T(8,128)(2,1)}), bf16[16,6,16,256]{3,2,1,0:T(8,128)(2,1)S(1)}, u32[]{:S(2)}, u32[]{:S(2)}) async-start(bf16[16,6,16,256]{3,2,1,0:T(8,128)(2,1)} %get-tuple-element.21), calls=%async_computation | async-start | bytes 1572864 | tf_op jit(solution)/shard_map/all_to_all | solution.py:423
  24.8 49.8 %all-gather.2.cloned.1.call-start = ((), (), s32[]{:S(2)}) async-start(), calls=%async_computation.3 | async-start | bytes 3481600 | tf_op jit(solution)/shard_map/all_gather | solution.py:438
  27.2 1.2 copy-start
  31.2 19.4 %collective-permute-start.2 = (bf16[1792,256]{1,0:T(8,128)(2,1)S(1)}, bf16[1792,256]{1,0:T(8,128)(2,1)S(1)}, u32[]{:S(2)}, u32[]{:S(2)}) collective-permute-start(bf16[1792,256]{1,0:T(8,128)(2,1)S(1)} %get-tuple-element.26.ranked), channel_id=1, source_target_pairs={{0,16},{16,0},{32,48},{48,32},{64,80},{80,64},{96,112},{112,96},{1... | collective-permute-start | bytes 2752520 | tf_op jit(solution)/shard_map/ppermute | solution.py:434
  45.4 6.4 %collective-permute-start.1 = (bf16[3,128,256]{2,1,0:T(8,128)(2,1)S(1)}, bf16[3,128,256]{2,1,0:T(8,128)(2,1)S(1)}, u32[]{:S(2)}, u32[]{:S(2)}) collective-permute-start(bf16[3,128,256]{2,1,0:T(8,128)(2,1)S(1)} %get-tuple-element.25), channel_id=1, source_target_pairs={{0,16},{16,0},{32,48},{48,32},{64,80},{80,64},{96,112},{112,96},{1... | collective-permute-start | bytes 589832 | tf_op jit(solution)/shard_map/ppermute | solution.py:444
  52.8 14.1 %collective-permute-start.3 = (bf16[64,3200]{1,0:T(8,128)(2,1)S(1)}, bf16[64,3200]{1,0:T(8,128)(2,1)S(1)}, u32[]{:S(2)}, u32[]{:S(2)}) collective-permute-start(bf16[64,3200]{1,0:T(8,128)(2,1)S(1)} %shard_map.126.rest_0_), channel_id=1, source_target_pairs={{0,32},{16,48},{32,0},{48,16},{64,96},{80,112},{96,64},{112,80},{1... | collective-permute-start | bytes 1228808 | tf_op jit(solution)/shard_map/ppermute | solution.py:459
  67.7 20.4 %all-to-all-start.1 = ((bf16[8,8,3200]{2,1,0:T(8,128)(2,1)}), bf16[8,8,3200]{2,1,0:T(8,128)(2,1)S(1)}, u32[]{:S(2)}, u32[]{:S(2)}) async-start(bf16[8,8,3200]{2,1,0:T(8,128)(2,1)} %fusion), calls=%async_computation.1 | async-start | bytes 819200 | tf_op jit(solution)/shard_map/all_to_all | solution.py:408
  88.1 0.8 copy-start.2
  90.7 15.7 %all-to-all-start.2 = ((bf16[8,8,3200]{2,1,0:T(8,128)(2,1)}), bf16[8,8,3200]{2,1,0:T(8,128)(2,1)S(1)}, u32[]{:S(2)}, u32[]{:S(2)}) async-start(bf16[8,8,3200]{2,1,0:T(8,128)(2,1)} %shard_map.128), calls=%async_computation.2 | async-start | bytes 819200 | tf_op jit(solution)/shard_map/all_to_all | solution.py:408
  94.1 1.8 %copy-start.1 = (bf16[768,1792]{1,0:T(8,128)(2,1)S(1)}, bf16[768,1792]{1,0:T(8,128)(2,1)}, u32[]{:S(2)}) copy-start(bf16[768,1792]{1,0:T(8,128)(2,1)} %get-tuple-element.20.hidden_far) | copy-start | bytes 8257540
  106.4 9.5 %collective-permute-start.4 = (bf16[64,3200]{1,0:T(8,128)(2,1)S(1)}, bf16[64,3200]{1,0:T(8,128)(2,1)S(1)}, u32[]{:S(2)}, u32[]{:S(2)}) collective-permute-start(bf16[64,3200]{1,0:T(8,128)(2,1)S(1)} %shard_map.129.first), channel_id=1, source_target_pairs={{0,16},{16,0},{32,48},{48,32},{64,80},{80,64},{96,112},{112,96},{1... | collective-permute-start | bytes 1228808 | tf_op jit(solution)/shard_map/ppermute | solution.py:509
  112.0 14.5 %collective-permute-start.5 = (bf16[64,3200]{1,0:T(8,128)(2,1)S(1)}, bf16[64,3200]{1,0:T(8,128)(2,1)S(1)}, u32[]{:S(2)}, u32[]{:S(2)}) collective-permute-start(bf16[64,3200]{1,0:T(8,128)(2,1)S(1)} %shard_map.129.first), channel_id=1, source_target_pairs={{0,32},{16,48},{32,0},{48,16},{64,96},{80,112},{96,64},{112,80},{1... | collective-permute-start | bytes 1228808 | tf_op jit(solution)/shard_map/ppermute | solution.py:508
  126.4 4.1 %collective-permute-start.6 = (bf16[64,3200]{1,0:T(8,128)(2,1)S(1)}, bf16[64,3200]{1,0:T(8,128)(2,1)S(1)}, u32[]{:S(2)}, u32[]{:S(2)}) collective-permute-start(bf16[64,3200]{1,0:T(8,128)(2,1)S(1)} %shard_map.131.first), channel_id=1, source_target_pairs={{0,16},{16,0},{32,48},{48,32},{64,80},{80,64},{96,112},{112,96},{1... | collective-permute-start | bytes 1228808 | tf_op jit(solution)/shard_map/ppermute | solution.py:534
Sparse Core Ops, SparseCore 0:
  28.3 45.0 all-gather.1
